TPU v7x, 512 devices: a whole 4x4x16 slice. The times are simulated.
512 devices in a mesh: grp: 2 (over z_hi), seq: 32 (over y, x, core), dp: 8 (over z_lo).
Axes of the slice: x: 4, y: 4, z: 16 (z_hi: 2, z_lo: 8; z = z_hi * 8 + z_lo), core: 2. Of those that a mesh axis runs over, the one named last changes fastest.
Arguments:
- queries: bfloat16 [8, 4096, 4096], P('dp', 'seq'), may hold values from -130 to 130
- keys: bfloat16 [8, 4096, 4096], P('dp', 'seq'), may hold values from -8 to 8
- values: bfloat16 [8, 4096, 4096], P('dp', 'seq', 'grp'), may hold values from -6 to 6
- cotangent: bfloat16 [8, 4096, 4096], P('dp', 'seq', 'grp'), may hold values from -0.078125 to 0.078125
- captions: bfloat16 [8, 512, 4096], P('dp', 'seq'), may hold values from -6 to 6
- caption_len: int32 [8], P('dp'), may hold values from 1 to 512, 2560 in all
- proj_weight: bfloat16 [4096, 8192], P('dp', 'seq'), may hold values from -0.09375 to 0.09375
Outputs:
- attended: bfloat16 [8, 4096, 4096], P('dp', 'seq', 'grp')
- proj_grad: float32 [4096, 8192], P('dp', 'seq')
Inputs may be any that keep to these rules, and one draw needn't show every extreme that they name: `caption_len`: each caption has at least one token; some caption has all 512.
All inputs are finite; a program needn't handle non-finite values. No bound on the sum of `caption_len` on one device may be relied on, other than what follows from the above.
Results may differ from a plain program's by a relative error of at most 0.0085.
The roundings to bfloat16 on the way count: a program that leaves them out, or rounds other values in their place, can miss the bound.
Values may be sent and summed in bfloat16 or wider, within the bound.
No kernel may reach another device: no remote copies, remote signals or barrier semaphores. Data moves between devices by JAX's collectives and lax.ppermute only.
A program may use at most 128 MiB of HBM per device.

v0:
```python
import math

import jax
import jax.numpy as jnp
from jax import lax
from jax.sharding import PartitionSpec as P

HD = 128


def shifted(block, axis, distance):
    devices = range(lax.axis_size(axis))
    route = [(i - distance, i) for i in devices if i - distance in devices]
    return lax.ppermute(block, axis, route)


def normalize(rows):
    wide = rows.astype(jnp.float32)
    square = jnp.mean(wide * wide, axis=-1, keepdims=True)
    return (wide * lax.rsqrt(square + 1e-06)).astype(jnp.bfloat16)


def softmax_rows(scores):
    top = jnp.max(scores, axis=-1, keepdims=True)
    expo = jnp.exp(scores - top)
    return expo / jnp.sum(expo, axis=-1, keepdims=True)


def self_attend(q_head, k_head, v_head):
    score_scale = 1.0 / math.sqrt(HD)
    seq_total = q_head.shape[0]
    block_rows = 512
    blocks = q_head.reshape(seq_total // block_rows, block_rows, q_head.shape[1])

    def one_block(query_block):
        scores = (
            lax.dot_general(
                query_block, k_head, (((1,), (1,)), ((), ())), preferred_element_type=jnp.float32
            )
            * score_scale
        )
        soft = softmax_rows(scores)
        return jnp.dot(soft.astype(jnp.bfloat16), v_head, preferred_element_type=jnp.float32)

    return lax.map(one_block, blocks).reshape(seq_total, q_head.shape[1])


def self_rows(q_head, k_head, v_head, start, count):
    total_rows = q_head.shape[0]
    width = q_head.shape[1]
    computed = self_attend(q_head[start : start + count], k_head, v_head)
    before = jnp.zeros((start, width), jnp.float32)
    after = jnp.zeros((total_rows - start - count, width), jnp.float32)
    return jnp.concatenate([before, computed, after], axis=0)


def cross_attend(q_head, text_kv, cot_head, length):
    score_scale = 1.0 / math.sqrt(HD)
    text_keys = text_kv[:, :HD]
    text_vals = text_kv[:, HD:]
    scores = (
        lax.dot_general(
            q_head, text_keys, (((1,), (1,)), ((), ())), preferred_element_type=jnp.float32
        )
        * score_scale
    )
    live_keys = jnp.arange(text_kv.shape[0], dtype=jnp.int32) < length
    scores = jnp.where(live_keys[None, :], scores, -jnp.inf)
    soft = softmax_rows(scores)
    soft_low = soft.astype(jnp.bfloat16)
    cross_out = jnp.dot(soft_low, text_vals, preferred_element_type=jnp.float32)
    back_soft = lax.dot_general(
        cot_head, text_vals, (((1,), (1,)), ((), ())), preferred_element_type=jnp.float32
    )
    grad_vals = lax.dot_general(
        soft_low, cot_head, (((0,), (0,)), ((), ())), preferred_element_type=jnp.float32
    )
    inner = jnp.sum(soft * back_soft, axis=-1, keepdims=True)
    grad_scores = (soft * (back_soft - inner) * score_scale).astype(jnp.bfloat16)
    grad_keys = lax.dot_general(
        grad_scores, q_head, (((0,), (0,)), ((), ())), preferred_element_type=jnp.float32
    )
    kv_grad = jnp.concatenate([grad_keys, grad_vals], axis=1).astype(jnp.bfloat16)
    return (cross_out, kv_grad)


def project_back(normed, kv_grad):
    return lax.dot_general(
        normed, kv_grad, (((0,), (0,)), ((), ())), preferred_element_type=jnp.float32
    )


def local(queries, keys, values, cotangent, captions, caption_len, proj_weight):
    group_side = lax.axis_index("grp")
    gathered = lax.all_gather(captions, "seq", axis=1, tiled=True)
    weight_full = lax.all_gather(proj_weight, "dp", axis=0, tiled=True)
    values_full, cot_full = (
        lax.all_gather(values, "grp", axis=2, tiled=True),
        lax.all_gather(cotangent, "grp", axis=2, tiled=True),
    )
    normed = normalize(gathered[0])
    blank_kv = jnp.zeros((normed.shape[0], weight_full.shape[1]), jnp.bfloat16)
    text_kv = lax.cond(
        group_side == 0,
        lambda: jnp.dot(normed, weight_full, preferred_element_type=jnp.float32).astype(
            jnp.bfloat16
        ),
        lambda: blank_kv,
    )
    q_rows, k_rows, v_rows, c_rows = (
        lax.all_to_all(queries, "seq", split_axis=2, concat_axis=1, tiled=True),
        lax.all_to_all(keys, "seq", split_axis=2, concat_axis=1, tiled=True),
        lax.all_to_all(values_full, "seq", split_axis=2, concat_axis=1, tiled=True),
        lax.all_to_all(cot_full, "seq", split_axis=2, concat_axis=1, tiled=True),
    )
    q_head = q_rows[0]
    k_head = k_rows[0]
    v_head = v_rows[0]
    c_head = c_rows[0]
    length = caption_len[0]
    seq_total = q_head.shape[0]
    blank_grad = jnp.zeros((normed.shape[1], weight_full.shape[1]), jnp.float32)
    split = seq_total // 2
    arrived = shifted(text_kv, "grp", 1)

    def latent_work():
        cross_out, kv_grad = cross_attend(q_head, arrived, c_head, length)
        return (self_rows(q_head, k_head, v_head, split, seq_total - split) + cross_out, kv_grad)

    def caption_self():
        return (self_rows(q_head, k_head, v_head, 0, split), blank_kv)

    head_out, kv_grad = lax.cond(group_side == 1, latent_work, caption_self)
    returned = shifted(kv_grad, "grp", -1)
    grad_term = lax.cond(
        group_side == 0, lambda: project_back(normed, returned), lambda: blank_grad
    )
    grad_share = lax.psum_scatter(grad_term, "dp", scatter_dimension=0, tiled=True)
    summed, grad_all = lax.psum((head_out, grad_share), "grp")
    whole_rows = lax.all_to_all(
        summed.astype(jnp.bfloat16)[None], "seq", split_axis=1, concat_axis=2, tiled=True
    )
    half_width = whole_rows.shape[2] // 2
    attended = lax.dynamic_slice_in_dim(whole_rows, group_side * half_width, half_width, 2)
    return (attended, grad_all)


def solution(mesh):
    return jax.shard_map(
        local,
        mesh=mesh,
        in_specs=(
            P("dp", "seq", None),
            P("dp", "seq", None),
            P("dp", "seq", "grp"),
            P("dp", "seq", "grp"),
            P("dp", "seq", None),
            P("dp"),
            P("dp", "seq"),
        ),
        out_specs=(P("dp", "seq", "grp"), P("dp", "seq")),
        check_vma=False,
    )
```

profile of v0, /device:TPU:1, one launch (start us, length us, event | category | flops | bytes accessed | tf_op | source)
XLA Modules:
  0.0 804.3 jit_solution(12286619773617785197)
XLA Ops:
  15.0 22.4 %reduce = bf16[4096,128]{1,0:T(8,128)(2,1)S(1)} reduce(bf16[4096,1,128]{2,1,0:T(2,128)(2,1)S(1)} %bitcast.99, bf16[]{:T(256)} %broadcast.77), dimensions={1}, to_apply=%bitcast.46.reduce_sub_computation | reduce | bytes 2097154
  38.5 10.5 %all-to-all-start = ((bf16[32,2,8192]{2,1,0:T(2,128)(2,1)}), bf16[32,2,8192]{2,1,0:T(2,128)(2,1)S(1)}, u32[]{:S(2)}, u32[]{:S(2)}) async-start(bf16[32,2,8192]{2,1,0:T(2,128)(2,1)} %reshape.42), calls=%async_computation | async-start | bytes 2097152 | tf_op jit(solution)/shard_map/all_to_all | solution.py:111
  54.6 23.3 %reduce.1 = bf16[4096,128]{1,0:T(8,128)(2,1)} reduce(bf16[4096,1,128]{2,1,0:T(2,128)(2,1)S(1)} %bitcast.103, bf16[]{:T(256)} %broadcast.77), dimensions={1}, to_apply=%bitcast.48.reduce_sub_computation | reduce | bytes 2097154
  80.1 7.9 all-to-all-start.1
  95.1 23.3 %reduce.2 = bf16[4096,128]{1,0:T(8,128)(2,1)} reduce(bf16[4096,1,128]{2,1,0:T(2,128)(2,1)S(1)} %bitcast.101, bf16[]{:T(256)} %broadcast.77), dimensions={1}, to_apply=%bitcast.50.reduce_sub_computation | reduce | bytes 2097154
  126.1 32.8 %all-gather.11.cloned.1.call-done = bf16[1,128,4096]{2,1,0:T(8,128)(2,1)} async-done(((bf16[1,128,2048]{2,1,0:T(8,128)(2,1)}), bf16[1,128,4096]{2,1,0:T(8,128)(2,1)}) %all-gather.11.cloned.1.call-update) | async-done | bytes 1048592 | tf_op jit(solution)/shard_map/all_gather | solution.py:99
  164.0 23.3 %reduce.3 = bf16[4096,128]{1,0:T(8,128)(2,1)} reduce(bf16[4096,1,128]{2,1,0:T(2,128)(2,1)S(1)} %bitcast.102, bf16[]{:T(256)} %broadcast.77), dimensions={1}, to_apply=%bitcast.52.reduce_sub_computation | reduce | bytes 2097154
  189.5 26.3 %all-gather.7.cloned.1.call-done = bf16[1,512,4096]{2,1,0:T(8,128)(2,1)} async-done(((bf16[1,16,4096]{2,1,0:T(8,128)(2,1)}), bf16[1,512,4096]{2,1,0:T(8,128)(2,1)}) %all-gather.7.cloned.1.call-update) | async-done | bytes 4194320 | tf_op jit(solution)/shard_map/all_gather | solution.py:95
  224.3 5.6 fusion.39
  229.9 52.7 %all-gather.9.cloned.1.call-done = bf16[4096,256]{1,0:T(8,128)(2,1)} async-done(((bf16[512,256]{1,0:T(8,128)(2,1)}), bf16[4096,256]{1,0:T(8,128)(2,1)}) %all-gather.9.cloned.1.call-update) | async-done | bytes 2097168 | tf_op jit(solution)/shard_map/all_gather | solution.py:96
  293.9 5.8 reshape.45
  302.1 5.8 reshape.47
  310.9 5.8 reshape.49
  318.4 34.6 %conditional.4 = (f32[4096,128]{1,0:T(8,128)}, bf16[512,256]{0,1:T(8,128)(2,1)}) conditional(s32[]{:T(128)} %convert_element_type.35, (bf16[4096,128]{1,0:T(8,128)(2,1)S(1)}, bf16[4096,128]{1,0:T(8,128)(2,1)S(1)}, bf16[4096,128]{1,0:T(8,128)(2,1)}) %tuple.106, (bf16[4096,128]{1,0:T(8,128)(2,1)S(1)}, bf16[4096,128]{1,0:T(8,128)(2,1)S(1)}, ...), branch_computations={%region_3.8_spmd, %region_8.16_spmd} | conditional | flops 3843149312 | bytes 182155536 | solution.py:133
  318.5 24.1 %while.18 = (s32[]{:T(128)}, f32[4,512,128]{2,1,0:T(8,128)}, bf16[4,512,128]{2,1,0:T(8,128)(2,1)S(1)}, bf16[4096,128]{1,0:T(8,128)(2,1)S(1)}, bf16[4096,128]{1,0:T(8,128)(2,1)}, /*index=5*/s32[]{:T(128)}) while((s32[]{:T(128)}, f32[4,512,128]{2,1,0:T(8,128)}, bf16[4,512,128]{2,1,0:T(8,128)(2,1)S(1)}, bf16[4096,128]{1,0:T(8,128)(2,1)S(1)}, ...), condition=%wide.region_7.7_spmd, body=%wide.region_4.6_spmd.sunk | while | flops 1092615168 | bytes 31861348 | solution.py:45
  355.4 22.9 %collective-permute-done.1 = bf16[512,256]{1,0:T(8,128)(2,1)S(1)} collective-permute-done((bf16[512,256]{1,0:T(8,128)(2,1)S(1)}, bf16[512,256]{1,0:T(8,128)(2,1)S(1)}, u32[]{:S(2)}, u32[]{:S(2)}) %collective-permute-start.1) | collective-permute-done | bytes 262176 | tf_op jit(solution)/shard_map/ppermute | solution.py:14
  378.4 5.4 conditional.5
  378.4 5.4 fusion.40
  383.8 193.9 %all-reduce.6 = bf16[4096,128]{1,0:T(8,128)(2,1)S(1)} all-reduce(f32[4096,128]{1,0:T(8,128)} %get-tuple-element.105), channel_id=1, replica_groups=mesh['grp'=2,'seq'=32,'dp'=8] {'grp'}, use_global_device_ids=true, to_apply=%region_16.17 | all-reduce | flops 524288 | bytes 3145728 | tf_op jit(solution)/shard_map/psum | solution.py:139
  577.7 16.7 %copy.69 = bf16[1,4096,128]{2,0,1:T(2,128)(2,1)S(1)} copy(bf16[1,4096,128]{2,1,0:T(8,128)(2,1)S(1)} %bitcast.104) | data formatting | bytes 2097152 | tf_op jit(solution)/shard_map/broadcast_in_dim | solution.py:141
  594.4 22.4 %reduce.4 = bf16[4096,128]{1,0:T(8,128)(2,1)S(1)} reduce(bf16[4096,1,128]{2,1,0:T(2,128)(2,1)S(1)} %bitcast.100, bf16[]{:T(256)} %broadcast.77), dimensions={1}, to_apply=%bitcast.73.reduce_sub_computation | reduce | bytes 2097154
  617.9 7.7 all-to-all-start.4
  625.7 25.9 %reduce-scatter.2.cloned.1.call-done = f32[512,256]{1,0:T(8,128)} async-done(((f32[4096,256]{1,0:T(8,128)}), f32[512,256]{1,0:T(8,128)}) %reduce-scatter.2.cloned.1.call-update) | async-done | bytes 524304 | tf_op jit(solution)/shard_map/reduce_scatter | solution.py:138
  654.5 140.8 %all-reduce.5.cloned.1.call-done = f32[512,256]{1,0:T(8,128)} async-done(((f32[512,256]{1,0:T(8,128)}), f32[512,256]{1,0:T(8,128)}) %all-reduce.5.cloned.1.call-update) | async-done | bytes 524304 | tf_op jit(solution)/shard_map/psum | solution.py:139
  (76 shorter events, 105.4 us)
Async XLA Ops:
  7.2 82.9 %all-gather.5.cloned.1.call-start = ((), (), s32[]{:S(2)}) async-start(), calls=%async_computation.6 | async-start | bytes 1572864 | tf_op jit(solution)/shard_map/all_gather | solution.py:98
  7.9 151.0 %all-gather.11.cloned.1.call-start = ((), (), s32[]{:S(2)}) async-start(), calls=%async_computation.9 | async-start | bytes 1572864 | tf_op jit(solution)/shard_map/all_gather | solution.py:99
  8.6 207.1 %all-gather.7.cloned.1.call-start = ((), (), s32[]{:S(2)}) async-start(), calls=%async_computation.7 | async-start | bytes 4325376 | tf_op jit(solution)/shard_map/all_gather | solution.py:95
  38.5 41.6 %all-to-all-start = ((bf16[32,2,8192]{2,1,0:T(2,128)(2,1)}), bf16[32,2,8192]{2,1,0:T(2,128)(2,1)S(1)}, u32[]{:S(2)}, u32[]{:S(2)}) async-start(bf16[32,2,8192]{2,1,0:T(2,128)(2,1)} %reshape.42), calls=%async_computation | async-start | bytes 2097152 | tf_op jit(solution)/shard_map/all_to_all | solution.py:111
  49.0 233.6 %all-gather.9.cloned.1.call-start = ((), (), s32[]{:S(2)}) async-start(), calls=%async_computation.8 | async-start | bytes 2359296 | tf_op jit(solution)/shard_map/all_gather | solution.py:96
  80.1 40.6 %all-to-all-start.1 = ((bf16[32,2,8192]{2,1,0:T(2,128)(2,1)}), bf16[32,2,8192]{2,1,0:T(2,128)(2,1)}, u32[]{:S(2)}, u32[]{:S(2)}) async-start(bf16[32,2,8192]{2,1,0:T(2,128)(2,1)} %reshape.44), calls=%async_computation.1 | async-start | bytes 2097152 | tf_op jit(solution)/shard_map/all_to_all | solution.py:112
  120.7 98.2 %all-to-all-start.2 = ((bf16[32,2,8192]{2,1,0:T(2,128)(2,1)}), bf16[32,2,8192]{2,1,0:T(2,128)(2,1)}, u32[]{:S(2)}, u32[]{:S(2)}) async-start(bf16[32,2,8192]{2,1,0:T(2,128)(2,1)} %reshape.46), calls=%async_computation.2 | async-start | bytes 2097152 | tf_op jit(solution)/shard_map/all_to_all | solution.py:113
  218.9 92.0 %all-to-all-start.3 = ((bf16[32,2,8192]{2,1,0:T(2,128)(2,1)}), bf16[32,2,8192]{2,1,0:T(2,128)(2,1)}, u32[]{:S(2)}, u32[]{:S(2)}) async-start(bf16[32,2,8192]{2,1,0:T(2,128)(2,1)} %reshape.48), calls=%async_computation.3 | async-start | bytes 2097152 | tf_op jit(solution)/shard_map/all_to_all | solution.py:114
  224.2 427.3 %reduce-scatter.2.cloned.1.call-start = ((), (), s32[]{:S(2)}) async-start(), calls=%async_computation.10 | async-start | bytes 4718592 | tf_op jit(solution)/shard_map/reduce_scatter | solution.py:138
  286.7 31.7 %collective-permute-start = (bf16[512,256]{1,0:T(8,128)(2,1)S(1)}, bf16[512,256]{1,0:T(8,128)(2,1)}, u32[]{:S(2)}, u32[]{:S(2)}) collective-permute-start(bf16[512,256]{1,0:T(8,128)(2,1)S(1)} %get-tuple-element.283), channel_id=1, source_target_pairs={{0,256},{1,257},{2,258},{3,259},{4,260},{5,261},{6,262},{7,263},{8... | collective-permute-start | bytes 786440 | tf_op jit(solution)/shard_map/ppermute | solution.py:14
  318.5 2.9 copy-start.2
  324.5 2.8 copy-start.2
  330.5 2.8 copy-start.2
  336.5 2.8 copy-start.2
  354.1 24.2 %collective-permute-start.1 = (bf16[512,256]{1,0:T(8,128)(2,1)S(1)}, bf16[512,256]{1,0:T(8,128)(2,1)S(1)}, u32[]{:S(2)}, u32[]{:S(2)}) collective-permute-start(bf16[512,256]{1,0:T(8,128)(2,1)S(1)} %copy.61), channel_id=1, source_target_pairs={{256,0},{257,1},{258,2},{259,3},{260,4},{261,5},{262,6},{263,7},{2... | collective-permute-start | bytes 786440 | tf_op jit(solution)/shard_map/ppermute | solution.py:14
  617.9 33.6 %all-to-all-start.4 = ((bf16[32,2,8192]{2,1,0:T(2,128)(2,1)}), bf16[32,2,8192]{2,1,0:T(2,128)(2,1)S(1)}, u32[]{:S(2)}, u32[]{:S(2)}) async-start(bf16[32,2,8192]{2,1,0:T(2,128)(2,1)} %reshape.50), calls=%async_computation.4 | async-start | bytes 2097152 | tf_op jit(solution)/shard_map/all_to_all | solution.py:140
  625.6 169.8 %all-reduce.5.cloned.1.call-start = ((), (), s32[]{:S(2)}) async-start(), calls=%async_computation.11 | async-start | bytes 1048576 | tf_op jit(solution)/shard_map/psum | solution.py:139
Sparse Core Ops, SparseCore 0:
  10.1 79.9 all-gather.4
  92.2 66.6 all-gather.10
  162.1 53.6 all-gather.6
  217.7 64.8 all-gather.8
  383.9 267.5 reduce-scatter.1
  654.3 141.0 all-reduce.4
where the time goes:
time: 814 us; the launch traced here: 804 us
  waiting for transfers between devices  306 us (38%)
  blocking collectives  194 us (24%)
  other arithmetic  130 us (16%)
  local copies, waits for them, and re-layouts  81.8 us (10%)
  starting transfers between devices  43.5 us (5%)
  matrix products  27.5 us (3%)
  between operations  14.5 us (2%)
    psum x1, blocking collectives, local(): summed, grad_all = lax.psum((head_out, grad_share), 'grp')  194 us
    psum x1, waiting for transfers between devices, local(): summed, grad_all = lax.psum((head_out, grad_share), 'grp')  141 us
    unnamed x5, other arithmetic  115 us
    all_gather x1, waiting for transfers between devices, local(): weight_full = lax.all_gather(proj_weight, 'dp', axis=0, tiled=True)  52.7 us
    unnamed x20, local copies, waits for them, and re-layouts  47.1 us
    all_gather x1, waiting for transfers between devices, local(): lax.all_gather(cotangent, 'grp', axis=2, tiled=True)  32.8 us
    all_gather x1, waiting for transfers between devices, local(): gathered = lax.all_gather(captions, 'seq', axis=1, tiled=True)  26.3 us
    reduce_scatter x1, waiting for transfers between devices, local(): lax.psum_scatter(grad_term, 'dp', scatter_dimension=0, tiled=True)  25.9 us
  transfers between devices with their start and end apart: 13, of which 7 were waited for; matrix products, arithmetic and copies ran while one was open for 25% of the time, Pallas kernels for 0%

commit v1 on v0

v1 whole, which is shorter than its diff:
```python
import math

import jax
import jax.numpy as jnp
from jax import lax
from jax.experimental import pallas as pl
from jax.experimental.pallas import tpu as pltpu
from jax.sharding import Mesh
from jax.sharding import PartitionSpec as P

HD = 128
SCALE = 1.0 / math.sqrt(HD)
LOG2E = math.log2(math.e)
PLANE = ("y", "x", "c")
CHIPS = ("y", "x")
RING = ("g", "d")
NT = (((1,), (1,)), ((), ()))
TN = (((0,), (0,)), ((), ()))
VMEM = 48 * 1024 * 1024
SWAP = [(0, 1), (1, 0)]


def normalize(rows):
    wide = rows.astype(jnp.float32)
    square = jnp.mean(wide * wide, axis=-1, keepdims=True)
    return (wide * lax.rsqrt(square + 1e-06)).astype(jnp.bfloat16)


def pack_kernel(side_ref, wide_ref, half_ref, out_ref):
    rows = out_ref.shape[2]
    for dest in range(out_ref.shape[0]):
        head, part = dest // 2, dest % 2
        for slot, ref in enumerate((wide_ref, half_ref)):
            out_ref[dest, slot] = ref[0, part * rows : (part + 1) * rows, head * HD : (head + 1) * HD]


def pack(side, wide, half):
    _, rows, width = half.shape
    dests = 2 * width // HD
    return pl.pallas_call(
        pack_kernel,
        grid_spec=pltpu.PrefetchScalarGridSpec(
            num_scalar_prefetch=1,
            grid=(1,),
            in_specs=[
                pl.BlockSpec((1, rows, width), lambda j, side_ref: (0, 0, side_ref[0])),
                pl.BlockSpec((1, rows, width), lambda j, side_ref: (0, 0, 0)),
            ],
            out_specs=pl.BlockSpec((dests, 2, rows // 2, HD), lambda j, side_ref: (0, 0, 0, 0)),
        ),
        out_shape=jax.ShapeDtypeStruct((dests, 2, rows // 2, HD), half.dtype),
        compiler_params=pltpu.CompilerParams(vmem_limit_bytes=VMEM),
        cost_estimate=pl.CostEstimate(flops=0, bytes_accessed=4 * rows * width * 2, transcendentals=0),
        name="pack",
    )(side, wide, half)


def unpack_kernel(in_ref, out_ref):
    rows = in_ref.shape[1]
    for source in range(in_ref.shape[0]):
        head, part = source // 2, source % 2
        out_ref[0, part * rows : (part + 1) * rows, head * HD : (head + 1) * HD] = in_ref[source]


def unpack(pieces):
    sources, rows, _ = pieces.shape
    width = sources // 2 * HD
    return pl.pallas_call(
        unpack_kernel,
        out_shape=jax.ShapeDtypeStruct((1, 2 * rows, width), pieces.dtype),
        compiler_params=pltpu.CompilerParams(vmem_limit_bytes=VMEM),
        cost_estimate=pl.CostEstimate(flops=0, bytes_accessed=8 * rows * width, transcendentals=0),
        name="unpack",
    )(pieces)


def project_kernel(spot_ref, rows_ref, own_ref, taken_ref, other_ref, out_ref):
    here, core = spot_ref[0], spot_ref[1]
    reach, depth, _ = taken_ref.shape
    n_dp = rows_ref.shape[1] // depth

    def part(block, weight):
        columns = pl.ds(pl.multiple_of(lax.rem(block + 2 * n_dp, n_dp) * depth, depth), depth)
        return jnp.dot(rows_ref[:, columns], weight, preferred_element_type=jnp.float32)

    way = 1 - 2 * core
    total = part(here, own_ref[...])
    for t in range(1, reach):
        total += part(here - way * t, taken_ref[t - 1])
        total += part(here + way * t, other_ref[t - 1])
    last = jnp.where(core == 0, taken_ref[reach - 1], other_ref[reach - 1])
    total += part(here - reach, last)
    out_ref[...] = total.astype(out_ref.dtype)


def project(spot, rows, own, taken, other):
    vmem = pl.BlockSpec(memory_space=pltpu.VMEM)
    return pl.pallas_call(
        project_kernel,
        in_specs=[pl.BlockSpec(memory_space=pltpu.SMEM), vmem, vmem, vmem, vmem],
        out_specs=vmem,
        out_shape=jax.ShapeDtypeStruct((rows.shape[0], own.shape[1]), jnp.bfloat16),
        compiler_params=pltpu.CompilerParams(vmem_limit_bytes=VMEM),
        cost_estimate=pl.CostEstimate(
            flops=2 * rows.size * own.shape[1], bytes_accessed=2 * (rows.size + 2 * taken.size), transcendentals=0
        ),
        name="project",
    )(spot, rows, own, taken, other)


def cross_kernel(length_ref, q_ref, c_ref, kv_ref, out_ref, grad_ref):
    step = pl.program_id(0)
    block = out_ref.shape[0]
    tokens = kv_ref.shape[0]
    q = q_ref[:, 0].reshape(block, HD)
    cot = c_ref[:, 0].reshape(block, HD)
    text_keys = kv_ref[:, :HD]
    text_vals = kv_ref[:, HD:]
    place = lax.broadcasted_iota(jnp.int32, (tokens, 1), 0)
    half = tokens // 2
    part = jnp.where(place >= half, 1, 0)
    inside = place - part * half
    token = (inside >> 4) * 32 + part * 16 + (inside & 15)
    live = token < length_ref[0]
    scores = lax.dot_general(text_keys, q, NT, preferred_element_type=jnp.float32) * SCALE
    scores = jnp.where(live, scores, -jnp.inf)
    top = jnp.max(scores, axis=0, keepdims=True)
    expo = jnp.exp(scores - top)
    soft = expo / jnp.sum(expo, axis=0, keepdims=True)
    soft_low = soft.astype(jnp.bfloat16)
    out_t = lax.dot_general(text_vals, soft_low, TN, preferred_element_type=jnp.float32)
    out_ref[...] = out_t.T
    back = lax.dot_general(text_vals, cot, NT, preferred_element_type=jnp.float32)
    inner = jnp.sum(soft * back, axis=0, keepdims=True)
    grad_scores = (soft * (back - inner) * SCALE).astype(jnp.bfloat16)
    grad_keys = jnp.dot(grad_scores, q, preferred_element_type=jnp.float32)
    grad_vals = jnp.dot(soft_low, cot, preferred_element_type=jnp.float32)

    @pl.when(step == 0)
    def _():
        grad_ref[:, :HD] = grad_keys
        grad_ref[:, HD:] = grad_vals

    @pl.when(step > 0)
    def _():
        grad_ref[:, :HD] += grad_keys
        grad_ref[:, HD:] += grad_vals


def cross_attend(length, q_cot, text_kv, blocks=4):
    sources, _, rows, _ = q_cot.shape
    queries = sources * rows
    tokens = text_kv.shape[0]
    return pl.pallas_call(
        cross_kernel,
        grid_spec=pltpu.PrefetchScalarGridSpec(
            num_scalar_prefetch=1,
            grid=(blocks,),
            in_specs=[
                pl.BlockSpec((sources // blocks, 1, rows, HD), lambda j, n: (j, 0, 0, 0)),
                pl.BlockSpec((sources // blocks, 1, rows, HD), lambda j, n: (j, 1, 0, 0)),
                pl.BlockSpec((tokens, 2 * HD), lambda j, n: (0, 0)),
            ],
            out_specs=[
                pl.BlockSpec((queries // blocks, HD), lambda j, n: (j, 0)),
                pl.BlockSpec((tokens, 2 * HD), lambda j, n: (0, 0)),
            ],
        ),
        out_shape=[
            jax.ShapeDtypeStruct((queries, HD), jnp.float32),
            jax.ShapeDtypeStruct((tokens, 2 * HD), jnp.float32),
        ],
        compiler_params=pltpu.CompilerParams(vmem_limit_bytes=VMEM),
        cost_estimate=pl.CostEstimate(
            flops=10 * queries * tokens * HD, bytes_accessed=3 * 1024 * 1024, transcendentals=queries * tokens
        ),
        name="cross",
    )(length, q_cot, q_cot, text_kv)


def self_kernel(q_ref, near_ref, far_ref, cross_ref, out_ref):
    block = out_ref.shape[0]
    half = near_ref.shape[0] * near_ref.shape[2]
    q = q_ref[:, 0].reshape(block, HD)
    scores = [
        lax.dot_general(q, ref[:, 0].reshape(half, HD), NT, preferred_element_type=jnp.float32)
        for ref in (near_ref, far_ref)
    ]
    top = jnp.maximum(*[jnp.max(s, axis=1, keepdims=True) for s in scores])
    total = 0.0
    out = 0.0
    for s, ref in zip(scores, (near_ref, far_ref)):
        expo = jnp.exp2((s - top) * (SCALE * LOG2E))
        total += jnp.sum(expo, axis=1, keepdims=True)
        out += jnp.dot(
            expo.astype(jnp.bfloat16), ref[:, 1].reshape(half, HD), preferred_element_type=jnp.float32
        )
    out_ref[...] = (out / total + cross_ref[...]).astype(out_ref.dtype)


def self_attend(q_cot, near, far, cross_out, blocks=8):
    sources, _, rows, _ = q_cot.shape
    queries = sources * rows
    whole = pl.BlockSpec(near.shape, lambda j: (0, 0, 0, 0))
    return pl.pallas_call(
        self_kernel,
        grid=(blocks,),
        in_specs=[
            pl.BlockSpec((sources // blocks, 1, rows, HD), lambda j: (j, 0, 0, 0)),
            whole,
            whole,
            pl.BlockSpec((queries // blocks, HD), lambda j: (j, 0)),
        ],
        out_specs=pl.BlockSpec((queries // blocks, HD), lambda j: (j, 0)),
        out_shape=jax.ShapeDtypeStruct((queries, HD), jnp.bfloat16),
        compiler_params=pltpu.CompilerParams(vmem_limit_bytes=VMEM),
        cost_estimate=pl.CostEstimate(
            flops=8 * queries * queries * HD, bytes_accessed=5 * 1024 * 1024, transcendentals=2 * queries * queries
        ),
        name="self_attention",
    )(q_cot, near, far, cross_out)


def local(queries, keys, values, cotangent, captions, caption_len, proj_weight):
    side = lax.axis_index("g")
    core = lax.axis_index("c")
    n_ring = lax.axis_size("g") * lax.axis_size("d")
    n_dp = lax.axis_size("d")
    n_chips = lax.axis_size("y") * lax.axis_size("x")
    sides = lax.axis_size("g")
    side_arg = side.astype(jnp.int32).reshape(1)

    normed = normalize(captions[0])
    rows, features = normed.shape

    mine = lax.ppermute(
        proj_weight, PLANE, [(n_chips * c + i, sides * i + c) for c in range(sides) for i in range(n_chips)]
    )
    def place(z, c):
        g, d = divmod(z % n_ring, n_dp)
        return (g * sides + c) * n_dp + d

    def from_plane(distance, to):
        pairs = []
        for z in range(n_ring):
            g = z // n_dp
            pairs.append((place(z - distance, g), place(z, to)))
        return lax.ppermute(mine, ("g", "c", "d"), pairs)

    moved = lax.ppermute(
        mine, ("g", "c", "d"), [(place(z, z // n_dp), place(z, 1 - z // n_dp)) for z in range(n_ring)]
    )
    own = jnp.where(core == side, mine, moved)
    reach = n_dp // 2
    taken = []
    for t in range(1, reach + 1):
        block = from_plane(t, 0)
        if t < reach:
            block = jnp.where(core == 0, block, from_plane(-t, 1))
        taken.append(block)
    taken = jnp.stack(taken)
    other = lax.ppermute(taken, "c", SWAP)

    half_rows = lax.all_to_all(
        jnp.broadcast_to(normed[None], (n_chips, rows, features)), CHIPS, 0, 0, tiled=True
    ).reshape(n_chips * rows, features)
    spot = jnp.stack([lax.axis_index("d"), core]).astype(jnp.int32)
    text_half = project(spot, half_rows, own, taken, other)
    text_kv = lax.all_gather(text_half, "c", axis=0, tiled=True)

    q_cot = lax.all_to_all(pack(side_arg, queries, cotangent), PLANE, 0, 0, tiled=True)
    cross_out, kv_part = cross_attend(caption_len, q_cot, text_kv)

    half_tokens = kv_part.shape[0] // 2
    keep = lax.dynamic_slice_in_dim(kv_part, core * half_tokens, half_tokens, 0)
    give = lax.dynamic_slice_in_dim(kv_part, (1 - core) * half_tokens, half_tokens, 0)
    kv_half = (keep + lax.ppermute(give, "c", SWAP)).astype(jnp.bfloat16)
    kv_home = lax.ppermute(
        kv_half,
        ("g",) + PLANE,
        [
            (g * 2 * n_chips + 2 * i + c, c * 2 * n_chips + n_chips * g + i)
            for g in range(sides)
            for i in range(n_chips)
            for c in range(2)
        ],
    )
    kv_all = lax.all_gather(kv_home, RING, axis=0, tiled=True)

    blocks = normed.reshape(rows, n_dp, features // n_dp).transpose(1, 0, 2)
    by_sample = lax.all_to_all(blocks, "d", 0, 0, tiled=True)
    spread = lax.all_gather(by_sample, ("c",) + CHIPS, axis=0, tiled=False)
    spread = spread.reshape(2, n_chips, n_dp, rows, features // n_dp).transpose(0, 2, 1, 3, 4)
    spread = spread.reshape(2 * n_chips * n_dp * rows, features // n_dp)

    near = lax.all_to_all(pack(side_arg, keys, values), PLANE, 0, 0, tiled=True)
    far = lax.ppermute(near, "c", SWAP)
    out_rows = self_attend(q_cot, near, far, cross_out)
    back = lax.all_to_all(out_rows.reshape(near.shape[0], near.shape[2], HD), PLANE, 0, 0, tiled=True)
    attended = unpack(back)

    proj_grad = lax.dot_general(spread, kv_all, TN, preferred_element_type=jnp.float32)
    return attended, proj_grad


def solution(mesh):
    inner = Mesh(mesh.devices.reshape(2, 4, 4, 2, 8), ("g", "y", "x", "c", "d"))
    return jax.shard_map(
        local,
        mesh=inner,
        in_specs=(
            P("d", PLANE, None),
            P("d", PLANE, None),
            P("d", PLANE, "g"),
            P("d", PLANE, "g"),
            P("d", PLANE, None),
            P("d"),
            P("d", PLANE),
        ),
        out_specs=(P("d", PLANE, "g"), P("d", PLANE)),
        check_vma=False,
    )
```

time: 814 us -> 251 us (0.31); the launches traced: 804 us -> 250 us
  waiting for transfers between devices: 306 us -> 47.7 us
  other arithmetic: 130 us -> 4.39 us
  blocking collectives: 194 us -> 71.3 us
  local copies, waits for them, and re-layouts: 81.8 us -> 11.3 us
  Pallas kernels: 0 us -> 26.9 us
  starting transfers between devices: 43.5 us -> 68.2 us
  matrix products: 27.5 us -> 4.94 us
    psum x1 -> x0, blocking collectives: 194 us -> none  [local(): summed, grad_all = lax.psum((head_out, grad_share), 'grp')]
    psum x1 -> x0, waiting for transfers between devices: 141 us -> none  [local(): summed, grad_all = lax.psum((head_out, grad_share), 'grp')]
    unnamed x5 -> x0, other arithmetic: 115 us -> none
    all_gather x4 -> x2, waiting for transfers between devices: 114 us -> 0.01 us  [the longest x1 0.01 us: local(): spread = lax.all_gather(by_sample, ('c',) + CHIPS, axis=0, tiled=False)]
    all_to_all x0 -> x3, blocking collectives: none -> 69.3 us  [the longest x1 30.9 us: local(): near = lax.all_to_all(pack(side_arg, keys, values), PLANE, 0, 0, tiled=True)]
    unnamed x20 -> x15, local copies, waits for them, and re-layouts: 47.1 us -> 4.84 us
    ppermute x2 -> x13, starting transfers between devices: 6.59 us -> 47.3 us  [the longest x7 18.7 us: from_plane(): return lax.ppermute(mine, ('g', 'c', 'd'), pairs)]
    pallas_call x0 -> x6, Pallas kernels: none -> 26.9 us  [the longest x1 16.7 us: self_attend(): pl.pallas_call(self_kernel, grid=(blocks,), in_specs=[pl.BlockSpec((sourc...]
  transfers between devices with their start and end apart: 13 -> 17, of which waited for: 7 -> 8; matrix products, arithmetic and copies ran while one was open for 25% -> 4% of each run, Pallas kernels for 0% -> 11%
where the time goes in v1:
time: 251 us; the launch traced here: 250 us
  blocking collectives  71.3 us (28%)
  starting transfers between devices  68.2 us (27%)
  waiting for transfers between devices  47.7 us (19%)
  Pallas kernels  26.9 us (11%)
  between operations  15 us (6%)
  local copies, waits for them, and re-layouts  11.3 us (5%)
  matrix products  4.94 us (2%)
  other arithmetic  4.39 us (2%)
    all_to_all x1, blocking collectives, local(): near = lax.all_to_all(pack(side_arg, keys, values), PLANE, 0, 0, tiled=True)  30.9 us
    all_to_all x1, blocking collectives, local(): by_sample = lax.all_to_all(blocks, 'd', 0, 0, tiled=True)  23.3 us
    ppermute x1, waiting for transfers between devices, local(): lax.ppermute(proj_weight, PLANE, [(n_chips * c + i, sides * i + c) for c...  23.2 us
    ppermute x7, starting transfers between devices, from_plane(): return lax.ppermute(mine, ('g', 'c', 'd'), pairs)  18.7 us
    pallas_call x1, Pallas kernels, self_attend(): pl.pallas_call(self_kernel, grid=(blocks,), in_specs=[pl.BlockSpec((sourc...  16.7 us
    all_to_all x1, blocking collectives, local(): lax.all_to_all(out_rows.reshape(near.shape[0], near.shape[2], HD), PLANE,...  15.1 us
    all_to_all x1, starting transfers between devices, local(): lax.all_to_all(pack(side_arg, queries, cotangent), PLANE, 0, 0, tiled=True)  13.9 us
    ppermute x1, starting transfers between devices, local(): lax.ppermute(kv_half, ('g',) + PLANE, [(g * 2 * n_chips + 2 * i + c, c *...  9.71 us
  transfers between devices with their start and end apart: 17, of which 8 were waited for; matrix products, arithmetic and copies ran while one was open for 4% of the time, Pallas kernels for 11%

profile of v1, /device:TPU:1, one launch (start us, length us, event | category | flops | bytes accessed | tf_op | source)
XLA Modules:
  0.0 249.8 jit_solution(2555940929311046723)
XLA Ops:
  9.4 23.3 %all_to_all.25 = bf16[8,16,512]{2,1,0:T(8,128)(2,1)} all-to-all(bf16[8,16,512]{2,1,0:T(8,128)(2,1)S(1)} %copy.14), channel_id=1, replica_groups=mesh['g'=2,'y'=4,'x'=4,'c'=2,'d'=8] {'d'}, dimensions={0} | all-to-all | bytes 262144 | tf_op jit(solution)/shard_map/all_to_all | solution.py:291
  35.3 6.9 %all-to-all-start.2 = ((bf16[16,16,4096]{2,1,0:T(8,128)(2,1)}), bf16[16,16,4096]{2,1,0:T(8,128)(2,1)S(1)}, u32[]{:S(2)}, u32[]{:S(2)}) async-start(bf16[16,16,4096]{2,1,0:T(8,128)(2,1)} %broadcast_in_dim.10), calls=%async_computation.2 | async-start | bytes 4194304 | tf_op jit(solution)/shard_map/all_to_all | solution.py:264
  42.2 6.3 %collective-permute-start.1 = (bf16[512,256]{1,0:T(8,128)(2,1)S(1)}, bf16[512,256]{1,0:T(8,128)(2,1)S(1)}, u32[]{:S(2)}, u32[]{:S(2)}) collective-permute-start(bf16[512,256]{1,0:T(8,128)(2,1)S(1)} %copy-done.6), channel_id=1, source_target_pairs={{0,0},{8,16},{16,32},{24,48},{32,64},{40,80},{48,96},{56,112},{64,... | collective-permute-start | bytes 786440 | tf_op jit(solution)/shard_map/ppermute | solution.py:236
  48.5 23.2 %collective-permute-done.1 = bf16[512,256]{1,0:T(8,128)(2,1)S(1)} collective-permute-done((bf16[512,256]{1,0:T(8,128)(2,1)S(1)}, bf16[512,256]{1,0:T(8,128)(2,1)S(1)}, u32[]{:S(2)}, u32[]{:S(2)}) %collective-permute-start.1) | collective-permute-done | bytes 262176 | tf_op jit(solution)/shard_map/ppermute | solution.py:236
  72.4 3.1 %collective-permute-start.8 = (bf16[512,256]{1,0:T(8,128)(2,1)S(1)}, bf16[512,256]{1,0:T(8,128)(2,1)S(1)}, u32[]{:S(2)}, u32[]{:S(2)}) collective-permute-start(bf16[512,256]{1,0:T(8,128)(2,1)S(1)} %collective-permute-done.1), channel_id=1, source_target_pairs={{3,8},{4,9},{5,10},{6,11},{7,12},{256,13},{257,14},{258,15},{267,2... | collective-permute-start | bytes 786440 | tf_op jit(solution)/shard_map/ppermute | solution.py:248
  76.2 5.5 %collective-permute-start.6 = (bf16[512,256]{1,0:T(8,128)(2,1)S(1)}, bf16[512,256]{1,0:T(8,128)(2,1)S(1)}, u32[]{:S(2)}, u32[]{:S(2)}) collective-permute-start(bf16[512,256]{1,0:T(8,128)(2,1)S(1)} %collective-permute-done.1), channel_id=1, source_target_pairs={{2,8},{3,9},{4,10},{5,11},{6,12},{7,13},{256,14},{257,15},{266,264... | collective-permute-start | bytes 786440 | tf_op jit(solution)/shard_map/ppermute | solution.py:248
  83.1 4.2 %collective-permute-done.8 = bf16[512,256]{1,0:T(8,128)(2,1)S(1)} collective-permute-done((bf16[512,256]{1,0:T(8,128)(2,1)S(1)}, bf16[512,256]{1,0:T(8,128)(2,1)S(1)}, u32[]{:S(2)}, u32[]{:S(2)}) %collective-permute-start.8) | collective-permute-done | bytes 262176 | tf_op jit(solution)/shard_map/ppermute | solution.py:248
  87.3 7.3 %collective-permute-start.4 = (bf16[512,256]{1,0:T(8,128)(2,1)S(1)}, bf16[512,256]{1,0:T(8,128)(2,1)S(1)}, u32[]{:S(2)}, u32[]{:S(2)}) collective-permute-start(bf16[512,256]{1,0:T(8,128)(2,1)S(1)} %collective-permute-done.1), channel_id=1, source_target_pairs={{1,8},{2,9},{3,10},{4,11},{5,12},{6,13},{7,14},{256,15},{265,264},... | collective-permute-start | bytes 786440 | tf_op jit(solution)/shard_map/ppermute | solution.py:248
  94.8 3.2 %collective-permute-done.4 = bf16[512,256]{1,0:T(8,128)(2,1)S(1)} collective-permute-done((bf16[512,256]{1,0:T(8,128)(2,1)S(1)}, bf16[512,256]{1,0:T(8,128)(2,1)S(1)}, u32[]{:S(2)}, u32[]{:S(2)}) %collective-permute-start.4) | collective-permute-done | bytes 262176 | tf_op jit(solution)/shard_map/ppermute | solution.py:248
  98.1 6.8 %collective-permute-start.10 = (bf16[4,512,256]{2,1,0:T(8,128)(2,1)S(1)}, bf16[4,512,256]{2,1,0:T(8,128)(2,1)}, u32[]{:S(2)}, u32[]{:S(2)}) collective-permute-start(bf16[4,512,256]{2,1,0:T(8,128)(2,1)S(1)} %pad_maximum_fusion.taken_ref), channel_id=1, source_target_pairs={{0,8},{8,0},{1,9},{9,1},{2,10},{10,2},{3,11},{11,3},{4,12},{12,4},... | collective-permute-start | bytes 3145736 | tf_op jit(solution)/shard_map/ppermute | solution.py:262
  108.4 13.9 %all-to-all-start = ((bf16[32,2,64,128]{3,2,1,0:T(8,128)(2,1)}), bf16[32,2,64,128]{3,2,1,0:T(8,128)(2,1)}, u32[]{:S(2)}, u32[]{:S(2)}) async-start(bf16[32,2,64,128]{3,2,1,0:T(8,128)(2,1)} %copy-done), calls=%async_computation | async-start | bytes 2097152 | tf_op jit(solution)/shard_map/all_to_all | solution.py:271
  128.9 2.0 all_gather.12.kv_ref
  130.9 8.6 %all-to-all-done.q_ref.c_ref = bf16[32,2,64,128]{3,2,1,0:T(8,128)(2,1)} async-done(((bf16[32,2,64,128]{3,2,1,0:T(8,128)(2,1)}), bf16[32,2,64,128]{3,2,1,0:T(8,128)(2,1)}, u32[]{:S(2)}, u32[]{:S(2)}) %all-to-all-start) | async-done | bytes 1048608 | tf_op jit(solution)/shard_map/all_to_all | solution.py:271
  139.6 6.9 %cross.1 = (f32[2048,128]{1,0:T(8,128)S(1)}, f32[512,256]{1,0:T(8,128)S(1)}) custom-call(s32[1]{0:T(128)S(6)} %copy.17.length_ref, bf16[32,2,64,128]{3,2,1,0:T(8,128)(2,1)} %all-to-all-done.q_ref.c_ref, bf16[32,2,64,128]{3,2,1,0:T(8,128)(2,1)} %all-to-all-done.q_ref.c_ref, bf16[512,256]{1,0:T(8,128)(2,1)S(1)} %all_gather.12.kv_ref), custom_call_target="tpu_custom_call" | custom-call | flops 1342177280 | bytes 3145728 | tf_op jit(solution)/shard_map/cross/pallas_call | solution.py:154
  146.5 2.3 collective-permute-start.11
  151.0 9.7 %collective-permute-start.12 = (bf16[256,256]{1,0:T(8,128)(2,1)S(1)}, bf16[256,256]{1,0:T(8,128)(2,1)S(1)}, u32[]{:S(2)}, u32[]{:S(2)}) collective-permute-start(bf16[256,256]{1,0:T(8,128)(2,1)S(1)} %add_convert_fusion), channel_id=1, source_target_pairs={{0,0},{8,256},{16,8},{24,264},{32,16},{40,272},{48,24},{56,280},{6... | collective-permute-start | bytes 393224 | tf_op jit(solution)/shard_map/ppermute | solution.py:278
  160.8 3.3 %collective-permute-done.12 = bf16[256,256]{1,0:T(8,128)(2,1)S(1)} collective-permute-done((bf16[256,256]{1,0:T(8,128)(2,1)S(1)}, bf16[256,256]{1,0:T(8,128)(2,1)S(1)}, u32[]{:S(2)}, u32[]{:S(2)}) %collective-permute-start.12) | collective-permute-done | bytes 131104 | tf_op jit(solution)/shard_map/ppermute | solution.py:278
  165.0 30.9 %all_to_all.26.near_ref = bf16[32,2,64,128]{3,2,1,0:T(8,128)(2,1)S(1)} all-to-all(bf16[32,2,64,128]{3,2,1,0:T(8,128)(2,1)S(1)} %pack.3), channel_id=1, replica_groups=mesh['g'=2,'y'=4,'x'=4,'c'=2,'d'=8] {'y','x','c'}, dimensions={0} | all-to-all | bytes 2097152 | tf_op jit(solution)/shard_map/all_to_all | solution.py:296
  195.9 2.3 collective-permute-start
  198.2 2.3 collective-permute-done.far_ref
  200.5 16.7 %self_attention.1 = bf16[2048,128]{1,0:T(8,128)(2,1)S(1)} custom-call(bf16[32,2,64,128]{3,2,1,0:T(8,128)(2,1)} %all-to-all-done.q_ref.c_ref, bf16[32,2,64,128]{3,2,1,0:T(8,128)(2,1)S(1)} %all_to_all.26.near_ref, bf16[32,2,64,128]{3,2,1,0:T(8,128)(2,1)S(1)} %collective-permute-done.far_ref, f32[2048,128]{1,0:T(8,128)S(1)} %get-tuple-element.4.cross_ref), custom_call_target="tpu_custom_call" | custom-call | flops 4294967296 | bytes 5242880 | tf_op jit(solution)/shard_map/self_attention/pallas_call | solution.py:205
  217.2 15.1 %all_to_all.27.in_ref = bf16[32,64,128]{2,1,0:T(8,128)(2,1)S(1)} all-to-all(bf16[32,64,128]{2,1,0:T(8,128)(2,1)S(1)} %bitcast.29), channel_id=1, replica_groups=mesh['g'=2,'y'=4,'x'=4,'c'=2,'d'=8] {'y','x','c'}, dimensions={0} | all-to-all | bytes 1048576 | tf_op jit(solution)/shard_map/all_to_all | solution.py:299
  233.2 4.8 %copy.15 = bf16[2,8,16,16,512]{4,3,2,1,0:T(8,128)(2,1)} copy(bf16[2,8,16,16,512]{4,3,1,2,0:T(8,128)(2,1)} %bitcast.30) | data formatting | bytes 8388608 | tf_op jit(solution)/shard_map/transpose | solution.py:293
  238.0 4.9 %fusion.2 = f32[512,256]{1,0:T(8,128)} fusion(bf16[4096,512]{1,0:T(8,128)(2,1)} %bitcast.31, bf16[4096,256]{1,0:T(8,128)(2,1)} %all-gather.4.cloned.1.call-done), kind=kOutput, calls=%fused_computation.14 | convolution fusion | flops 1073741824 | bytes 6815744 | tf_op jit(solution)/shard_map/dot_general | solution.py:302
  (53 shorter events, 21.1 us)
Async XLA Ops:
  7.2 226.0 %all-gather.6.cloned.1.call-start = ((), (), s32[]{:S(2)}) async-start(), calls=%async_computation.6 | async-start | bytes 4325376 | tf_op jit(solution)/shard_map/all_gather | solution.py:292
  35.3 6.9 %copy-start.6 = (bf16[512,256]{1,0:T(8,128)(2,1)S(1)}, bf16[512,256]{1,0:T(8,128)(2,1)}, u32[]{:S(2)}) copy-start(bf16[512,256]{1,0:T(8,128)(2,1)} %param.13) | copy-start | bytes 786436
  35.3 73.1 %all-to-all-start.2 = ((bf16[16,16,4096]{2,1,0:T(8,128)(2,1)}), bf16[16,16,4096]{2,1,0:T(8,128)(2,1)S(1)}, u32[]{:S(2)}, u32[]{:S(2)}) async-start(bf16[16,16,4096]{2,1,0:T(8,128)(2,1)} %broadcast_in_dim.10), calls=%async_computation.2 | async-start | bytes 4194304 | tf_op jit(solution)/shard_map/all_to_all | solution.py:264
  42.2 29.5 %collective-permute-start.1 = (bf16[512,256]{1,0:T(8,128)(2,1)S(1)}, bf16[512,256]{1,0:T(8,128)(2,1)S(1)}, u32[]{:S(2)}, u32[]{:S(2)}) collective-permute-start(bf16[512,256]{1,0:T(8,128)(2,1)S(1)} %copy-done.6), channel_id=1, source_target_pairs={{0,0},{8,16},{16,32},{24,48},{32,64},{40,80},{48,96},{56,112},{64,... | collective-permute-start | bytes 786440 | tf_op jit(solution)/shard_map/ppermute | solution.py:236
  71.7 10.7 %collective-permute-start.7 = (bf16[512,256]{1,0:T(8,128)(2,1)S(1)}, bf16[512,256]{1,0:T(8,128)(2,1)S(1)}, u32[]{:S(2)}, u32[]{:S(2)}) collective-permute-start(bf16[512,256]{1,0:T(8,128)(2,1)S(1)} %collective-permute-done.1), channel_id=1, source_target_pairs={{261,0},{262,1},{263,2},{0,3},{1,4},{2,5},{3,6},{4,7},{13,256},{14... | collective-permute-start | bytes 786440 | tf_op jit(solution)/shard_map/ppermute | solution.py:248
  72.4 14.9 %collective-permute-start.8 = (bf16[512,256]{1,0:T(8,128)(2,1)S(1)}, bf16[512,256]{1,0:T(8,128)(2,1)S(1)}, u32[]{:S(2)}, u32[]{:S(2)}) collective-permute-start(bf16[512,256]{1,0:T(8,128)(2,1)S(1)} %collective-permute-done.1), channel_id=1, source_target_pairs={{3,8},{4,9},{5,10},{6,11},{7,12},{256,13},{257,14},{258,15},{267,2... | collective-permute-start | bytes 786440 | tf_op jit(solution)/shard_map/ppermute | solution.py:248
  75.5 19.2 %collective-permute-start.5 = (bf16[512,256]{1,0:T(8,128)(2,1)S(1)}, bf16[512,256]{1,0:T(8,128)(2,1)S(1)}, u32[]{:S(2)}, u32[]{:S(2)}) collective-permute-start(bf16[512,256]{1,0:T(8,128)(2,1)S(1)} %collective-permute-done.1), channel_id=1, source_target_pairs={{262,0},{263,1},{0,2},{1,3},{2,4},{3,5},{4,6},{5,7},{14,256},{15,2... | collective-permute-start | bytes 786440 | tf_op jit(solution)/shard_map/ppermute | solution.py:248
  76.2 18.5 %collective-permute-start.6 = (bf16[512,256]{1,0:T(8,128)(2,1)S(1)}, bf16[512,256]{1,0:T(8,128)(2,1)S(1)}, u32[]{:S(2)}, u32[]{:S(2)}) collective-permute-start(bf16[512,256]{1,0:T(8,128)(2,1)S(1)} %collective-permute-done.1), channel_id=1, source_target_pairs={{2,8},{3,9},{4,10},{5,11},{6,12},{7,13},{256,14},{257,15},{266,264... | collective-permute-start | bytes 786440 | tf_op jit(solution)/shard_map/ppermute | solution.py:248
  81.7 16.3 %collective-permute-start.9 = (bf16[512,256]{1,0:T(8,128)(2,1)S(1)}, bf16[512,256]{1,0:T(8,128)(2,1)S(1)}, u32[]{:S(2)}, u32[]{:S(2)}) collective-permute-start(bf16[512,256]{1,0:T(8,128)(2,1)S(1)} %collective-permute-done.1), channel_id=1, source_target_pairs={{260,0},{261,1},{262,2},{263,3},{0,4},{1,5},{2,6},{3,7},{12,256},{... | collective-permute-start | bytes 786440 | tf_op jit(solution)/shard_map/ppermute | solution.py:248
  82.4 12.4 %collective-permute-start.3 = (bf16[512,256]{1,0:T(8,128)(2,1)S(1)}, bf16[512,256]{1,0:T(8,128)(2,1)S(1)}, u32[]{:S(2)}, u32[]{:S(2)}) collective-permute-start(bf16[512,256]{1,0:T(8,128)(2,1)S(1)} %collective-permute-done.1), channel_id=1, source_target_pairs={{263,0},{0,1},{1,2},{2,3},{3,4},{4,5},{5,6},{6,7},{15,256},{264,25... | collective-permute-start | bytes 786440 | tf_op jit(solution)/shard_map/ppermute | solution.py:248
  87.3 10.6 %collective-permute-start.4 = (bf16[512,256]{1,0:T(8,128)(2,1)S(1)}, bf16[512,256]{1,0:T(8,128)(2,1)S(1)}, u32[]{:S(2)}, u32[]{:S(2)}) collective-permute-start(bf16[512,256]{1,0:T(8,128)(2,1)S(1)} %collective-permute-done.1), channel_id=1, source_target_pairs={{1,8},{2,9},{3,10},{4,11},{5,12},{6,13},{7,14},{256,15},{265,264},... | collective-permute-start | bytes 786440 | tf_op jit(solution)/shard_map/ppermute | solution.py:248
  98.1 28.8 %collective-permute-start.10 = (bf16[4,512,256]{2,1,0:T(8,128)(2,1)S(1)}, bf16[4,512,256]{2,1,0:T(8,128)(2,1)}, u32[]{:S(2)}, u32[]{:S(2)}) collective-permute-start(bf16[4,512,256]{2,1,0:T(8,128)(2,1)S(1)} %pad_maximum_fusion.taken_ref), channel_id=1, source_target_pairs={{0,8},{8,0},{1,9},{9,1},{2,10},{10,2},{3,11},{11,3},{4,12},{12,4},... | collective-permute-start | bytes 3145736 | tf_op jit(solution)/shard_map/ppermute | solution.py:262
  104.9 1.2 copy-start.1
  106.2 1.0 copy-start.3
  107.4 1.0 copy-start
  108.4 31.2 %all-to-all-start = ((bf16[32,2,64,128]{3,2,1,0:T(8,128)(2,1)}), bf16[32,2,64,128]{3,2,1,0:T(8,128)(2,1)}, u32[]{:S(2)}, u32[]{:S(2)}) async-start(bf16[32,2,64,128]{3,2,1,0:T(8,128)(2,1)} %copy-done), calls=%async_computation | async-start | bytes 2097152 | tf_op jit(solution)/shard_map/all_to_all | solution.py:271
  122.4 115.7 %all-gather.4.cloned.1.call-start = ((), (), s32[]{:S(2)}) async-start(), calls=%async_computation.5 | async-start | bytes 2228224 | tf_op jit(solution)/shard_map/all_gather | solution.py:288
  122.4 3.6 %collective-permute-start.2 = (bf16[512,256]{1,0:T(8,128)(2,1)S(1)}, bf16[512,256]{1,0:T(8,128)(2,1)}, u32[]{:S(2)}, u32[]{:S(2)}) collective-permute-start(bf16[512,256]{1,0:T(8,128)(2,1)S(1)} %collective-permute-done.1), channel_id=1, source_target_pairs={{0,8},{1,9},{2,10},{3,11},{4,12},{5,13},{6,14},{7,15},{264,256},{2... | collective-permute-start | bytes 786440 | tf_op jit(solution)/shard_map/ppermute | solution.py:250
  130.9 33.8 %copy-start.2 = (bf16[1,128,4096]{2,1,0:T(8,128)(2,1)S(1)}, bf16[1,128,4096]{2,1,0:T(8,128)(2,1)}, u32[]{:S(2)}) copy-start(bf16[1,128,4096]{2,1,0:T(8,128)(2,1)} %wide_ref.3) | copy-start | bytes 3145732
  130.9 33.9 %copy-start.4 = (bf16[1,128,2048]{2,1,0:T(8,128)(2,1)S(1)}, bf16[1,128,2048]{2,1,0:T(8,128)(2,1)}, u32[]{:S(2)}) copy-start(bf16[1,128,2048]{2,1,0:T(8,128)(2,1)} %half_ref.3) | copy-start | bytes 1572868
  146.5 3.6 %collective-permute-start.11 = (f32[256,256]{1,0:T(8,128)S(1)}, f32[256,256]{1,0:T(8,128)}, u32[]{:S(2)}, u32[]{:S(2)}) collective-permute-start(f32[256,256]{1,0:T(8,128)S(1)} %constant_dynamic-slice_fusion), channel_id=1, source_target_pairs={{0,8},{8,0},{1,9},{9,1},{2,10},{10,2},{3,11},{11,3},{4,12},{12,4},... | collective-permute-start | bytes 786440 | tf_op jit(solution)/shard_map/ppermute | solution.py:277
  151.0 13.0 %collective-permute-start.12 = (bf16[256,256]{1,0:T(8,128)(2,1)S(1)}, bf16[256,256]{1,0:T(8,128)(2,1)S(1)}, u32[]{:S(2)}, u32[]{:S(2)}) collective-permute-start(bf16[256,256]{1,0:T(8,128)(2,1)S(1)} %add_convert_fusion), channel_id=1, source_target_pairs={{0,0},{8,256},{16,8},{24,264},{32,16},{40,272},{48,24},{56,280},{6... | collective-permute-start | bytes 393224 | tf_op jit(solution)/shard_map/ppermute | solution.py:278
  164.1 0.7 copy-start.5
  195.9 4.6 %collective-permute-start = (bf16[32,2,64,128]{3,2,1,0:T(8,128)(2,1)S(1)}, bf16[32,2,64,128]{3,2,1,0:T(8,128)(2,1)S(1)}, u32[]{:S(2)}, u32[]{:S(2)}) collective-permute-start(bf16[32,2,64,128]{3,2,1,0:T(8,128)(2,1)S(1)} %all_to_all.26.near_ref), channel_id=1, source_target_pairs={{0,8},{8,0},{1,9},{9,1},{2,10},{10,2},{3,11},{11,3},{4,12},{12,4},... | collective-permute-start | bytes 3145736 | tf_op jit(solution)/shard_map/ppermute | solution.py:297
Sparse Core Ops, SparseCore 0:
  32.8 71.5 all-gather.5
  164.9 65.6 all-gather.3

commit v2 on v1

v2 whole, which is shorter than its diff:
```python
import math

import jax
import jax.numpy as jnp
from jax import lax
from jax.experimental import pallas as pl
from jax.experimental.pallas import tpu as pltpu
from jax.sharding import Mesh
from jax.sharding import PartitionSpec as P

HD = 128
SCALE = 1.0 / math.sqrt(HD)
LOG2E = math.log2(math.e)
PLANE = ("y", "x", "c")
RING = ("g", "d")
NT = (((1,), (1,)), ((), ()))
TN = (((0,), (0,)), ((), ()))
MIB = 1024 * 1024
SWAP = [(0, 1), (1, 0)]


def column_of(chip, chips, side):
    half = chips // 2
    return pl.multiple_of((2 * (chip % half) + lax.rem(chip // half + side, 2)) * HD, HD)


def prepare_kernel(
    spot_ref, wide_any, half_any, text_any, out_ref, blocks_ref, wide_ref, half_ref, text_ref, normed_ref, sems
):
    here = spot_ref[1]
    dests = out_ref.shape[0]
    width = half_any.shape[2]
    columns = pl.ds(pl.multiple_of(spot_ref[0] * width, width), width)
    copies = [
        pltpu.make_async_copy(text_any, text_ref, sems.at[0]),
        pltpu.make_async_copy(wide_any.at[:, :, columns], wide_ref, sems.at[1]),
        pltpu.make_async_copy(half_any, half_ref, sems.at[2]),
    ]
    for copy in copies:
        copy.start()
    copies[0].wait()
    n_dp, text_rows, depth = blocks_ref.shape
    rows = half_ref.shape[1] // 2
    wide = text_ref[0].astype(jnp.float32)
    square = jnp.mean(wide * wide, axis=-1, keepdims=True)
    normed_ref[...] = (wide * lax.rsqrt(square + 1e-06)).astype(jnp.bfloat16)
    for block in range(n_dp):
        blocks_ref[block] = normed_ref[:, block * depth : (block + 1) * depth]
    copies[1].wait()
    copies[2].wait()
    slots = n_dp // 2
    start = slots * depth // HD * text_rows
    for part in range(2):
        for slot in range(slots):
            away = (slot or slots) if part else -slot
            block = lax.rem(here + away + n_dp, n_dp)
            for lane in range(depth // HD):
                column = pl.multiple_of(block * depth + lane * HD, HD)
                piece = normed_ref[:, pl.ds(column, HD)]
                place = (slot * (depth // HD) + lane) * text_rows
                for head in range(dests // 2):
                    out_ref[2 * head + part, place : place + text_rows] = piece
        for head in range(dests // 2):
            columns = pl.ds(column_of(head, dests // 2, spot_ref[0]), HD)
            for slot, ref in enumerate((wide_ref, half_ref)):
                out_ref[2 * head + part, start + slot * rows : start + (slot + 1) * rows] = ref[
                    0, part * rows : (part + 1) * rows, columns
                ]


def prepare(spot, wide, half, text, n_dp):
    _, rows, width = half.shape
    _, text_rows, features = text.shape
    dests = 2 * width // HD
    pieces = features // 2 // HD * text_rows + rows
    depth = features // n_dp
    return pl.pallas_call(
        prepare_kernel,
        grid_spec=pltpu.PrefetchScalarGridSpec(
            num_scalar_prefetch=1,
            grid=(1,),
            in_specs=[pl.BlockSpec(memory_space=pltpu.HBM)] * 3,
            out_specs=[
                pl.BlockSpec((dests, pieces, HD), lambda j, spot_ref: (0, 0, 0)),
                pl.BlockSpec((n_dp, text_rows, depth), lambda j, spot_ref: (0, 0, 0)),
            ],
            scratch_shapes=[
                pltpu.VMEM(half.shape, half.dtype),
                pltpu.VMEM(half.shape, half.dtype),
                pltpu.VMEM(text.shape, text.dtype),
                pltpu.VMEM((text_rows, features), jnp.bfloat16),
                pltpu.SemaphoreType.DMA((3,)),
            ],
        ),
        out_shape=[
            jax.ShapeDtypeStruct((dests, pieces, HD), half.dtype),
            jax.ShapeDtypeStruct((n_dp, text_rows, depth), half.dtype),
        ],
        compiler_params=pltpu.CompilerParams(vmem_limit_bytes=16 * MIB),
        cost_estimate=pl.CostEstimate(
            flops=4 * text.size, bytes_accessed=2 * dests * pieces * HD + 4 * rows * width, transcendentals=0
        ),
        name="prepare",
    )(spot, wide, half, text)


def pack_kernel(spot_ref, wide_ref, half_ref, out_ref):
    rows = out_ref.shape[2]
    for dest in range(out_ref.shape[0]):
        head, part = dest // 2, dest % 2
        columns = pl.ds(column_of(head, out_ref.shape[0] // 2, spot_ref[0]), HD)
        for slot, ref in enumerate((wide_ref, half_ref)):
            out_ref[dest, slot] = ref[0, part * rows : (part + 1) * rows, columns]


def pack(spot, wide, half):
    _, rows, width = half.shape
    dests = 2 * width // HD
    return pl.pallas_call(
        pack_kernel,
        grid_spec=pltpu.PrefetchScalarGridSpec(
            num_scalar_prefetch=1,
            grid=(1,),
            in_specs=[
                pl.BlockSpec((1, rows, width), lambda j, spot_ref: (0, 0, spot_ref[0])),
                pl.BlockSpec((1, rows, width), lambda j, spot_ref: (0, 0, 0)),
            ],
            out_specs=pl.BlockSpec((dests, 2, rows // 2, HD), lambda j, spot_ref: (0, 0, 0, 0)),
        ),
        out_shape=jax.ShapeDtypeStruct((dests, 2, rows // 2, HD), half.dtype),
        compiler_params=pltpu.CompilerParams(vmem_limit_bytes=12 * MIB),
        cost_estimate=pl.CostEstimate(flops=0, bytes_accessed=4 * rows * width * 2, transcendentals=0),
        name="pack",
    )(spot, wide, half)


def unpack_kernel(spot_ref, in_ref, out_ref):
    rows = in_ref.shape[1]
    for source in range(in_ref.shape[0]):
        head, part = source // 2, source % 2
        columns = pl.ds(column_of(head, in_ref.shape[0] // 2, spot_ref[0]), HD)
        out_ref[0, part * rows : (part + 1) * rows, columns] = in_ref[source]


def unpack(spot, pieces):
    sources, rows, _ = pieces.shape
    width = sources // 2 * HD
    return pl.pallas_call(
        unpack_kernel,
        in_specs=[pl.BlockSpec(memory_space=pltpu.SMEM), pl.BlockSpec(memory_space=pltpu.VMEM)],
        out_shape=jax.ShapeDtypeStruct((1, 2 * rows, width), pieces.dtype),
        compiler_params=pltpu.CompilerParams(vmem_limit_bytes=8 * MIB),
        cost_estimate=pl.CostEstimate(flops=0, bytes_accessed=8 * rows * width, transcendentals=0),
        name="unpack",
    )(spot, pieces)


def project_kernel(spot_ref, text_ref, *refs):
    weight_refs, (out_ref, full_ref, half_ref, sems) = refs[:6], refs[6:]
    depth = full_ref.shape[1]
    groups = depth // HD
    sources = text_ref.shape[0]
    rows = out_ref.shape[0] // sources
    slots = [full_ref.at[k] for k in range(4)] + [half_ref.at[k] for k in range(2)]
    copies = [
        pltpu.make_async_copy(source, slot, sems.at[k])
        for k, (source, slot) in enumerate(zip(weight_refs, slots))
    ]
    for copy in copies:
        copy.start()
    for copy in copies:
        copy.wait()
    far = jnp.concatenate([half_ref[0], half_ref[1]], axis=1)
    weights = [jnp.where(spot_ref[2] == 0, full_ref[0], far), full_ref[1], full_ref[2], full_ref[3]]
    total = 0.0
    for slot, weight in enumerate(weights):
        block = jnp.concatenate(
            [
                text_ref[:, (slot * groups + k) * rows : (slot * groups + k + 1) * rows].reshape(sources * rows, HD)
                for k in range(groups)
            ],
            axis=1,
        )
        total += jnp.dot(block, weight, preferred_element_type=jnp.float32)
    out_ref[...] = total


def project(spot, received, text_rows, weights):
    sources = received.shape[0]
    depth, columns = weights[0].shape
    pieces = 4 * depth // HD * text_rows
    return pl.pallas_call(
        project_kernel,
        grid=(1,),
        in_specs=[
            pl.BlockSpec(memory_space=pltpu.SMEM),
            pl.BlockSpec((sources, pieces, HD), lambda j: (0, 0, 0)),
            *[pl.BlockSpec(memory_space=pltpu.HBM)] * 6,
        ],
        out_specs=pl.BlockSpec((sources * text_rows, columns), lambda j: (0, 0)),
        out_shape=jax.ShapeDtypeStruct((sources * text_rows, columns), jnp.float32),
        scratch_shapes=[
            pltpu.VMEM((4, depth, columns), jnp.bfloat16),
            pltpu.VMEM((2, depth, columns // 2), jnp.bfloat16),
            pltpu.SemaphoreType.DMA((6,)),
        ],
        compiler_params=pltpu.CompilerParams(vmem_limit_bytes=16 * MIB),
        cost_estimate=pl.CostEstimate(
            flops=8 * sources * text_rows * depth * columns, bytes_accessed=4 * MIB, transcendentals=0
        ),
        name="project",
    )(spot, received, *weights)


def cross_kernel(length_ref, spot_ref, q_ref, c_ref, near_ref, far_ref, out_ref, keep_ref, give_ref, total_ref):
    step = pl.program_id(0)
    block = out_ref.shape[0]
    tokens = near_ref.shape[0]
    q = q_ref[...].reshape(block, HD)
    cot = c_ref[...].reshape(block, HD)
    text_kv = (near_ref[...] + far_ref[...]).astype(jnp.bfloat16)
    text_keys = text_kv[:, :HD]
    text_vals = text_kv[:, HD:]
    live = lax.broadcasted_iota(jnp.int32, (tokens, 1), 0) < length_ref[0]
    scores = lax.dot_general(text_keys, q, NT, preferred_element_type=jnp.float32) * SCALE
    scores = jnp.where(live, scores, -jnp.inf)
    top = jnp.max(scores, axis=0, keepdims=True)
    expo = jnp.exp(scores - top)
    soft = expo / jnp.sum(expo, axis=0, keepdims=True)
    soft_low = soft.astype(jnp.bfloat16)
    out_t = lax.dot_general(text_vals, soft_low, TN, preferred_element_type=jnp.float32)
    out_ref[...] = out_t.T
    back = lax.dot_general(text_vals, cot, NT, preferred_element_type=jnp.float32)
    inner = jnp.sum(soft * back, axis=0, keepdims=True)
    grad_scores = (soft * (back - inner) * SCALE).astype(jnp.bfloat16)
    grad_keys = jnp.dot(grad_scores, q, preferred_element_type=jnp.float32)
    grad_vals = jnp.dot(soft_low, cot, preferred_element_type=jnp.float32)

    grads = jnp.concatenate([grad_keys, grad_vals], axis=1).reshape(total_ref.shape)

    @pl.when(step == 0)
    def _():
        total_ref[...] = grads

    @pl.when(step > 0)
    def _():
        total_ref[...] += grads

    @pl.when(step == pl.num_programs(0) - 1)
    def _():
        core = spot_ref[2]
        keep_ref[...] = total_ref[:, core].reshape(keep_ref.shape)
        give_ref[...] = total_ref[:, 1 - core].reshape(give_ref.shape)


def cross_attend(length, spot, received, rows, near, far, blocks=4):
    sources, pieces, _ = received.shape
    queries = sources * rows
    tokens, columns = near.shape
    last = pieces // rows
    text = pl.BlockSpec((tokens, columns), lambda j, n, s: (0, 0))
    half = pl.BlockSpec((tokens // 2, columns), lambda j, n, s: (0, 0))
    return pl.pallas_call(
        cross_kernel,
        grid_spec=pltpu.PrefetchScalarGridSpec(
            num_scalar_prefetch=2,
            grid=(blocks,),
            in_specs=[
                pl.BlockSpec((sources // blocks, rows, HD), lambda j, n, s: (j, last - 2, 0)),
                pl.BlockSpec((sources // blocks, rows, HD), lambda j, n, s: (j, last - 1, 0)),
                text,
                text,
            ],
            out_specs=[pl.BlockSpec((queries // blocks, HD), lambda j, n, s: (j, 0)), half, half],
            scratch_shapes=[pltpu.VMEM((sources // 2, 2, tokens // sources, columns), jnp.float32)],
        ),
        out_shape=[
            jax.ShapeDtypeStruct((queries, HD), jnp.float32),
            jax.ShapeDtypeStruct((tokens // 2, columns), jnp.float32),
            jax.ShapeDtypeStruct((tokens // 2, columns), jnp.float32),
        ],
        compiler_params=pltpu.CompilerParams(vmem_limit_bytes=24 * MIB),
        cost_estimate=pl.CostEstimate(
            flops=10 * queries * tokens * HD, bytes_accessed=4 * MIB, transcendentals=queries * tokens
        ),
        name="cross",
    )(length, spot, received, received, near, far)


def self_kernel(q_ref, near_ref, far_ref, cross_ref, out_ref):
    block = out_ref.shape[0]
    half = near_ref.shape[0] * near_ref.shape[2]
    q = q_ref[...].reshape(block, HD)
    scores = [
        lax.dot_general(q, ref[:, 0].reshape(half, HD), NT, preferred_element_type=jnp.float32)
        for ref in (near_ref, far_ref)
    ]
    top = jnp.maximum(*[jnp.max(s, axis=1, keepdims=True) for s in scores])
    total = 0.0
    out = 0.0
    for s, ref in zip(scores, (near_ref, far_ref)):
        expo = jnp.exp2((s - top) * (SCALE * LOG2E))
        total += jnp.sum(expo, axis=1, keepdims=True)
        out += jnp.dot(
            expo.astype(jnp.bfloat16), ref[:, 1].reshape(half, HD), preferred_element_type=jnp.float32
        )
    out_ref[...] = (out / total + cross_ref[...]).astype(out_ref.dtype)


def self_attend(received, near, far, cross_out, blocks=8):
    sources, _, rows, _ = near.shape
    queries = sources * rows
    last = received.shape[1] // rows
    whole = pl.BlockSpec(near.shape, lambda j: (0, 0, 0, 0))
    return pl.pallas_call(
        self_kernel,
        grid=(blocks,),
        in_specs=[
            pl.BlockSpec((sources // blocks, rows, HD), lambda j: (j, last - 2, 0)),
            whole,
            whole,
            pl.BlockSpec((queries // blocks, HD), lambda j: (j, 0)),
        ],
        out_specs=pl.BlockSpec((queries // blocks, HD), lambda j: (j, 0)),
        out_shape=jax.ShapeDtypeStruct((queries, HD), jnp.bfloat16),
        compiler_params=pltpu.CompilerParams(vmem_limit_bytes=36 * MIB),
        cost_estimate=pl.CostEstimate(
            flops=8 * queries * queries * HD, bytes_accessed=5 * MIB, transcendentals=2 * queries * queries
        ),
        name="self_attention",
    )(received, near, far, cross_out)


def finish_kernel(spot_ref, text_ref, kv_ref, keep_ref, give_ref):
    core, home = spot_ref[2], spot_ref[3]
    n_dp = text_ref.shape[1]
    tokens = kv_ref.shape[1]
    wanted = lax.rem(home + core, 2)
    keep, give = 0.0, 0.0
    for sample in range(n_dp):
        text = text_ref[:, sample].reshape(tokens, text_ref.shape[3])
        keep += lax.dot_general(text, kv_ref[wanted * n_dp + sample], TN, preferred_element_type=jnp.float32)
        give += lax.dot_general(text, kv_ref[(1 - wanted) * n_dp + sample], TN, preferred_element_type=jnp.float32)
    keep_ref[...] = keep
    give_ref[...] = give


def finish(spot, text, kv_all):
    depth = text.shape[3]
    columns = kv_all.shape[2]
    vmem = pl.BlockSpec(memory_space=pltpu.VMEM)
    return pl.pallas_call(
        finish_kernel,
        in_specs=[pl.BlockSpec(memory_space=pltpu.SMEM), vmem, vmem],
        out_specs=[vmem, vmem],
        out_shape=[jax.ShapeDtypeStruct((depth, columns), jnp.float32)] * 2,
        compiler_params=pltpu.CompilerParams(vmem_limit_bytes=20 * MIB),
        cost_estimate=pl.CostEstimate(flops=4 * text.size * columns, bytes_accessed=6 * MIB, transcendentals=0),
        name="finish",
    )(spot, text, kv_all)


def local(queries, keys, values, cotangent, captions, caption_len, proj_weight):
    side, turn, core = lax.axis_index("g"), lax.axis_index("d"), lax.axis_index("c")
    sides, n_dp = lax.axis_size("g"), lax.axis_size("d")
    n_ring = sides * n_dp
    n_chips = lax.axis_size("y") * lax.axis_size("x")
    home_side = lax.axis_index("y") // (lax.axis_size("y") // 2)
    spot = jnp.stack([side, turn, core, home_side]).astype(jnp.int32)
    text_rows, features = captions.shape[1:]

    def across(chip):
        return (chip + n_chips // 2) % n_chips

    passed = lax.ppermute(
        proj_weight,
        PLANE,
        [(2 * j, 2 * j + 1) for j in range(n_chips)] + [(2 * j + 1, 2 * across(j)) for j in range(n_chips)],
    )
    second = lax.ppermute(proj_weight, PLANE, [(2 * j + 1, 2 * across(j) + 1) for j in range(n_chips)])
    sent, blocks = prepare(spot, queries, cotangent, captions, n_dp)

    sent, passed, second = lax.optimization_barrier((sent, passed, second))
    received = lax.all_to_all(sent, PLANE, 0, 0, tiled=True)
    at_home = jnp.where(core == 0, proj_weight, passed)
    away = jnp.where(core == 0, passed, second)
    head_of_side = (jnp.where(home_side == 0, at_home, away), jnp.where(home_side == 0, away, at_home))

    def place(z, c):
        g, d = divmod(z % n_ring, n_dp)
        return (g * sides + c) * n_dp + d

    def block_for(distance):
        to_side = (side * n_dp + turn + distance + n_ring) % n_ring // n_dp
        return jnp.where(to_side == 0, head_of_side[0], head_of_side[1])

    def send(block, up, down):
        pairs = [(place(z, 0), place(z + up, 0)) for z in range(n_ring) if up]
        pairs += [(place(z, 1), place(z + down, 1)) for z in range(n_ring)]
        return lax.ppermute(block, ("g", "c", "d"), pairs)

    reach = n_dp // 2
    weights = [jnp.where(side == 0, head_of_side[0], head_of_side[1])]
    weights += [send(block_for((1 - 2 * core) * t), t, -t) for t in range(1, reach)]
    weights.append(send(block_for(-reach)[:, :HD], 0, -reach))
    weights.append(send(block_for(reach)[:, HD:], 0, reach))

    received, keys, values = lax.optimization_barrier((received, keys, values))
    near = lax.all_to_all(pack(spot, keys, values), PLANE, 0, 0, tiled=True)

    text_near = project(spot, received, text_rows, weights)
    text_far = lax.ppermute(text_near, "c", SWAP)
    rows = queries.shape[1] // 2
    cross_out, keep, give = cross_attend(caption_len, spot, received, rows, text_near, text_far)

    kv_half = (keep + lax.ppermute(give, "c", SWAP)).astype(jnp.bfloat16)
    kv_half, near, blocks = lax.optimization_barrier((kv_half, near, blocks))

    kv_all = lax.all_gather(kv_half, RING, axis=0, tiled=False)

    by_sample = lax.all_to_all(blocks, "d", 0, 0, tiled=True)
    spread = lax.all_to_all(
        jnp.broadcast_to(by_sample[None], (n_chips,) + by_sample.shape), ("y", "x"), 0, 0, tiled=True
    )

    far = lax.ppermute(near, "c", SWAP)
    out_rows = self_attend(received, near, far, cross_out)
    back = lax.all_to_all(out_rows.reshape(near.shape[0], rows, HD), PLANE, 0, 0, tiled=True)
    attended = unpack(spot, back)

    spread, back = lax.optimization_barrier((spread, back))
    keep, give = finish(spot, spread, kv_all)
    total = keep + lax.ppermute(give, "c", SWAP)
    moved = lax.ppermute(total, PLANE, [(2 * j + 1, 2 * across(j) + 1) for j in range(n_chips)])
    proj_grad = jnp.where(core == 0, total, moved)
    return attended, proj_grad


def solution(mesh):
    inner = Mesh(mesh.devices.reshape(2, 4, 4, 2, 8), ("g", "y", "x", "c", "d"))
    return jax.shard_map(
        local,
        mesh=inner,
        in_specs=(
            P("d", PLANE, None),
            P("d", PLANE, None),
            P("d", PLANE, "g"),
            P("d", PLANE, "g"),
            P("d", PLANE, None),
            P("d"),
            P("d", PLANE),
        ),
        out_specs=(P("d", PLANE, "g"), P("d", PLANE)),
        check_vma=False,
    )
```

time: 251 us -> 211 us (0.84)
  waiting for transfers between devices: 47.7 us -> 22.8 us
  blocking collectives: 71.3 us -> 46.9 us
  Pallas kernels: 26.9 us -> 34.8 us
  starting transfers between devices: 68.2 us -> 74.2 us
  matrix products: 4.94 us -> 0 us
    ppermute x11 -> x10, waiting for transfers between devices: 35.5 us -> 9.01 us  [the longest x1 7.47 us: local(): lax.ppermute(total, PLANE, [(2 * j + 1, 2 * across(j) + 1) for j in range...]
    all_to_all x3 -> x2, blocking collectives: 69.3 us -> 46.9 us  [the longest x1 30.7 us: local(): lax.all_to_all(jnp.broadcast_to(by_sample[None], (n_chips,) + by_sample.s...]
    ppermute x11 -> x10, starting transfers between devices: 42.7 us -> 49.1 us  [the longest x5 26.1 us: send(): return lax.ppermute(block, ('g', 'c', 'd'), pairs)]
    pallas_call x2 -> x4, Pallas kernels: 2.9 us -> 8.79 us  [the longest x1 3.3 us: project(): pl.pallas_call(project_kernel, grid=(1,), in_specs=[pl.BlockSpec(memory_s...]
    unnamed x15 -> x26, local copies, waits for them, and re-layouts: 4.84 us -> 10.4 us
    dot_general x1 -> x0, matrix products: 4.94 us -> none  [local(): lax.dot_general(spread, kv_all, TN, preferred_element_type=jnp.float32)]
    transpose x2 -> x0, local copies, waits for them, and re-layouts: 4.89 us -> none  [the longest x1 4.84 us: local(): spread.reshape(2, n_chips, n_dp, rows, features // n_dp)]
    all_to_all x2 -> x3, waiting for transfers between devices: 8.65 us -> 12.5 us  [the longest x1 8.88 us: local(): received = lax.all_to_all(sent, PLANE, 0, 0, tiled=True)]
  transfers between devices with their start and end apart: 17 -> 16, of which waited for: 8 -> 5; matrix products, arithmetic and copies ran while one was open for 4% -> 2% of each run, Pallas kernels for 11% -> 14%
where the time goes in v2:
time: 211 us; the launch traced here: 210 us
  starting transfers between devices  74.2 us (35%)
  blocking collectives  46.9 us (22%)
  Pallas kernels  34.8 us (16%)
  waiting for transfers between devices  22.8 us (11%)
  between operations  15.2 us (7%)
  local copies, waits for them, and re-layouts  10.6 us (5%)
  other arithmetic  5.1 us (2%)
    all_to_all x1, blocking collectives, local(): lax.all_to_all(jnp.broadcast_to(by_sample[None], (n_chips,) + by_sample.s...  30.7 us
    ppermute x5, starting transfers between devices, send(): return lax.ppermute(block, ('g', 'c', 'd'), pairs)  26.1 us
    pallas_call x1, Pallas kernels, self_attend(): pl.pallas_call(self_kernel, grid=(blocks,), in_specs=[pl.BlockSpec((sourc...  17.4 us
    all_to_all x1, blocking collectives, local(): lax.all_to_all(out_rows.reshape(near.shape[0], rows, HD), PLANE, 0, 0, ti...  16.2 us
    all_to_all x1, starting transfers between devices, local(): by_sample = lax.all_to_all(blocks, 'd', 0, 0, tiled=True)  11.5 us
    unnamed x26, local copies, waits for them, and re-layouts  10.4 us
    all_to_all x1, waiting for transfers between devices, local(): received = lax.all_to_all(sent, PLANE, 0, 0, tiled=True)  8.88 us
    pallas_call x1, Pallas kernels, cross_attend(): pl.pallas_call(cross_kernel, grid_spec=pltpu.PrefetchScalarGridSpec(num_s...  7.77 us
  transfers between devices with their start and end apart: 16, of which 5 were waited for; matrix products, arithmetic and copies ran while one was open for 2% of the time, Pallas kernels for 14%

profile of v2, /device:TPU:1, one launch (start us, length us, event | category | flops | bytes accessed | tf_op | source)
XLA Modules:
  0.0 209.6 jit_solution(8670417664051248775)
XLA Ops:
  7.2 6.2 %collective-permute-start = (bf16[512,256]{1,0:T(8,128)(2,1)}, bf16[512,256]{1,0:T(8,128)(2,1)}, u32[]{:S(2)}, u32[]{:S(2)}) collective-permute-start(bf16[512,256]{1,0:T(8,128)(2,1)} %param.13), channel_id=1, source_target_pairs={{0,8},{16,24},{32,40},{48,56},{64,72},{80,88},{96,104},{112,120},{... | collective-permute-start | bytes 786440 | tf_op jit(solution)/shard_map/ppermute | solution.py:375
  13.4 7.3 %collective-permute-start.1 = (bf16[512,256]{1,0:T(8,128)(2,1)}, bf16[512,256]{1,0:T(8,128)(2,1)}, u32[]{:S(2)}, u32[]{:S(2)}) collective-permute-start(bf16[512,256]{1,0:T(8,128)(2,1)} %param.13), channel_id=1, source_target_pairs={{8,136},{24,152},{40,168},{56,184},{72,200},{88,216},{104,232},{12... | collective-permute-start | bytes 786440 | tf_op jit(solution)/shard_map/ppermute | solution.py:380
  24.0 2.2 %prepare.1 = (bf16[32,384,128]{2,1,0:T(8,128)(2,1)S(1)}, bf16[8,16,512]{2,1,0:T(8,128)(2,1)}) custom-call(s32[4]{0:T(128)S(1)} %pad_add_fusion.spot_ref, bf16[1,128,4096]{2,1,0:T(8,128)(2,1)S(1)} %copy-done.4, bf16[1,128,2048]{2,1,0:T(8,128)(2,1)S(1)} %copy-done.6, bf16[1,16,4096]{2,1,0:T(8,128)(2,1)S(1)} %copy-done.9), custom_call_target="tpu_custom_call" | custom-call | flops 262144 | bytes 4194304 | tf_op jit(solution)/shard_map/prepare/pallas_call | solution.py:77
  27.9 4.0 %all-to-all-start = ((bf16[32,384,128]{2,1,0:T(8,128)(2,1)}), bf16[32,384,128]{2,1,0:T(8,128)(2,1)S(1)}, u32[]{:S(2)}, u32[]{:S(2)}) async-start(bf16[32,384,128]{2,1,0:T(8,128)(2,1)} %copy-done.1), calls=%async_computation | async-start | bytes 6291456 | tf_op jit(solution)/shard_map/all_to_all | solution.py:384
  34.7 9.1 %collective-permute-start.2 = (bf16[512,256]{1,0:T(8,128)(2,1)}, bf16[512,256]{1,0:T(8,128)(2,1)}, u32[]{:S(2)}, u32[]{:S(2)}) collective-permute-start(bf16[512,256]{1,0:T(8,128)(2,1)} %get-tuple-element.42), channel_id=1, source_target_pairs={{0,1},{1,2},{2,3},{3,4},{4,5},{5,6},{6,7},{7,256},{256,257},{257,2... | collective-permute-start | bytes 786440 | tf_op jit(solution)/shard_map/ppermute | solution.py:400
  43.8 3.1 %collective-permute-start.3 = (bf16[512,256]{1,0:T(8,128)(2,1)}, bf16[512,256]{1,0:T(8,128)(2,1)}, u32[]{:S(2)}, u32[]{:S(2)}) collective-permute-start(bf16[512,256]{1,0:T(8,128)(2,1)} %get-tuple-element.41), channel_id=1, source_target_pairs={{0,2},{1,3},{2,4},{3,5},{4,6},{5,7},{6,256},{7,257},{256,258},{257... | collective-permute-start | bytes 786440 | tf_op jit(solution)/shard_map/ppermute | solution.py:400
  46.9 4.7 %collective-permute-start.4 = (bf16[512,256]{1,0:T(8,128)(2,1)}, bf16[512,256]{1,0:T(8,128)(2,1)}, u32[]{:S(2)}, u32[]{:S(2)}) collective-permute-start(bf16[512,256]{1,0:T(8,128)(2,1)} %get-tuple-element.36), channel_id=1, source_target_pairs={{0,3},{1,4},{2,5},{3,6},{4,7},{5,256},{6,257},{7,258},{256,259},{2... | collective-permute-start | bytes 786440 | tf_op jit(solution)/shard_map/ppermute | solution.py:400
  52.4 2.8 %collective-permute-start.5 = (bf16[512,128]{1,0:T(8,128)(2,1)}, bf16[512,128]{1,0:T(8,128)(2,1)S(1)}, u32[]{:S(2)}, u32[]{:S(2)}) collective-permute-start(bf16[512,128]{1,0:T(8,128)(2,1)} %get-tuple-element.40), channel_id=1, source_target_pairs={{8,268},{9,269},{10,270},{11,271},{12,8},{13,9},{14,10},{15,11},{2... | collective-permute-start | bytes 393224 | tf_op jit(solution)/shard_map/ppermute | solution.py:400
  55.2 6.4 %collective-permute-start.6 = (bf16[512,128]{1,0:T(8,128)(2,1)}, bf16[512,128]{1,0:T(8,128)(2,1)}, u32[]{:S(2)}, u32[]{:S(2)}) collective-permute-start(bf16[512,128]{1,0:T(8,128)(2,1)} %get-tuple-element.39), channel_id=1, source_target_pairs={{8,12},{9,13},{10,14},{11,15},{12,264},{13,265},{14,266},{15,267},... | collective-permute-start | bytes 393224 | tf_op jit(solution)/shard_map/ppermute | solution.py:400
  61.6 8.9 %all-to-all-done.text_ref.q_ref.c_ref = bf16[32,384,128]{2,1,0:T(8,128)(2,1)S(1)} async-done(((bf16[32,384,128]{2,1,0:T(8,128)(2,1)}), bf16[32,384,128]{2,1,0:T(8,128)(2,1)S(1)}, u32[]{:S(2)}, u32[]{:S(2)}) %all-to-all-start) | async-done | bytes 3145760 | tf_op jit(solution)/shard_map/all_to_all | solution.py:384
  70.5 3.3 %project.1.near_ref = f32[512,256]{1,0:T(8,128)} custom-call(s32[4]{0:T(128)S(1)} %pad_add_fusion.spot_ref, bf16[32,384,128]{2,1,0:T(8,128)(2,1)S(1)} %all-to-all-done.text_ref.q_ref.c_ref, bf16[512,256]{1,0:T(8,128)(2,1)S(1)} %get-tuple-element.43.refs_0_, bf16[512,256]{1,0:T(8,128)(2,1)} %collective-permute-done.2.refs_1_, ...), custom_call_target="tpu_custom_call" | custom-call | flops 536870912 | bytes 4194304 | tf_op jit(solution)/shard_map/project/pallas_call | solution.py:192
  73.8 3.4 %collective-permute-start.7 = (f32[512,256]{1,0:T(8,128)}, f32[512,256]{1,0:T(8,128)}, u32[]{:S(2)}, u32[]{:S(2)}) collective-permute-start(f32[512,256]{1,0:T(8,128)} %project.1.near_ref), channel_id=1, source_target_pairs={{0,8},{8,0},{1,9},{9,1},{2,10},{10,2},{3,11},{11,3},{4,12},{12,4},... | collective-permute-start | bytes 1572872 | tf_op jit(solution)/shard_map/ppermute | solution.py:412
  79.1 5.1 %all-to-all-start.1 = ((bf16[32,2,64,128]{3,2,1,0:T(8,128)(2,1)}), bf16[32,2,64,128]{3,2,1,0:T(8,128)(2,1)}, u32[]{:S(2)}, u32[]{:S(2)}) async-start(bf16[32,2,64,128]{3,2,1,0:T(8,128)(2,1)} %copy-done), calls=%async_computation.1 | async-start | bytes 2097152 | tf_op jit(solution)/shard_map/all_to_all | solution.py:409
  84.9 7.8 %cross.1 = (f32[2048,128]{1,0:T(8,128)S(1)}, f32[256,256]{1,0:T(8,128)S(1)}, f32[256,256]{1,0:T(8,128)S(1)}) custom-call(s32[1]{0:T(128)S(6)} %copy.9.length_ref, s32[4]{0:T(128)S(1)} %pad_add_fusion.spot_ref, bf16[32,384,128]{2,1,0:T(8,128)(2,1)S(1)} %all-to-all-done.text_ref.q_ref.c_ref, bf16[32,384,128]{2,1,0:T(8,128)(2,1)S(1)} %all-to-all-done.text_ref.q_ref.c_ref, ...), custom_call_target="tpu_custom_call" | custom-call | flops 1342177280 | bytes 4194304 | tf_op jit(solution)/shard_map/cross/pallas_call | solution.py:263
  93.7 2.2 %collective-permute-start.8 = (f32[256,256]{1,0:T(8,128)S(1)}, f32[256,256]{1,0:T(8,128)S(1)}, u32[]{:S(2)}, u32[]{:S(2)}) collective-permute-start(f32[256,256]{1,0:T(8,128)S(1)} %get-tuple-element.25), channel_id=1, source_target_pairs={{0,8},{8,0},{1,9},{9,1},{2,10},{10,2},{3,11},{11,3},{4,12},{12,4},... | collective-permute-start | bytes 786440 | tf_op jit(solution)/shard_map/ppermute | solution.py:416
  97.8 3.6 %all-to-all-done.1.near_ref = bf16[32,2,64,128]{3,2,1,0:T(8,128)(2,1)} async-done(((bf16[32,2,64,128]{3,2,1,0:T(8,128)(2,1)}), bf16[32,2,64,128]{3,2,1,0:T(8,128)(2,1)}, u32[]{:S(2)}, u32[]{:S(2)}) %all-to-all-start.1) | async-done | bytes 1048608 | tf_op jit(solution)/shard_map/all_to_all | solution.py:409
  101.4 2.3 %collective-permute-start.9 = (bf16[32,2,64,128]{3,2,1,0:T(8,128)(2,1)}, bf16[32,2,64,128]{3,2,1,0:T(8,128)(2,1)}, u32[]{:S(2)}, u32[]{:S(2)}) collective-permute-start(bf16[32,2,64,128]{3,2,1,0:T(8,128)(2,1)} %all-to-all-done.1.near_ref), channel_id=1, source_target_pairs={{0,8},{8,0},{1,9},{9,1},{2,10},{10,2},{3,11},{11,3},{4,12},{12,4},... | collective-permute-start | bytes 3145736 | tf_op jit(solution)/shard_map/ppermute | solution.py:426
  103.7 11.5 %all-to-all-start.3 = ((bf16[8,16,512]{2,1,0:T(8,128)(2,1)}), bf16[8,16,512]{2,1,0:T(8,128)(2,1)S(1)}, u32[]{:S(2)}, u32[]{:S(2)}) async-start(bf16[8,16,512]{2,1,0:T(8,128)(2,1)} %get-tuple-element.31), calls=%async_computation.3 | async-start | bytes 262144 | tf_op jit(solution)/shard_map/all_to_all | solution.py:421
  116.4 17.4 %self_attention.1 = bf16[2048,128]{1,0:T(8,128)(2,1)S(1)} custom-call(bf16[32,384,128]{2,1,0:T(8,128)(2,1)S(1)} %all-to-all-done.text_ref.q_ref.c_ref, bf16[32,2,64,128]{3,2,1,0:T(8,128)(2,1)} %all-to-all-done.1.near_ref, bf16[32,2,64,128]{3,2,1,0:T(8,128)(2,1)} %collective-permute-done.9.far_ref, f32[2048,128]{1,0:T(8,128)S(1)} %copy-done.11), custom_call_target="tpu_custom_call" | custom-call | flops 4294967296 | bytes 5242880 | tf_op jit(solution)/shard_map/self_attention/pallas_call | solution.py:315
  134.7 16.2 %all_to_all.25.in_ref = bf16[32,64,128]{2,1,0:T(8,128)(2,1)} all-to-all(bf16[32,64,128]{2,1,0:T(8,128)(2,1)} %bitcast.7), channel_id=1, replica_groups=mesh['g'=2,'y'=4,'x'=4,'c'=2,'d'=8] {'y','x','c'}, dimensions={0} | all-to-all | bytes 1048576 | tf_op jit(solution)/shard_map/all_to_all | solution.py:428
  151.2 30.7 %all_to_all.26.text_ref = bf16[16,8,16,512]{3,2,1,0:T(8,128)(2,1)S(1)} all-to-all(bf16[16,8,16,512]{3,2,1,0:T(8,128)(2,1)S(1)} %broadcast_in_dim.2), channel_id=1, replica_groups=mesh['g'=2,'y'=4,'x'=4,'c'=2,'d'=8] {'y','x'}, dimensions={0} | all-to-all | bytes 4194304 | tf_op jit(solution)/shard_map/all_to_all | solution.py:422
  185.3 3.6 %collective-permute-start.10 = (f32[512,256]{1,0:T(8,128)S(1)}, f32[512,256]{1,0:T(8,128)S(1)}, u32[]{:S(2)}, u32[]{:S(2)}) collective-permute-start(f32[512,256]{1,0:T(8,128)S(1)} %get-tuple-element.35), channel_id=1, source_target_pairs={{0,8},{8,0},{1,9},{9,1},{2,10},{10,2},{3,11},{11,3},{4,12},{12,4},... | collective-permute-start | bytes 1572872 | tf_op jit(solution)/shard_map/ppermute | solution.py:433
  190.5 2.5 %collective-permute-start.11 = (f32[512,256]{1,0:T(8,128)S(1)}, f32[512,256]{1,0:T(8,128)S(1)}, u32[]{:S(2)}, u32[]{:S(2)}) collective-permute-start(f32[512,256]{1,0:T(8,128)S(1)} %add.80), channel_id=1, source_target_pairs={{8,136},{24,152},{40,168},{56,184},{72,200},{88,216},{104,232},{12... | collective-permute-start | bytes 1572872 | tf_op jit(solution)/shard_map/ppermute | solution.py:434
  194.4 7.5 %collective-permute-done.11 = f32[512,256]{1,0:T(8,128)S(1)} collective-permute-done((f32[512,256]{1,0:T(8,128)S(1)}, f32[512,256]{1,0:T(8,128)S(1)}, u32[]{:S(2)}, u32[]{:S(2)}) %collective-permute-start.11) | collective-permute-done | bytes 524320 | tf_op jit(solution)/shard_map/ppermute | solution.py:434
  (52 shorter events, 22.6 us)
Async XLA Ops:
  7.2 20.7 %collective-permute-start = (bf16[512,256]{1,0:T(8,128)(2,1)}, bf16[512,256]{1,0:T(8,128)(2,1)}, u32[]{:S(2)}, u32[]{:S(2)}) collective-permute-start(bf16[512,256]{1,0:T(8,128)(2,1)} %param.13), channel_id=1, source_target_pairs={{0,8},{16,24},{32,40},{48,56},{64,72},{80,88},{96,104},{112,120},{... | collective-permute-start | bytes 786440 | tf_op jit(solution)/shard_map/ppermute | solution.py:375
  13.4 14.5 %collective-permute-start.1 = (bf16[512,256]{1,0:T(8,128)(2,1)}, bf16[512,256]{1,0:T(8,128)(2,1)}, u32[]{:S(2)}, u32[]{:S(2)}) collective-permute-start(bf16[512,256]{1,0:T(8,128)(2,1)} %param.13), channel_id=1, source_target_pairs={{8,136},{24,152},{40,168},{56,184},{72,200},{88,216},{104,232},{12... | collective-permute-start | bytes 786440 | tf_op jit(solution)/shard_map/ppermute | solution.py:380
  20.8 1.2 copy-start.4
  26.2 1.6 copy-start.1
  27.9 4.2 %copy-start.12 = (bf16[512,256]{1,0:T(8,128)(2,1)S(1)}, bf16[512,256]{1,0:T(8,128)(2,1)}, u32[]{:S(2)}) copy-start(bf16[512,256]{1,0:T(8,128)(2,1)} %param.13) | copy-start | bytes 786436
  27.9 42.6 %all-to-all-start = ((bf16[32,384,128]{2,1,0:T(8,128)(2,1)}), bf16[32,384,128]{2,1,0:T(8,128)(2,1)S(1)}, u32[]{:S(2)}, u32[]{:S(2)}) async-start(bf16[32,384,128]{2,1,0:T(8,128)(2,1)} %copy-done.1), calls=%async_computation | async-start | bytes 6291456 | tf_op jit(solution)/shard_map/all_to_all | solution.py:384
  34.7 35.8 %collective-permute-start.2 = (bf16[512,256]{1,0:T(8,128)(2,1)}, bf16[512,256]{1,0:T(8,128)(2,1)}, u32[]{:S(2)}, u32[]{:S(2)}) collective-permute-start(bf16[512,256]{1,0:T(8,128)(2,1)} %get-tuple-element.42), channel_id=1, source_target_pairs={{0,1},{1,2},{2,3},{3,4},{4,5},{5,6},{6,7},{7,256},{256,257},{257,2... | collective-permute-start | bytes 786440 | tf_op jit(solution)/shard_map/ppermute | solution.py:400
  43.8 26.7 %collective-permute-start.3 = (bf16[512,256]{1,0:T(8,128)(2,1)}, bf16[512,256]{1,0:T(8,128)(2,1)}, u32[]{:S(2)}, u32[]{:S(2)}) collective-permute-start(bf16[512,256]{1,0:T(8,128)(2,1)} %get-tuple-element.41), channel_id=1, source_target_pairs={{0,2},{1,3},{2,4},{3,5},{4,6},{5,7},{6,256},{7,257},{256,258},{257... | collective-permute-start | bytes 786440 | tf_op jit(solution)/shard_map/ppermute | solution.py:400
  46.9 23.6 %collective-permute-start.4 = (bf16[512,256]{1,0:T(8,128)(2,1)}, bf16[512,256]{1,0:T(8,128)(2,1)}, u32[]{:S(2)}, u32[]{:S(2)}) collective-permute-start(bf16[512,256]{1,0:T(8,128)(2,1)} %get-tuple-element.36), channel_id=1, source_target_pairs={{0,3},{1,4},{2,5},{3,6},{4,7},{5,256},{6,257},{7,258},{256,259},{2... | collective-permute-start | bytes 786440 | tf_op jit(solution)/shard_map/ppermute | solution.py:400
  52.4 18.1 %collective-permute-start.5 = (bf16[512,128]{1,0:T(8,128)(2,1)}, bf16[512,128]{1,0:T(8,128)(2,1)S(1)}, u32[]{:S(2)}, u32[]{:S(2)}) collective-permute-start(bf16[512,128]{1,0:T(8,128)(2,1)} %get-tuple-element.40), channel_id=1, source_target_pairs={{8,268},{9,269},{10,270},{11,271},{12,8},{13,9},{14,10},{15,11},{2... | collective-permute-start | bytes 393224 | tf_op jit(solution)/shard_map/ppermute | solution.py:400
  55.2 15.3 %collective-permute-start.6 = (bf16[512,128]{1,0:T(8,128)(2,1)}, bf16[512,128]{1,0:T(8,128)(2,1)}, u32[]{:S(2)}, u32[]{:S(2)}) collective-permute-start(bf16[512,128]{1,0:T(8,128)(2,1)} %get-tuple-element.39), channel_id=1, source_target_pairs={{8,12},{9,13},{10,14},{11,15},{12,264},{13,265},{14,266},{15,267},... | collective-permute-start | bytes 393224 | tf_op jit(solution)/shard_map/ppermute | solution.py:400
  70.5 6.7 %copy-start.5 = (bf16[1,128,4096]{2,1,0:T(8,128)(2,1)S(1)}, bf16[1,128,4096]{2,1,0:T(8,128)(2,1)}, u32[]{:S(2)}) copy-start(bf16[1,128,4096]{2,1,0:T(8,128)(2,1)} %wide_ref) | copy-start | bytes 3145732
  70.5 6.7 %copy-start.8 = (bf16[1,128,2048]{2,1,0:T(8,128)(2,1)S(1)}, bf16[1,128,2048]{2,1,0:T(8,128)(2,1)}, u32[]{:S(2)}) copy-start(bf16[1,128,2048]{2,1,0:T(8,128)(2,1)} %half_ref) | copy-start | bytes 1572868
  73.8 11.0 %collective-permute-start.7 = (f32[512,256]{1,0:T(8,128)}, f32[512,256]{1,0:T(8,128)}, u32[]{:S(2)}, u32[]{:S(2)}) collective-permute-start(f32[512,256]{1,0:T(8,128)} %project.1.near_ref), channel_id=1, source_target_pairs={{0,8},{8,0},{1,9},{9,1},{2,10},{10,2},{3,11},{11,3},{4,12},{12,4},... | collective-permute-start | bytes 1572872 | tf_op jit(solution)/shard_map/ppermute | solution.py:412
  79.1 22.3 %all-to-all-start.1 = ((bf16[32,2,64,128]{3,2,1,0:T(8,128)(2,1)}), bf16[32,2,64,128]{3,2,1,0:T(8,128)(2,1)}, u32[]{:S(2)}, u32[]{:S(2)}) async-start(bf16[32,2,64,128]{3,2,1,0:T(8,128)(2,1)} %copy-done), calls=%async_computation.1 | async-start | bytes 2097152 | tf_op jit(solution)/shard_map/all_to_all | solution.py:409
  84.2 97.7 %all-gather.3.cloned.1.call-start = ((), (), s32[]{:S(2)}) async-start(), calls=%async_computation.5 | async-start | bytes 2228224 | tf_op jit(solution)/shard_map/all_gather | solution.py:419
  93.7 3.4 %collective-permute-start.8 = (f32[256,256]{1,0:T(8,128)S(1)}, f32[256,256]{1,0:T(8,128)S(1)}, u32[]{:S(2)}, u32[]{:S(2)}) collective-permute-start(f32[256,256]{1,0:T(8,128)S(1)} %get-tuple-element.25), channel_id=1, source_target_pairs={{0,8},{8,0},{1,9},{9,1},{2,10},{10,2},{3,11},{11,3},{4,12},{12,4},... | collective-permute-start | bytes 786440 | tf_op jit(solution)/shard_map/ppermute | solution.py:416
  101.4 13.8 %collective-permute-start.9 = (bf16[32,2,64,128]{3,2,1,0:T(8,128)(2,1)}, bf16[32,2,64,128]{3,2,1,0:T(8,128)(2,1)}, u32[]{:S(2)}, u32[]{:S(2)}) collective-permute-start(bf16[32,2,64,128]{3,2,1,0:T(8,128)(2,1)} %all-to-all-done.1.near_ref), channel_id=1, source_target_pairs={{0,8},{8,0},{1,9},{9,1},{2,10},{10,2},{3,11},{11,3},{4,12},{12,4},... | collective-permute-start | bytes 3145736 | tf_op jit(solution)/shard_map/ppermute | solution.py:426
  103.7 30.9 %all-to-all-start.3 = ((bf16[8,16,512]{2,1,0:T(8,128)(2,1)}), bf16[8,16,512]{2,1,0:T(8,128)(2,1)S(1)}, u32[]{:S(2)}, u32[]{:S(2)}) async-start(bf16[8,16,512]{2,1,0:T(8,128)(2,1)} %get-tuple-element.31), calls=%async_computation.3 | async-start | bytes 262144 | tf_op jit(solution)/shard_map/all_to_all | solution.py:421
  115.2 1.2 copy-start.11
  181.8 1.6 copy-start.2
  183.4 9.5 %copy-start.3 = (bf16[32,64,128]{2,1,0:T(8,128)(2,1)S(1)}, bf16[32,64,128]{2,1,0:T(8,128)(2,1)}, u32[]{:S(2)}) copy-start(bf16[32,64,128]{2,1,0:T(8,128)(2,1)} %all_to_all.25.in_ref) | copy-start | bytes 1572868
  185.3 5.1 %collective-permute-start.10 = (f32[512,256]{1,0:T(8,128)S(1)}, f32[512,256]{1,0:T(8,128)S(1)}, u32[]{:S(2)}, u32[]{:S(2)}) collective-permute-start(f32[512,256]{1,0:T(8,128)S(1)} %get-tuple-element.35), channel_id=1, source_target_pairs={{0,8},{8,0},{1,9},{9,1},{2,10},{10,2},{3,11},{11,3},{4,12},{12,4},... | collective-permute-start | bytes 1572872 | tf_op jit(solution)/shard_map/ppermute | solution.py:433
  190.5 11.4 %collective-permute-start.11 = (f32[512,256]{1,0:T(8,128)S(1)}, f32[512,256]{1,0:T(8,128)S(1)}, u32[]{:S(2)}, u32[]{:S(2)}) collective-permute-start(f32[512,256]{1,0:T(8,128)S(1)} %add.80), channel_id=1, source_target_pairs={{8,136},{24,152},{40,168},{56,184},{72,200},{88,216},{104,232},{12... | collective-permute-start | bytes 1572872 | tf_op jit(solution)/shard_map/ppermute | solution.py:434
  (5 other events, 4.7 us)
Sparse Core Ops, SparseCore 0:
  101.5 65.5 all-gather.2

commit v3 on v2

--- a/solution.py
+++ b/solution.py
@@ -96,7 +96,7 @@
             jax.ShapeDtypeStruct((dests, pieces, HD), half.dtype),
             jax.ShapeDtypeStruct((n_dp, text_rows, depth), half.dtype),
         ],
-        compiler_params=pltpu.CompilerParams(vmem_limit_bytes=16 * MIB),
+        compiler_params=pltpu.CompilerParams(vmem_limit_bytes=12 * MIB),
         cost_estimate=pl.CostEstimate(
             flops=4 * text.size, bytes_accessed=2 * dests * pieces * HD + 4 * rows * width, transcendentals=0
         ),
@@ -128,7 +128,7 @@
             out_specs=pl.BlockSpec((dests, 2, rows // 2, HD), lambda j, spot_ref: (0, 0, 0, 0)),
         ),
         out_shape=jax.ShapeDtypeStruct((dests, 2, rows // 2, HD), half.dtype),
-        compiler_params=pltpu.CompilerParams(vmem_limit_bytes=12 * MIB),
+        compiler_params=pltpu.CompilerParams(vmem_limit_bytes=8 * MIB),
         cost_estimate=pl.CostEstimate(flops=0, bytes_accessed=4 * rows * width * 2, transcendentals=0),
         name="pack",
     )(spot, wide, half)
@@ -149,7 +149,7 @@
         unpack_kernel,
         in_specs=[pl.BlockSpec(memory_space=pltpu.SMEM), pl.BlockSpec(memory_space=pltpu.VMEM)],
         out_shape=jax.ShapeDtypeStruct((1, 2 * rows, width), pieces.dtype),
-        compiler_params=pltpu.CompilerParams(vmem_limit_bytes=8 * MIB),
+        compiler_params=pltpu.CompilerParams(vmem_limit_bytes=4 * MIB),
         cost_estimate=pl.CostEstimate(flops=0, bytes_accessed=8 * rows * width, transcendentals=0),
         name="unpack",
     )(spot, pieces)
@@ -204,7 +204,7 @@
             pltpu.VMEM((2, depth, columns // 2), jnp.bfloat16),
             pltpu.SemaphoreType.DMA((6,)),
         ],
-        compiler_params=pltpu.CompilerParams(vmem_limit_bytes=16 * MIB),
+        compiler_params=pltpu.CompilerParams(vmem_limit_bytes=10 * MIB),
         cost_estimate=pl.CostEstimate(
             flops=8 * sources * text_rows * depth * columns, bytes_accessed=4 * MIB, transcendentals=0
         ),
@@ -253,7 +253,7 @@
         give_ref[...] = total_ref[:, 1 - core].reshape(give_ref.shape)
 
 
-def cross_attend(length, spot, received, rows, near, far, blocks=4):
+def cross_attend(length, spot, received, rows, near, far, blocks=2):
     sources, pieces, _ = received.shape
     queries = sources * rows
     tokens, columns = near.shape
@@ -279,7 +279,7 @@
             jax.ShapeDtypeStruct((tokens // 2, columns), jnp.float32),
             jax.ShapeDtypeStruct((tokens // 2, columns), jnp.float32),
         ],
-        compiler_params=pltpu.CompilerParams(vmem_limit_bytes=24 * MIB),
+        compiler_params=pltpu.CompilerParams(vmem_limit_bytes=20 * MIB),
         cost_estimate=pl.CostEstimate(
             flops=10 * queries * tokens * HD, bytes_accessed=4 * MIB, transcendentals=queries * tokens
         ),
@@ -323,7 +323,7 @@
         ],
         out_specs=pl.BlockSpec((queries // blocks, HD), lambda j: (j, 0)),
         out_shape=jax.ShapeDtypeStruct((queries, HD), jnp.bfloat16),
-        compiler_params=pltpu.CompilerParams(vmem_limit_bytes=36 * MIB),
+        compiler_params=pltpu.CompilerParams(vmem_limit_bytes=20 * MIB),
         cost_estimate=pl.CostEstimate(
             flops=8 * queries * queries * HD, bytes_accessed=5 * MIB, transcendentals=2 * queries * queries
         ),
@@ -354,7 +354,7 @@
         in_specs=[pl.BlockSpec(memory_space=pltpu.SMEM), vmem, vmem],
         out_specs=[vmem, vmem],
         out_shape=[jax.ShapeDtypeStruct((depth, columns), jnp.float32)] * 2,
-        compiler_params=pltpu.CompilerParams(vmem_limit_bytes=20 * MIB),
+        compiler_params=pltpu.CompilerParams(vmem_limit_bytes=14 * MIB),
         cost_estimate=pl.CostEstimate(flops=4 * text.size * columns, bytes_accessed=6 * MIB, transcendentals=0),
         name="finish",
     )(spot, text, kv_all)
@@ -425,6 +425,7 @@
 
     far = lax.ppermute(near, "c", SWAP)
     out_rows = self_attend(received, near, far, cross_out)
+    spread, out_rows = lax.optimization_barrier((spread, out_rows))
     back = lax.all_to_all(out_rows.reshape(near.shape[0], rows, HD), PLANE, 0, 0, tiled=True)
     attended = unpack(spot, back)
 

time: 211 us -> 205 us (0.972)
  starting transfers between devices: 74.2 us -> 68.5 us
  blocking collectives: 46.9 us -> 42.8 us
  waiting for transfers between devices: 22.8 us -> 25.8 us
  local copies, waits for them, and re-layouts: 10.6 us -> 12.8 us
    all_to_all x1, blocking collectives: 30.7 us -> 21.7 us  [local(): by_sample = lax.all_to_all(blocks, 'd', 0, 0, tiled=True)]
    all_to_all x1, starting transfers between devices: 11.5 us -> 4.45 us  [local(): lax.all_to_all(jnp.broadcast_to(by_sample[None], (n_chips,) + by_sample.s...]
    all_to_all x1, blocking collectives: 16.2 us -> 21.1 us  [local(): lax.all_to_all(out_rows.reshape(near.shape[0], rows, HD), PLANE, 0, 0, ti...]
    ppermute x1, waiting for transfers between devices: 0.01 us -> 2.48 us  [local(): far = lax.ppermute(near, 'c', SWAP)]
    unnamed x26 -> x30, local copies, waits for them, and re-layouts: 10.4 us -> 11.1 us
  transfers between devices with their start and end apart: 16 -> 16, of which waited for: 5 -> 6; matrix products, arithmetic and copies ran while one was open for 2% -> 3% of each run, Pallas kernels for 14% -> 14%
where the time goes in v3:
time: 205 us; the launch traced here: 204 us
  starting transfers between devices  68.5 us (33%)
  blocking collectives  42.8 us (21%)
  Pallas kernels  33.9 us (17%)
  waiting for transfers between devices  25.8 us (13%)
  between operations  15.2 us (7%)
  local copies, waits for them, and re-layouts  12.8 us (6%)
  other arithmetic  5.08 us (2%)
    ppermute x5, starting transfers between devices, send(): return lax.ppermute(block, ('g', 'c', 'd'), pairs)  26.1 us
    all_to_all x1, blocking collectives, local(): by_sample = lax.all_to_all(blocks, 'd', 0, 0, tiled=True)  21.7 us
    all_to_all x1, blocking collectives, local(): lax.all_to_all(out_rows.reshape(near.shape[0], rows, HD), PLANE, 0, 0, ti...  21.1 us
    pallas_call x1, Pallas kernels, self_attend(): pl.pallas_call(self_kernel, grid=(blocks,), in_specs=[pl.BlockSpec((sourc...  17.2 us
    unnamed x30, local copies, waits for them, and re-layouts  11.1 us
    all_to_all x1, waiting for transfers between devices, local(): received = lax.all_to_all(sent, PLANE, 0, 0, tiled=True)  8.9 us
    ppermute x1, starting transfers between devices, local(): lax.ppermute(proj_weight, PLANE, [(2 * j + 1, 2 * across(j) + 1) for j in...  7.34 us
    ppermute x1, waiting for transfers between devices, local(): lax.ppermute(total, PLANE, [(2 * j + 1, 2 * across(j) + 1) for j in range...  6.92 us
  transfers between devices with their start and end apart: 16, of which 6 were waited for; matrix products, arithmetic and copies ran while one was open for 3% of the time, Pallas kernels for 14%

profile of v3, /device:TPU:1, one launch (start us, length us, event | category | flops | bytes accessed | tf_op | source)
XLA Modules:
  0.0 204.1 jit_solution(1118946186694093256)
XLA Ops:
  7.2 6.2 %collective-permute-start = (bf16[512,256]{1,0:T(8,128)(2,1)}, bf16[512,256]{1,0:T(8,128)(2,1)}, u32[]{:S(2)}, u32[]{:S(2)}) collective-permute-start(bf16[512,256]{1,0:T(8,128)(2,1)} %param.13), channel_id=1, source_target_pairs={{0,8},{16,24},{32,40},{48,56},{64,72},{80,88},{96,104},{112,120},{... | collective-permute-start | bytes 786440 | tf_op jit(solution)/shard_map/ppermute | solution.py:375
  13.4 7.3 %collective-permute-start.1 = (bf16[512,256]{1,0:T(8,128)(2,1)}, bf16[512,256]{1,0:T(8,128)(2,1)}, u32[]{:S(2)}, u32[]{:S(2)}) collective-permute-start(bf16[512,256]{1,0:T(8,128)(2,1)} %param.13), channel_id=1, source_target_pairs={{8,136},{24,152},{40,168},{56,184},{72,200},{88,216},{104,232},{12... | collective-permute-start | bytes 786440 | tf_op jit(solution)/shard_map/ppermute | solution.py:380
  27.9 4.0 %all-to-all-start = ((bf16[32,384,128]{2,1,0:T(8,128)(2,1)}), bf16[32,384,128]{2,1,0:T(8,128)(2,1)S(1)}, u32[]{:S(2)}, u32[]{:S(2)}) async-start(bf16[32,384,128]{2,1,0:T(8,128)(2,1)} %copy-done.1), calls=%async_computation | async-start | bytes 6291456 | tf_op jit(solution)/shard_map/all_to_all | solution.py:384
  34.7 9.1 %collective-permute-start.2 = (bf16[512,256]{1,0:T(8,128)(2,1)}, bf16[512,256]{1,0:T(8,128)(2,1)}, u32[]{:S(2)}, u32[]{:S(2)}) collective-permute-start(bf16[512,256]{1,0:T(8,128)(2,1)} %get-tuple-element.46), channel_id=1, source_target_pairs={{0,1},{1,2},{2,3},{3,4},{4,5},{5,6},{6,7},{7,256},{256,257},{257,2... | collective-permute-start | bytes 786440 | tf_op jit(solution)/shard_map/ppermute | solution.py:400
  43.8 3.1 %collective-permute-start.3 = (bf16[512,256]{1,0:T(8,128)(2,1)}, bf16[512,256]{1,0:T(8,128)(2,1)}, u32[]{:S(2)}, u32[]{:S(2)}) collective-permute-start(bf16[512,256]{1,0:T(8,128)(2,1)} %get-tuple-element.45), channel_id=1, source_target_pairs={{0,2},{1,3},{2,4},{3,5},{4,6},{5,7},{6,256},{7,257},{256,258},{257... | collective-permute-start | bytes 786440 | tf_op jit(solution)/shard_map/ppermute | solution.py:400
  46.9 4.7 %collective-permute-start.4 = (bf16[512,256]{1,0:T(8,128)(2,1)}, bf16[512,256]{1,0:T(8,128)(2,1)}, u32[]{:S(2)}, u32[]{:S(2)}) collective-permute-start(bf16[512,256]{1,0:T(8,128)(2,1)} %get-tuple-element.40), channel_id=1, source_target_pairs={{0,3},{1,4},{2,5},{3,6},{4,7},{5,256},{6,257},{7,258},{256,259},{2... | collective-permute-start | bytes 786440 | tf_op jit(solution)/shard_map/ppermute | solution.py:400
  52.4 2.8 %collective-permute-start.5 = (bf16[512,128]{1,0:T(8,128)(2,1)}, bf16[512,128]{1,0:T(8,128)(2,1)S(1)}, u32[]{:S(2)}, u32[]{:S(2)}) collective-permute-start(bf16[512,128]{1,0:T(8,128)(2,1)} %get-tuple-element.44), channel_id=1, source_target_pairs={{8,268},{9,269},{10,270},{11,271},{12,8},{13,9},{14,10},{15,11},{2... | collective-permute-start | bytes 393224 | tf_op jit(solution)/shard_map/ppermute | solution.py:400
  55.2 6.4 %collective-permute-start.6 = (bf16[512,128]{1,0:T(8,128)(2,1)}, bf16[512,128]{1,0:T(8,128)(2,1)}, u32[]{:S(2)}, u32[]{:S(2)}) collective-permute-start(bf16[512,128]{1,0:T(8,128)(2,1)} %get-tuple-element.43), channel_id=1, source_target_pairs={{8,12},{9,13},{10,14},{11,15},{12,264},{13,265},{14,266},{15,267},... | collective-permute-start | bytes 393224 | tf_op jit(solution)/shard_map/ppermute | solution.py:400
  61.6 8.9 %all-to-all-done.text_ref.q_ref.c_ref = bf16[32,384,128]{2,1,0:T(8,128)(2,1)S(1)} async-done(((bf16[32,384,128]{2,1,0:T(8,128)(2,1)}), bf16[32,384,128]{2,1,0:T(8,128)(2,1)S(1)}, u32[]{:S(2)}, u32[]{:S(2)}) %all-to-all-start) | async-done | bytes 3145760 | tf_op jit(solution)/shard_map/all_to_all | solution.py:384
  70.5 3.3 %project.1.near_ref = f32[512,256]{1,0:T(8,128)} custom-call(s32[4]{0:T(128)S(1)} %pad_add_fusion.spot_ref, bf16[32,384,128]{2,1,0:T(8,128)(2,1)S(1)} %all-to-all-done.text_ref.q_ref.c_ref, bf16[512,256]{1,0:T(8,128)(2,1)S(1)} %get-tuple-element.47.refs_0_, bf16[512,256]{1,0:T(8,128)(2,1)} %collective-permute-done.2.refs_1_, ...), custom_call_target="tpu_custom_call" | custom-call | flops 536870912 | bytes 4194304 | tf_op jit(solution)/shard_map/project/pallas_call | solution.py:192
  73.8 3.4 %collective-permute-start.7 = (f32[512,256]{1,0:T(8,128)}, f32[512,256]{1,0:T(8,128)}, u32[]{:S(2)}, u32[]{:S(2)}) collective-permute-start(f32[512,256]{1,0:T(8,128)} %project.1.near_ref), channel_id=1, source_target_pairs={{0,8},{8,0},{1,9},{9,1},{2,10},{10,2},{3,11},{11,3},{4,12},{12,4},... | collective-permute-start | bytes 1572872 | tf_op jit(solution)/shard_map/ppermute | solution.py:412
  79.1 5.1 %all-to-all-start.1 = ((bf16[32,2,64,128]{3,2,1,0:T(8,128)(2,1)}), bf16[32,2,64,128]{3,2,1,0:T(8,128)(2,1)}, u32[]{:S(2)}, u32[]{:S(2)}) async-start(bf16[32,2,64,128]{3,2,1,0:T(8,128)(2,1)} %copy-done), calls=%async_computation.1 | async-start | bytes 2097152 | tf_op jit(solution)/shard_map/all_to_all | solution.py:409
  84.9 6.6 %cross.1 = (f32[2048,128]{1,0:T(8,128)S(1)}, f32[256,256]{1,0:T(8,128)S(1)}, f32[256,256]{1,0:T(8,128)S(1)}) custom-call(s32[1]{0:T(128)S(6)} %copy.9.length_ref, s32[4]{0:T(128)S(1)} %pad_add_fusion.spot_ref, bf16[32,384,128]{2,1,0:T(8,128)(2,1)S(1)} %all-to-all-done.text_ref.q_ref.c_ref, bf16[32,384,128]{2,1,0:T(8,128)(2,1)S(1)} %all-to-all-done.text_ref.q_ref.c_ref, ...), custom_call_target="tpu_custom_call" | custom-call | flops 1342177280 | bytes 4194304 | tf_op jit(solution)/shard_map/cross/pallas_call | solution.py:263
  96.7 4.7 %all-to-all-done.1.near_ref = bf16[32,2,64,128]{3,2,1,0:T(8,128)(2,1)} async-done(((bf16[32,2,64,128]{3,2,1,0:T(8,128)(2,1)}), bf16[32,2,64,128]{3,2,1,0:T(8,128)(2,1)}, u32[]{:S(2)}, u32[]{:S(2)}) %all-to-all-start.1) | async-done | bytes 1048608 | tf_op jit(solution)/shard_map/all_to_all | solution.py:409
  101.4 21.7 %all_to_all.25 = bf16[8,16,512]{2,1,0:T(8,128)(2,1)S(1)} all-to-all(bf16[8,16,512]{2,1,0:T(8,128)(2,1)S(1)} %copy-done.11), channel_id=1, replica_groups=mesh['g'=2,'y'=4,'x'=4,'c'=2,'d'=8] {'d'}, dimensions={0} | all-to-all | bytes 262144 | tf_op jit(solution)/shard_map/all_to_all | solution.py:421
  124.8 4.5 %all-to-all-start.3 = ((bf16[16,8,16,512]{3,2,1,0:T(8,128)(2,1)}), bf16[16,8,16,512]{3,2,1,0:T(8,128)(2,1)}, u32[]{:S(2)}, u32[]{:S(2)}) async-start(bf16[16,8,16,512]{3,2,1,0:T(8,128)(2,1)} %broadcast_in_dim.2), calls=%async_computation.3 | async-start | bytes 4194304 | tf_op jit(solution)/shard_map/all_to_all | solution.py:422
  129.2 4.4 %collective-permute-start.9 = (bf16[32,2,64,128]{3,2,1,0:T(8,128)(2,1)}, bf16[32,2,64,128]{3,2,1,0:T(8,128)(2,1)S(1)}, u32[]{:S(2)}, u32[]{:S(2)}) collective-permute-start(bf16[32,2,64,128]{3,2,1,0:T(8,128)(2,1)} %all-to-all-done.1.near_ref), channel_id=1, source_target_pairs={{0,8},{8,0},{1,9},{9,1},{2,10},{10,2},{3,11},{11,3},{4,12},{12,4},... | collective-permute-start | bytes 3145736 | tf_op jit(solution)/shard_map/ppermute | solution.py:426
  133.6 2.5 %collective-permute-done.9.far_ref = bf16[32,2,64,128]{3,2,1,0:T(8,128)(2,1)S(1)} collective-permute-done((bf16[32,2,64,128]{3,2,1,0:T(8,128)(2,1)}, bf16[32,2,64,128]{3,2,1,0:T(8,128)(2,1)S(1)}, u32[]{:S(2)}, u32[]{:S(2)}) %collective-permute-start.9) | collective-permute-done | bytes 1048608 | tf_op jit(solution)/shard_map/ppermute | solution.py:426
  137.3 17.2 %self_attention.1 = bf16[2048,128]{1,0:T(8,128)(2,1)S(1)} custom-call(bf16[32,384,128]{2,1,0:T(8,128)(2,1)S(1)} %all-to-all-done.text_ref.q_ref.c_ref, bf16[32,2,64,128]{3,2,1,0:T(8,128)(2,1)} %all-to-all-done.1.near_ref, bf16[32,2,64,128]{3,2,1,0:T(8,128)(2,1)S(1)} %collective-permute-done.9.far_ref, f32[2048,128]{1,0:T(8,128)S(1)} %copy-done.13), custom_call_target="tpu_custom_call" | custom-call | flops 4294967296 | bytes 5242880 | tf_op jit(solution)/shard_map/self_attention/pallas_call | solution.py:315
  155.3 21.1 %all_to_all.26.in_ref = bf16[32,64,128]{2,1,0:T(8,128)(2,1)} all-to-all(bf16[32,64,128]{2,1,0:T(8,128)(2,1)} %bitcast.7), channel_id=1, replica_groups=mesh['g'=2,'y'=4,'x'=4,'c'=2,'d'=8] {'y','x','c'}, dimensions={0} | all-to-all | bytes 1048576 | tf_op jit(solution)/shard_map/all_to_all | solution.py:429
  178.1 2.9 %finish.1 = (f32[512,256]{1,0:T(8,128)S(1)}, f32[512,256]{1,0:T(8,128)S(1)}) custom-call(s32[4]{0:T(128)S(1)} %pad_add_fusion.spot_ref, bf16[16,8,16,512]{3,2,1,0:T(8,128)(2,1)} %all-to-all-done.3.text_ref, bf16[16,256,256]{2,1,0:T(8,128)(2,1)S(1)} %bitcast.6), custom_call_target="tpu_custom_call" | custom-call | flops 1073741824 | bytes 6291456 | tf_op jit(solution)/shard_map/finish/pallas_call | solution.py:352
  181.0 2.4 %collective-permute-start.10 = (f32[512,256]{1,0:T(8,128)S(1)}, f32[512,256]{1,0:T(8,128)S(1)}, u32[]{:S(2)}, u32[]{:S(2)}) collective-permute-start(f32[512,256]{1,0:T(8,128)S(1)} %get-tuple-element.39), channel_id=1, source_target_pairs={{0,8},{8,0},{1,9},{9,1},{2,10},{10,2},{3,11},{11,3},{4,12},{12,4},... | collective-permute-start | bytes 1572872 | tf_op jit(solution)/shard_map/ppermute | solution.py:434
  185.0 3.0 %collective-permute-start.11 = (f32[512,256]{1,0:T(8,128)S(1)}, f32[512,256]{1,0:T(8,128)S(1)}, u32[]{:S(2)}, u32[]{:S(2)}) collective-permute-start(f32[512,256]{1,0:T(8,128)S(1)} %add.80), channel_id=1, source_target_pairs={{8,136},{24,152},{40,168},{56,184},{72,200},{88,216},{104,232},{12... | collective-permute-start | bytes 1572872 | tf_op jit(solution)/shard_map/ppermute | solution.py:435
  189.5 6.9 %collective-permute-done.11 = f32[512,256]{1,0:T(8,128)S(1)} collective-permute-done((f32[512,256]{1,0:T(8,128)S(1)}, f32[512,256]{1,0:T(8,128)S(1)}, u32[]{:S(2)}, u32[]{:S(2)}) %collective-permute-start.11) | collective-permute-done | bytes 524320 | tf_op jit(solution)/shard_map/ppermute | solution.py:435
  (56 shorter events, 26.7 us)
Async XLA Ops:
  7.2 20.7 %collective-permute-start = (bf16[512,256]{1,0:T(8,128)(2,1)}, bf16[512,256]{1,0:T(8,128)(2,1)}, u32[]{:S(2)}, u32[]{:S(2)}) collective-permute-start(bf16[512,256]{1,0:T(8,128)(2,1)} %param.13), channel_id=1, source_target_pairs={{0,8},{16,24},{32,40},{48,56},{64,72},{80,88},{96,104},{112,120},{... | collective-permute-start | bytes 786440 | tf_op jit(solution)/shard_map/ppermute | solution.py:375
  13.4 14.5 %collective-permute-start.1 = (bf16[512,256]{1,0:T(8,128)(2,1)}, bf16[512,256]{1,0:T(8,128)(2,1)}, u32[]{:S(2)}, u32[]{:S(2)}) collective-permute-start(bf16[512,256]{1,0:T(8,128)(2,1)} %param.13), channel_id=1, source_target_pairs={{8,136},{24,152},{40,168},{56,184},{72,200},{88,216},{104,232},{12... | collective-permute-start | bytes 786440 | tf_op jit(solution)/shard_map/ppermute | solution.py:380
  25.6 1.6 copy-start.1
  27.9 4.2 %copy-start.14 = (bf16[512,256]{1,0:T(8,128)(2,1)S(1)}, bf16[512,256]{1,0:T(8,128)(2,1)}, u32[]{:S(2)}) copy-start(bf16[512,256]{1,0:T(8,128)(2,1)} %param.13) | copy-start | bytes 786436
  27.9 42.6 %all-to-all-start = ((bf16[32,384,128]{2,1,0:T(8,128)(2,1)}), bf16[32,384,128]{2,1,0:T(8,128)(2,1)S(1)}, u32[]{:S(2)}, u32[]{:S(2)}) async-start(bf16[32,384,128]{2,1,0:T(8,128)(2,1)} %copy-done.1), calls=%async_computation | async-start | bytes 6291456 | tf_op jit(solution)/shard_map/all_to_all | solution.py:384
  34.7 35.8 %collective-permute-start.2 = (bf16[512,256]{1,0:T(8,128)(2,1)}, bf16[512,256]{1,0:T(8,128)(2,1)}, u32[]{:S(2)}, u32[]{:S(2)}) collective-permute-start(bf16[512,256]{1,0:T(8,128)(2,1)} %get-tuple-element.46), channel_id=1, source_target_pairs={{0,1},{1,2},{2,3},{3,4},{4,5},{5,6},{6,7},{7,256},{256,257},{257,2... | collective-permute-start | bytes 786440 | tf_op jit(solution)/shard_map/ppermute | solution.py:400
  43.8 26.7 %collective-permute-start.3 = (bf16[512,256]{1,0:T(8,128)(2,1)}, bf16[512,256]{1,0:T(8,128)(2,1)}, u32[]{:S(2)}, u32[]{:S(2)}) collective-permute-start(bf16[512,256]{1,0:T(8,128)(2,1)} %get-tuple-element.45), channel_id=1, source_target_pairs={{0,2},{1,3},{2,4},{3,5},{4,6},{5,7},{6,256},{7,257},{256,258},{257... | collective-permute-start | bytes 786440 | tf_op jit(solution)/shard_map/ppermute | solution.py:400
  46.9 23.6 %collective-permute-start.4 = (bf16[512,256]{1,0:T(8,128)(2,1)}, bf16[512,256]{1,0:T(8,128)(2,1)}, u32[]{:S(2)}, u32[]{:S(2)}) collective-permute-start(bf16[512,256]{1,0:T(8,128)(2,1)} %get-tuple-element.40), channel_id=1, source_target_pairs={{0,3},{1,4},{2,5},{3,6},{4,7},{5,256},{6,257},{7,258},{256,259},{2... | collective-permute-start | bytes 786440 | tf_op jit(solution)/shard_map/ppermute | solution.py:400
  52.4 18.1 %collective-permute-start.5 = (bf16[512,128]{1,0:T(8,128)(2,1)}, bf16[512,128]{1,0:T(8,128)(2,1)S(1)}, u32[]{:S(2)}, u32[]{:S(2)}) collective-permute-start(bf16[512,128]{1,0:T(8,128)(2,1)} %get-tuple-element.44), channel_id=1, source_target_pairs={{8,268},{9,269},{10,270},{11,271},{12,8},{13,9},{14,10},{15,11},{2... | collective-permute-start | bytes 393224 | tf_op jit(solution)/shard_map/ppermute | solution.py:400
  55.2 15.3 %collective-permute-start.6 = (bf16[512,128]{1,0:T(8,128)(2,1)}, bf16[512,128]{1,0:T(8,128)(2,1)}, u32[]{:S(2)}, u32[]{:S(2)}) collective-permute-start(bf16[512,128]{1,0:T(8,128)(2,1)} %get-tuple-element.43), channel_id=1, source_target_pairs={{8,12},{9,13},{10,14},{11,15},{12,264},{13,265},{14,266},{15,267},... | collective-permute-start | bytes 393224 | tf_op jit(solution)/shard_map/ppermute | solution.py:400
  70.5 6.7 %copy-start.5 = (bf16[1,128,4096]{2,1,0:T(8,128)(2,1)S(1)}, bf16[1,128,4096]{2,1,0:T(8,128)(2,1)}, u32[]{:S(2)}) copy-start(bf16[1,128,4096]{2,1,0:T(8,128)(2,1)} %wide_ref) | copy-start | bytes 3145732
  70.5 6.7 %copy-start.8 = (bf16[1,128,2048]{2,1,0:T(8,128)(2,1)S(1)}, bf16[1,128,2048]{2,1,0:T(8,128)(2,1)}, u32[]{:S(2)}) copy-start(bf16[1,128,2048]{2,1,0:T(8,128)(2,1)} %half_ref) | copy-start | bytes 1572868
  73.8 11.1 %collective-permute-start.7 = (f32[512,256]{1,0:T(8,128)}, f32[512,256]{1,0:T(8,128)}, u32[]{:S(2)}, u32[]{:S(2)}) collective-permute-start(f32[512,256]{1,0:T(8,128)} %project.1.near_ref), channel_id=1, source_target_pairs={{0,8},{8,0},{1,9},{9,1},{2,10},{10,2},{3,11},{11,3},{4,12},{12,4},... | collective-permute-start | bytes 1572872 | tf_op jit(solution)/shard_map/ppermute | solution.py:412
  79.1 22.3 %all-to-all-start.1 = ((bf16[32,2,64,128]{3,2,1,0:T(8,128)(2,1)}), bf16[32,2,64,128]{3,2,1,0:T(8,128)(2,1)}, u32[]{:S(2)}, u32[]{:S(2)}) async-start(bf16[32,2,64,128]{3,2,1,0:T(8,128)(2,1)} %copy-done), calls=%async_computation.1 | async-start | bytes 2097152 | tf_op jit(solution)/shard_map/all_to_all | solution.py:409
  84.2 92.3 %all-gather.3.cloned.1.call-start = ((), (), s32[]{:S(2)}) async-start(), calls=%async_computation.5 | async-start | bytes 2228224 | tf_op jit(solution)/shard_map/all_gather | solution.py:419
  84.9 16.6 %copy-start.11 = (bf16[8,16,512]{2,1,0:T(8,128)(2,1)S(1)}, bf16[8,16,512]{2,1,0:T(8,128)(2,1)}, u32[]{:S(2)}) copy-start(bf16[8,16,512]{2,1,0:T(8,128)(2,1)} %copy-done.10) | copy-start | bytes 393220
  92.6 3.4 %collective-permute-start.8 = (f32[256,256]{1,0:T(8,128)S(1)}, f32[256,256]{1,0:T(8,128)S(1)}, u32[]{:S(2)}, u32[]{:S(2)}) collective-permute-start(f32[256,256]{1,0:T(8,128)S(1)} %get-tuple-element.27), channel_id=1, source_target_pairs={{0,8},{8,0},{1,9},{9,1},{2,10},{10,2},{3,11},{11,3},{4,12},{12,4},... | collective-permute-start | bytes 786440 | tf_op jit(solution)/shard_map/ppermute | solution.py:416
  124.8 30.6 %all-to-all-start.3 = ((bf16[16,8,16,512]{3,2,1,0:T(8,128)(2,1)}), bf16[16,8,16,512]{3,2,1,0:T(8,128)(2,1)}, u32[]{:S(2)}, u32[]{:S(2)}) async-start(bf16[16,8,16,512]{3,2,1,0:T(8,128)(2,1)} %broadcast_in_dim.2), calls=%async_computation.3 | async-start | bytes 4194304 | tf_op jit(solution)/shard_map/all_to_all | solution.py:422
  129.2 6.8 %collective-permute-start.9 = (bf16[32,2,64,128]{3,2,1,0:T(8,128)(2,1)}, bf16[32,2,64,128]{3,2,1,0:T(8,128)(2,1)S(1)}, u32[]{:S(2)}, u32[]{:S(2)}) collective-permute-start(bf16[32,2,64,128]{3,2,1,0:T(8,128)(2,1)} %all-to-all-done.1.near_ref), channel_id=1, source_target_pairs={{0,8},{8,0},{1,9},{9,1},{2,10},{10,2},{3,11},{11,3},{4,12},{12,4},... | collective-permute-start | bytes 3145736 | tf_op jit(solution)/shard_map/ppermute | solution.py:426
  136.1 1.2 copy-start.13
  176.5 1.6 copy-start.2
  178.1 9.9 %copy-start.3 = (bf16[32,64,128]{2,1,0:T(8,128)(2,1)S(1)}, bf16[32,64,128]{2,1,0:T(8,128)(2,1)}, u32[]{:S(2)}) copy-start(bf16[32,64,128]{2,1,0:T(8,128)(2,1)} %all_to_all.26.in_ref) | copy-start | bytes 1572868
  181.0 3.9 %collective-permute-start.10 = (f32[512,256]{1,0:T(8,128)S(1)}, f32[512,256]{1,0:T(8,128)S(1)}, u32[]{:S(2)}, u32[]{:S(2)}) collective-permute-start(f32[512,256]{1,0:T(8,128)S(1)} %get-tuple-element.39), channel_id=1, source_target_pairs={{0,8},{8,0},{1,9},{9,1},{2,10},{10,2},{3,11},{11,3},{4,12},{12,4},... | collective-permute-start | bytes 1572872 | tf_op jit(solution)/shard_map/ppermute | solution.py:434
  185.0 11.4 %collective-permute-start.11 = (f32[512,256]{1,0:T(8,128)S(1)}, f32[512,256]{1,0:T(8,128)S(1)}, u32[]{:S(2)}, u32[]{:S(2)}) collective-permute-start(f32[512,256]{1,0:T(8,128)S(1)} %add.80), channel_id=1, source_target_pairs={{8,136},{24,152},{40,168},{56,184},{72,200},{88,216},{104,232},{12... | collective-permute-start | bytes 1572872 | tf_op jit(solution)/shard_map/ppermute | solution.py:435
  (7 other events, 6.7 us)
Sparse Core Ops, SparseCore 0:
  101.6 65.0 all-gather.2

commit v4 on v3

--- a/solution.py
+++ b/solution.py
@@ -279,7 +279,7 @@
             jax.ShapeDtypeStruct((tokens // 2, columns), jnp.float32),
             jax.ShapeDtypeStruct((tokens // 2, columns), jnp.float32),
         ],
-        compiler_params=pltpu.CompilerParams(vmem_limit_bytes=20 * MIB),
+        compiler_params=pltpu.CompilerParams(vmem_limit_bytes=56 * MIB),
         cost_estimate=pl.CostEstimate(
             flops=10 * queries * tokens * HD, bytes_accessed=4 * MIB, transcendentals=queries * tokens
         ),
@@ -331,30 +331,49 @@
     )(received, near, far, cross_out)
 
 
-def finish_kernel(spot_ref, text_ref, kv_ref, keep_ref, give_ref):
+def finish_kernel(spot_ref, text_any, kv_any, keep_ref, give_ref, text_ref, kv_ref, sems):
     core, home = spot_ref[2], spot_ref[3]
-    n_dp = text_ref.shape[1]
-    tokens = kv_ref.shape[1]
+    n_dp = text_any.shape[1]
+    tokens = kv_any.shape[1]
     wanted = lax.rem(home + core, 2)
+    copies = [
+        (
+            pltpu.make_async_copy(text_any.at[:, sample], text_ref.at[sample], sems.at[0, sample]),
+            pltpu.make_async_copy(kv_any.at[wanted * n_dp + sample], kv_ref.at[0, sample], sems.at[1, sample]),
+            pltpu.make_async_copy(kv_any.at[(1 - wanted) * n_dp + sample], kv_ref.at[1, sample], sems.at[2, sample]),
+        )
+        for sample in range(n_dp)
+    ]
+    for group in copies:
+        for copy in group:
+            copy.start()
     keep, give = 0.0, 0.0
-    for sample in range(n_dp):
-        text = text_ref[:, sample].reshape(tokens, text_ref.shape[3])
-        keep += lax.dot_general(text, kv_ref[wanted * n_dp + sample], TN, preferred_element_type=jnp.float32)
-        give += lax.dot_general(text, kv_ref[(1 - wanted) * n_dp + sample], TN, preferred_element_type=jnp.float32)
+    for sample, group in enumerate(copies):
+        for copy in group:
+            copy.wait()
+        text = text_ref[sample].reshape(tokens, text_any.shape[3])
+        keep += lax.dot_general(text, kv_ref[0, sample], TN, preferred_element_type=jnp.float32)
+        give += lax.dot_general(text, kv_ref[1, sample], TN, preferred_element_type=jnp.float32)
     keep_ref[...] = keep
     give_ref[...] = give
 
 
 def finish(spot, text, kv_all):
-    depth = text.shape[3]
-    columns = kv_all.shape[2]
+    chips, n_dp, text_rows, depth = text.shape
+    _, tokens, columns = kv_all.shape
     vmem = pl.BlockSpec(memory_space=pltpu.VMEM)
+    hbm = pl.BlockSpec(memory_space=pltpu.HBM)
     return pl.pallas_call(
         finish_kernel,
-        in_specs=[pl.BlockSpec(memory_space=pltpu.SMEM), vmem, vmem],
+        in_specs=[pl.BlockSpec(memory_space=pltpu.SMEM), hbm, hbm],
         out_specs=[vmem, vmem],
         out_shape=[jax.ShapeDtypeStruct((depth, columns), jnp.float32)] * 2,
-        compiler_params=pltpu.CompilerParams(vmem_limit_bytes=14 * MIB),
+        scratch_shapes=[
+            pltpu.VMEM((n_dp, chips, text_rows, depth), text.dtype),
+            pltpu.VMEM((2, n_dp, tokens, columns), kv_all.dtype),
+            pltpu.SemaphoreType.DMA((3, n_dp)),
+        ],
+        compiler_params=pltpu.CompilerParams(vmem_limit_bytes=56 * MIB),
         cost_estimate=pl.CostEstimate(flops=4 * text.size * columns, bytes_accessed=6 * MIB, transcendentals=0),
         name="finish",
     )(spot, text, kv_all)
@@ -432,8 +451,10 @@
     spread, back = lax.optimization_barrier((spread, back))
     keep, give = finish(spot, spread, kv_all)
     total = keep + lax.ppermute(give, "c", SWAP)
-    moved = lax.ppermute(total, PLANE, [(2 * j + 1, 2 * across(j) + 1) for j in range(n_chips)])
-    proj_grad = jnp.where(core == 0, total, moved)
+    moved = lax.ppermute(
+        total.astype(jnp.bfloat16), PLANE, [(2 * j + 1, 2 * across(j) + 1) for j in range(n_chips)]
+    )
+    proj_grad = jnp.where(core == 0, total, moved.astype(jnp.float32))
     return attended, proj_grad
 
 

time: 205 us -> 204 us (level)
  waiting for transfers between devices: 25.8 us -> 21.2 us
  Pallas kernels: 33.9 us -> 38 us
  local copies, waits for them, and re-layouts: 12.8 us -> 10.4 us
  other arithmetic: 5.08 us -> 7.16 us
    ppermute x1, waiting for transfers between devices: 6.92 us -> 3.41 us  [local(): lax.ppermute(total.astype(jnp.bfloat16), PLANE, [(2 * j + 1, 2 * across(j...]
    unnamed x30 -> x34, local copies, waits for them, and re-layouts: 11.1 us -> 8.73 us
where the time goes in v4:
time: 204 us; the launch traced here: 203 us
  starting transfers between devices  68.4 us (34%)
  blocking collectives  42.5 us (21%)
  Pallas kernels  38 us (19%)
  waiting for transfers between devices  21.2 us (10%)
  between operations  15.2 us (7%)
  local copies, waits for them, and re-layouts  10.4 us (5%)
  other arithmetic  7.16 us (4%)
    ppermute x5, starting transfers between devices, send(): return lax.ppermute(block, ('g', 'c', 'd'), pairs)  26.1 us
    all_to_all x1, blocking collectives, local(): by_sample = lax.all_to_all(blocks, 'd', 0, 0, tiled=True)  22.1 us
    all_to_all x1, blocking collectives, local(): lax.all_to_all(out_rows.reshape(near.shape[0], rows, HD), PLANE, 0, 0, ti...  20.4 us
    pallas_call x1, Pallas kernels, self_attend(): pl.pallas_call(self_kernel, grid=(blocks,), in_specs=[pl.BlockSpec((sourc...  16 us
    all_to_all x1, waiting for transfers between devices, local(): received = lax.all_to_all(sent, PLANE, 0, 0, tiled=True)  8.85 us
    unnamed x34, local copies, waits for them, and re-layouts  8.73 us
    pallas_call x1, Pallas kernels, cross_attend(): pl.pallas_call(cross_kernel, grid_spec=pltpu.PrefetchScalarGridSpec(num_s...  7.94 us
    ppermute x1, starting transfers between devices, local(): lax.ppermute(proj_weight, PLANE, [(2 * j + 1, 2 * across(j) + 1) for j in...  7.34 us
  transfers between devices with their start and end apart: 16, of which 6 were waited for; matrix products, arithmetic and copies ran while one was open for 3% of the time, Pallas kernels for 14%

profile of v4, /device:TPU:1, one launch (start us, length us, event | category | flops | bytes accessed | tf_op | source)
XLA Modules:
  0.0 202.9 jit_solution(11831427538144286489)
XLA Ops:
  7.2 6.2 %collective-permute-start = (bf16[512,256]{1,0:T(8,128)(2,1)}, bf16[512,256]{1,0:T(8,128)(2,1)}, u32[]{:S(2)}, u32[]{:S(2)}) collective-permute-start(bf16[512,256]{1,0:T(8,128)(2,1)} %param.13), channel_id=1, source_target_pairs={{0,8},{16,24},{32,40},{48,56},{64,72},{80,88},{96,104},{112,120},{... | collective-permute-start | bytes 786440 | tf_op jit(solution)/shard_map/ppermute | solution.py:394
  13.4 7.3 %collective-permute-start.1 = (bf16[512,256]{1,0:T(8,128)(2,1)}, bf16[512,256]{1,0:T(8,128)(2,1)}, u32[]{:S(2)}, u32[]{:S(2)}) collective-permute-start(bf16[512,256]{1,0:T(8,128)(2,1)} %param.13), channel_id=1, source_target_pairs={{8,136},{24,152},{40,168},{56,184},{72,200},{88,216},{104,232},{12... | collective-permute-start | bytes 786440 | tf_op jit(solution)/shard_map/ppermute | solution.py:399
  27.9 4.0 %all-to-all-start = ((bf16[32,384,128]{2,1,0:T(8,128)(2,1)}), bf16[32,384,128]{2,1,0:T(8,128)(2,1)S(1)}, u32[]{:S(2)}, u32[]{:S(2)}) async-start(bf16[32,384,128]{2,1,0:T(8,128)(2,1)} %copy-done.2), calls=%async_computation | async-start | bytes 6291456 | tf_op jit(solution)/shard_map/all_to_all | solution.py:403
  34.8 9.1 %collective-permute-start.2 = (bf16[512,256]{1,0:T(8,128)(2,1)}, bf16[512,256]{1,0:T(8,128)(2,1)}, u32[]{:S(2)}, u32[]{:S(2)}) collective-permute-start(bf16[512,256]{1,0:T(8,128)(2,1)} %get-tuple-element.48), channel_id=1, source_target_pairs={{0,1},{1,2},{2,3},{3,4},{4,5},{5,6},{6,7},{7,256},{256,257},{257,2... | collective-permute-start | bytes 786440 | tf_op jit(solution)/shard_map/ppermute | solution.py:419
  43.9 3.1 %collective-permute-start.3 = (bf16[512,256]{1,0:T(8,128)(2,1)}, bf16[512,256]{1,0:T(8,128)(2,1)}, u32[]{:S(2)}, u32[]{:S(2)}) collective-permute-start(bf16[512,256]{1,0:T(8,128)(2,1)} %get-tuple-element.47), channel_id=1, source_target_pairs={{0,2},{1,3},{2,4},{3,5},{4,6},{5,7},{6,256},{7,257},{256,258},{257... | collective-permute-start | bytes 786440 | tf_op jit(solution)/shard_map/ppermute | solution.py:419
  46.9 4.7 %collective-permute-start.4 = (bf16[512,256]{1,0:T(8,128)(2,1)}, bf16[512,256]{1,0:T(8,128)(2,1)}, u32[]{:S(2)}, u32[]{:S(2)}) collective-permute-start(bf16[512,256]{1,0:T(8,128)(2,1)} %get-tuple-element.42), channel_id=1, source_target_pairs={{0,3},{1,4},{2,5},{3,6},{4,7},{5,256},{6,257},{7,258},{256,259},{2... | collective-permute-start | bytes 786440 | tf_op jit(solution)/shard_map/ppermute | solution.py:419
  52.5 2.8 %collective-permute-start.5 = (bf16[512,128]{1,0:T(8,128)(2,1)}, bf16[512,128]{1,0:T(8,128)(2,1)S(1)}, u32[]{:S(2)}, u32[]{:S(2)}) collective-permute-start(bf16[512,128]{1,0:T(8,128)(2,1)} %get-tuple-element.46), channel_id=1, source_target_pairs={{8,268},{9,269},{10,270},{11,271},{12,8},{13,9},{14,10},{15,11},{2... | collective-permute-start | bytes 393224 | tf_op jit(solution)/shard_map/ppermute | solution.py:419
  55.3 6.4 %collective-permute-start.6 = (bf16[512,128]{1,0:T(8,128)(2,1)}, bf16[512,128]{1,0:T(8,128)(2,1)}, u32[]{:S(2)}, u32[]{:S(2)}) collective-permute-start(bf16[512,128]{1,0:T(8,128)(2,1)} %get-tuple-element.45), channel_id=1, source_target_pairs={{8,12},{9,13},{10,14},{11,15},{12,264},{13,265},{14,266},{15,267},... | collective-permute-start | bytes 393224 | tf_op jit(solution)/shard_map/ppermute | solution.py:419
  61.6 8.8 %all-to-all-done.text_ref.q_ref.c_ref = bf16[32,384,128]{2,1,0:T(8,128)(2,1)S(1)} async-done(((bf16[32,384,128]{2,1,0:T(8,128)(2,1)}), bf16[32,384,128]{2,1,0:T(8,128)(2,1)S(1)}, u32[]{:S(2)}, u32[]{:S(2)}) %all-to-all-start) | async-done | bytes 3145760 | tf_op jit(solution)/shard_map/all_to_all | solution.py:403
  70.6 4.3 %project.1.near_ref = f32[512,256]{1,0:T(8,128)} custom-call(s32[4]{0:T(128)S(1)} %pad_add_fusion.spot_ref, bf16[32,384,128]{2,1,0:T(8,128)(2,1)S(1)} %all-to-all-done.text_ref.q_ref.c_ref, bf16[512,256]{1,0:T(8,128)(2,1)S(1)} %get-tuple-element.49.refs_0_, bf16[512,256]{1,0:T(8,128)(2,1)} %collective-permute-done.2.refs_1_, ...), custom_call_target="tpu_custom_call" | custom-call | flops 536870912 | bytes 4194304 | tf_op jit(solution)/shard_map/project/pallas_call | solution.py:192
  74.8 3.4 %collective-permute-start.7 = (f32[512,256]{1,0:T(8,128)}, f32[512,256]{1,0:T(8,128)}, u32[]{:S(2)}, u32[]{:S(2)}) collective-permute-start(f32[512,256]{1,0:T(8,128)} %project.1.near_ref), channel_id=1, source_target_pairs={{0,8},{8,0},{1,9},{9,1},{2,10},{10,2},{3,11},{11,3},{4,12},{12,4},... | collective-permute-start | bytes 1572872 | tf_op jit(solution)/shard_map/ppermute | solution.py:431
  80.1 4.1 %all-to-all-start.1 = ((bf16[32,2,64,128]{3,2,1,0:T(8,128)(2,1)}), bf16[32,2,64,128]{3,2,1,0:T(8,128)(2,1)S(1)}, u32[]{:S(2)}, u32[]{:S(2)}) async-start(bf16[32,2,64,128]{3,2,1,0:T(8,128)(2,1)} %pack.1), calls=%async_computation.1 | async-start | bytes 2097152 | tf_op jit(solution)/shard_map/all_to_all | solution.py:428
  84.9 7.9 %cross.1 = (f32[2048,128]{1,0:T(8,128)}, f32[256,256]{1,0:T(8,128)}, f32[256,256]{1,0:T(8,128)}) custom-call(s32[1]{0:T(128)S(6)} %copy.9.length_ref, s32[4]{0:T(128)} %copy-done.13, bf16[32,384,128]{2,1,0:T(8,128)(2,1)} %copy-done, bf16[32,384,128]{2,1,0:T(8,128)(2,1)} %copy-done, f32[512,256]{1,0:T(8,128)} %project.1.near_ref, ...), custom_call_target="tpu_custom_call" | custom-call | flops 1342177280 | bytes 4194304 | tf_op jit(solution)/shard_map/cross/pallas_call | solution.py:263
  98.1 3.3 %all-to-all-done.1.near_ref = bf16[32,2,64,128]{3,2,1,0:T(8,128)(2,1)S(1)} async-done(((bf16[32,2,64,128]{3,2,1,0:T(8,128)(2,1)}), bf16[32,2,64,128]{3,2,1,0:T(8,128)(2,1)S(1)}, u32[]{:S(2)}, u32[]{:S(2)}) %all-to-all-start.1) | async-done | bytes 1048608 | tf_op jit(solution)/shard_map/all_to_all | solution.py:428
  101.4 22.1 %all_to_all.25 = bf16[8,16,512]{2,1,0:T(8,128)(2,1)S(1)} all-to-all(bf16[8,16,512]{2,1,0:T(8,128)(2,1)S(1)} %copy-done.12), channel_id=1, replica_groups=mesh['g'=2,'y'=4,'x'=4,'c'=2,'d'=8] {'d'}, dimensions={0} | all-to-all | bytes 262144 | tf_op jit(solution)/shard_map/all_to_all | solution.py:440
  125.1 4.7 %all-to-all-start.3 = ((bf16[16,8,16,512]{3,2,1,0:T(8,128)(2,1)}), bf16[16,8,16,512]{3,2,1,0:T(8,128)(2,1)}, u32[]{:S(2)}, u32[]{:S(2)}) async-start(bf16[16,8,16,512]{3,2,1,0:T(8,128)(2,1)} %broadcast_in_dim.2), calls=%async_computation.3 | async-start | bytes 4194304 | tf_op jit(solution)/shard_map/all_to_all | solution.py:441
  129.8 4.3 %collective-permute-start.9 = (bf16[32,2,64,128]{3,2,1,0:T(8,128)(2,1)}, bf16[32,2,64,128]{3,2,1,0:T(8,128)(2,1)S(1)}, u32[]{:S(2)}, u32[]{:S(2)}) collective-permute-start(bf16[32,2,64,128]{3,2,1,0:T(8,128)(2,1)} %copy-done.5), channel_id=1, source_target_pairs={{0,8},{8,0},{1,9},{9,1},{2,10},{10,2},{3,11},{11,3},{4,12},{12,4},... | collective-permute-start | bytes 3145736 | tf_op jit(solution)/shard_map/ppermute | solution.py:445
  134.1 2.5 %collective-permute-done.9.far_ref = bf16[32,2,64,128]{3,2,1,0:T(8,128)(2,1)S(1)} collective-permute-done((bf16[32,2,64,128]{3,2,1,0:T(8,128)(2,1)}, bf16[32,2,64,128]{3,2,1,0:T(8,128)(2,1)S(1)}, u32[]{:S(2)}, u32[]{:S(2)}) %collective-permute-start.9) | collective-permute-done | bytes 1048608 | tf_op jit(solution)/shard_map/ppermute | solution.py:445
  139.1 16.0 %self_attention.1 = bf16[2048,128]{1,0:T(8,128)(2,1)S(1)} custom-call(bf16[32,384,128]{2,1,0:T(8,128)(2,1)S(1)} %copy-done.1, bf16[32,2,64,128]{3,2,1,0:T(8,128)(2,1)S(1)} %copy-done.6, bf16[32,2,64,128]{3,2,1,0:T(8,128)(2,1)S(1)} %collective-permute-done.9.far_ref, f32[2048,128]{1,0:T(8,128)S(1)} %copy-done.15), custom_call_target="tpu_custom_call" | custom-call | flops 4294967296 | bytes 5242880 | tf_op jit(solution)/shard_map/self_attention/pallas_call | solution.py:315
  155.9 20.4 %all_to_all.26.in_ref = bf16[32,64,128]{2,1,0:T(8,128)(2,1)S(1)} all-to-all(bf16[32,64,128]{2,1,0:T(8,128)(2,1)} %bitcast.6), channel_id=1, replica_groups=mesh['g'=2,'y'=4,'x'=4,'c'=2,'d'=8] {'y','x','c'}, dimensions={0} | all-to-all | bytes 1048576 | tf_op jit(solution)/shard_map/all_to_all | solution.py:448
  176.4 5.0 %finish.1 = (f32[512,256]{1,0:T(8,128)}, f32[512,256]{1,0:T(8,128)}) custom-call(s32[4]{0:T(128)} %copy-done.13, bf16[16,8,16,512]{3,2,1,0:T(8,128)(2,1)} %all-to-all-done.3.text_any, bf16[16,256,256]{2,1,0:T(8,128)(2,1)} %bitcast.7), custom_call_target="tpu_custom_call" | custom-call | flops 1073741824 | bytes 6291456 | tf_op jit(solution)/shard_map/finish/pallas_call | solution.py:366
  181.3 2.4 %collective-permute-start.10 = (f32[512,256]{1,0:T(8,128)}, f32[512,256]{1,0:T(8,128)S(1)}, u32[]{:S(2)}, u32[]{:S(2)}) collective-permute-start(f32[512,256]{1,0:T(8,128)} %get-tuple-element.39), channel_id=1, source_target_pairs={{0,8},{8,0},{1,9},{9,1},{2,10},{10,2},{3,11},{11,3},{4,12},{12,4},... | collective-permute-start | bytes 1572872 | tf_op jit(solution)/shard_map/ppermute | solution.py:453
  186.6 3.7 %collective-permute-start.11 = (bf16[512,256]{1,0:T(8,128)(2,1)S(1)}, bf16[512,256]{1,0:T(8,128)(2,1)S(1)}, u32[]{:S(2)}, u32[]{:S(2)}) collective-permute-start(bf16[512,256]{1,0:T(8,128)(2,1)S(1)} %get-tuple-element.40), channel_id=1, source_target_pairs={{8,136},{24,152},{40,168},{56,184},{72,200},{88,216},{104,232},{12... | collective-permute-start | bytes 786440 | tf_op jit(solution)/shard_map/ppermute | solution.py:454
  191.8 3.4 %collective-permute-done.11 = bf16[512,256]{1,0:T(8,128)(2,1)S(1)} collective-permute-done((bf16[512,256]{1,0:T(8,128)(2,1)S(1)}, bf16[512,256]{1,0:T(8,128)(2,1)S(1)}, u32[]{:S(2)}, u32[]{:S(2)}) %collective-permute-start.11) | collective-permute-done | bytes 262176 | tf_op jit(solution)/shard_map/ppermute | solution.py:454
  (60 shorter events, 27.8 us)
Async XLA Ops:
  7.2 20.7 %collective-permute-start = (bf16[512,256]{1,0:T(8,128)(2,1)}, bf16[512,256]{1,0:T(8,128)(2,1)}, u32[]{:S(2)}, u32[]{:S(2)}) collective-permute-start(bf16[512,256]{1,0:T(8,128)(2,1)} %param.13), channel_id=1, source_target_pairs={{0,8},{16,24},{32,40},{48,56},{64,72},{80,88},{96,104},{112,120},{... | collective-permute-start | bytes 786440 | tf_op jit(solution)/shard_map/ppermute | solution.py:394
  13.4 14.5 %collective-permute-start.1 = (bf16[512,256]{1,0:T(8,128)(2,1)}, bf16[512,256]{1,0:T(8,128)(2,1)}, u32[]{:S(2)}, u32[]{:S(2)}) collective-permute-start(bf16[512,256]{1,0:T(8,128)(2,1)} %param.13), channel_id=1, source_target_pairs={{8,136},{24,152},{40,168},{56,184},{72,200},{88,216},{104,232},{12... | collective-permute-start | bytes 786440 | tf_op jit(solution)/shard_map/ppermute | solution.py:399
  24.0 54.2 %copy-start.13 = (s32[4]{0:T(128)}, s32[4]{0:T(128)S(1)}, u32[]{:S(2)}) copy-start(s32[4]{0:T(128)S(1)} %pad_add_fusion.spot_ref) | copy-start | bytes 52
  27.9 42.6 %all-to-all-start = ((bf16[32,384,128]{2,1,0:T(8,128)(2,1)}), bf16[32,384,128]{2,1,0:T(8,128)(2,1)S(1)}, u32[]{:S(2)}, u32[]{:S(2)}) async-start(bf16[32,384,128]{2,1,0:T(8,128)(2,1)} %copy-done.2), calls=%async_computation | async-start | bytes 6291456 | tf_op jit(solution)/shard_map/all_to_all | solution.py:403
  34.8 35.7 %collective-permute-start.2 = (bf16[512,256]{1,0:T(8,128)(2,1)}, bf16[512,256]{1,0:T(8,128)(2,1)}, u32[]{:S(2)}, u32[]{:S(2)}) collective-permute-start(bf16[512,256]{1,0:T(8,128)(2,1)} %get-tuple-element.48), channel_id=1, source_target_pairs={{0,1},{1,2},{2,3},{3,4},{4,5},{5,6},{6,7},{7,256},{256,257},{257,2... | collective-permute-start | bytes 786440 | tf_op jit(solution)/shard_map/ppermute | solution.py:419
  43.9 26.7 %collective-permute-start.3 = (bf16[512,256]{1,0:T(8,128)(2,1)}, bf16[512,256]{1,0:T(8,128)(2,1)}, u32[]{:S(2)}, u32[]{:S(2)}) collective-permute-start(bf16[512,256]{1,0:T(8,128)(2,1)} %get-tuple-element.47), channel_id=1, source_target_pairs={{0,2},{1,3},{2,4},{3,5},{4,6},{5,7},{6,256},{7,257},{256,258},{257... | collective-permute-start | bytes 786440 | tf_op jit(solution)/shard_map/ppermute | solution.py:419
  46.9 23.6 %collective-permute-start.4 = (bf16[512,256]{1,0:T(8,128)(2,1)}, bf16[512,256]{1,0:T(8,128)(2,1)}, u32[]{:S(2)}, u32[]{:S(2)}) collective-permute-start(bf16[512,256]{1,0:T(8,128)(2,1)} %get-tuple-element.42), channel_id=1, source_target_pairs={{0,3},{1,4},{2,5},{3,6},{4,7},{5,256},{6,257},{7,258},{256,259},{2... | collective-permute-start | bytes 786440 | tf_op jit(solution)/shard_map/ppermute | solution.py:419
  52.5 18.0 %collective-permute-start.5 = (bf16[512,128]{1,0:T(8,128)(2,1)}, bf16[512,128]{1,0:T(8,128)(2,1)S(1)}, u32[]{:S(2)}, u32[]{:S(2)}) collective-permute-start(bf16[512,128]{1,0:T(8,128)(2,1)} %get-tuple-element.46), channel_id=1, source_target_pairs={{8,268},{9,269},{10,270},{11,271},{12,8},{13,9},{14,10},{15,11},{2... | collective-permute-start | bytes 393224 | tf_op jit(solution)/shard_map/ppermute | solution.py:419
  55.3 15.2 %collective-permute-start.6 = (bf16[512,128]{1,0:T(8,128)(2,1)}, bf16[512,128]{1,0:T(8,128)(2,1)}, u32[]{:S(2)}, u32[]{:S(2)}) collective-permute-start(bf16[512,128]{1,0:T(8,128)(2,1)} %get-tuple-element.45), channel_id=1, source_target_pairs={{8,12},{9,13},{10,14},{11,15},{12,264},{13,265},{14,266},{15,267},... | collective-permute-start | bytes 393224 | tf_op jit(solution)/shard_map/ppermute | solution.py:419
  70.5 4.3 %copy-start = (bf16[32,384,128]{2,1,0:T(8,128)(2,1)}, bf16[32,384,128]{2,1,0:T(8,128)(2,1)S(1)}, u32[]{:S(2)}) copy-start(bf16[32,384,128]{2,1,0:T(8,128)(2,1)S(1)} %all-to-all-done.text_ref.q_ref.c_ref) | copy-start | bytes 9437188
  70.5 7.7 %copy-start.4 = (bf16[1,128,4096]{2,1,0:T(8,128)(2,1)S(1)}, bf16[1,128,4096]{2,1,0:T(8,128)(2,1)}, u32[]{:S(2)}) copy-start(bf16[1,128,4096]{2,1,0:T(8,128)(2,1)} %wide_ref) | copy-start | bytes 3145732
  70.5 7.7 %copy-start.9 = (bf16[1,128,2048]{2,1,0:T(8,128)(2,1)S(1)}, bf16[1,128,2048]{2,1,0:T(8,128)(2,1)}, u32[]{:S(2)}) copy-start(bf16[1,128,2048]{2,1,0:T(8,128)(2,1)} %half_ref) | copy-start | bytes 1572868
  74.8 10.1 %collective-permute-start.7 = (f32[512,256]{1,0:T(8,128)}, f32[512,256]{1,0:T(8,128)}, u32[]{:S(2)}, u32[]{:S(2)}) collective-permute-start(f32[512,256]{1,0:T(8,128)} %project.1.near_ref), channel_id=1, source_target_pairs={{0,8},{8,0},{1,9},{9,1},{2,10},{10,2},{3,11},{11,3},{4,12},{12,4},... | collective-permute-start | bytes 1572872 | tf_op jit(solution)/shard_map/ppermute | solution.py:431
  80.1 21.3 %all-to-all-start.1 = ((bf16[32,2,64,128]{3,2,1,0:T(8,128)(2,1)}), bf16[32,2,64,128]{3,2,1,0:T(8,128)(2,1)S(1)}, u32[]{:S(2)}, u32[]{:S(2)}) async-start(bf16[32,2,64,128]{3,2,1,0:T(8,128)(2,1)} %pack.1), calls=%async_computation.1 | async-start | bytes 2097152 | tf_op jit(solution)/shard_map/all_to_all | solution.py:428
  84.2 92.2 %all-gather.3.cloned.1.call-start = ((), (), s32[]{:S(2)}) async-start(), calls=%async_computation.5 | async-start | bytes 2228224 | tf_op jit(solution)/shard_map/all_gather | solution.py:438
  84.9 16.5 %copy-start.12 = (bf16[8,16,512]{2,1,0:T(8,128)(2,1)S(1)}, bf16[8,16,512]{2,1,0:T(8,128)(2,1)}, u32[]{:S(2)}) copy-start(bf16[8,16,512]{2,1,0:T(8,128)(2,1)} %copy-done.11) | copy-start | bytes 393220
  92.8 3.6 %collective-permute-start.8 = (f32[256,256]{1,0:T(8,128)}, f32[256,256]{1,0:T(8,128)S(1)}, u32[]{:S(2)}, u32[]{:S(2)}) collective-permute-start(f32[256,256]{1,0:T(8,128)} %get-tuple-element.27), channel_id=1, source_target_pairs={{0,8},{8,0},{1,9},{9,1},{2,10},{10,2},{3,11},{11,3},{4,12},{12,4},... | collective-permute-start | bytes 786440 | tf_op jit(solution)/shard_map/ppermute | solution.py:435
  101.4 22.1 %copy-start.5 = (bf16[32,2,64,128]{3,2,1,0:T(8,128)(2,1)}, bf16[32,2,64,128]{3,2,1,0:T(8,128)(2,1)S(1)}, u32[]{:S(2)}) copy-start(bf16[32,2,64,128]{3,2,1,0:T(8,128)(2,1)S(1)} %all-to-all-done.1.near_ref) | copy-start | bytes 3145732
  125.1 11.5 %copy-start.1 = (bf16[32,384,128]{2,1,0:T(8,128)(2,1)S(1)}, bf16[32,384,128]{2,1,0:T(8,128)(2,1)}, u32[]{:S(2)}) copy-start(bf16[32,384,128]{2,1,0:T(8,128)(2,1)} %copy-done) | copy-start | bytes 9437188
  125.1 30.8 %all-to-all-start.3 = ((bf16[16,8,16,512]{3,2,1,0:T(8,128)(2,1)}), bf16[16,8,16,512]{3,2,1,0:T(8,128)(2,1)}, u32[]{:S(2)}, u32[]{:S(2)}) async-start(bf16[16,8,16,512]{3,2,1,0:T(8,128)(2,1)} %broadcast_in_dim.2), calls=%async_computation.3 | async-start | bytes 4194304 | tf_op jit(solution)/shard_map/all_to_all | solution.py:441
  129.8 6.8 %collective-permute-start.9 = (bf16[32,2,64,128]{3,2,1,0:T(8,128)(2,1)}, bf16[32,2,64,128]{3,2,1,0:T(8,128)(2,1)S(1)}, u32[]{:S(2)}, u32[]{:S(2)}) collective-permute-start(bf16[32,2,64,128]{3,2,1,0:T(8,128)(2,1)} %copy-done.5), channel_id=1, source_target_pairs={{0,8},{8,0},{1,9},{9,1},{2,10},{10,2},{3,11},{11,3},{4,12},{12,4},... | collective-permute-start | bytes 3145736 | tf_op jit(solution)/shard_map/ppermute | solution.py:445
  176.3 13.9 %copy-start.14 = (s32[4]{0:T(128)S(1)}, s32[4]{0:T(128)}, u32[]{:S(2)}) copy-start(s32[4]{0:T(128)} %copy-done.13) | copy-start | bytes 52
  181.3 4.1 %collective-permute-start.10 = (f32[512,256]{1,0:T(8,128)}, f32[512,256]{1,0:T(8,128)S(1)}, u32[]{:S(2)}, u32[]{:S(2)}) collective-permute-start(f32[512,256]{1,0:T(8,128)} %get-tuple-element.39), channel_id=1, source_target_pairs={{0,8},{8,0},{1,9},{9,1},{2,10},{10,2},{3,11},{11,3},{4,12},{12,4},... | collective-permute-start | bytes 1572872 | tf_op jit(solution)/shard_map/ppermute | solution.py:453
  186.6 8.6 %collective-permute-start.11 = (bf16[512,256]{1,0:T(8,128)(2,1)S(1)}, bf16[512,256]{1,0:T(8,128)(2,1)S(1)}, u32[]{:S(2)}, u32[]{:S(2)}) collective-permute-start(bf16[512,256]{1,0:T(8,128)(2,1)S(1)} %get-tuple-element.40), channel_id=1, source_target_pairs={{8,136},{24,152},{40,168},{56,184},{72,200},{88,216},{104,232},{12... | collective-permute-start | bytes 786440 | tf_op jit(solution)/shard_map/ppermute | solution.py:454
  (9 other events, 12.9 us)
Sparse Core Ops, SparseCore 0:
  101.5 65.5 all-gather.2

commit v5 on v4

--- a/solution.py
+++ b/solution.py
@@ -19,9 +19,15 @@
 SWAP = [(0, 1), (1, 0)]
 
 
+def mirrored(chip, chips, width=4):
+    return chips - width - chip + 2 * (chip % width)
+
+
 def column_of(chip, chips, side):
     half = chips // 2
-    return pl.multiple_of((2 * (chip % half) + lax.rem(chip // half + side, 2)) * HD, HD)
+    first = 2 * (chip % half)
+    second = 2 * (mirrored(chip, chips) % half) + 1
+    return pl.multiple_of(jnp.where(side == chip // half, first, second) * HD, HD)
 
 
 def prepare_kernel(
@@ -323,7 +329,7 @@
         ],
         out_specs=pl.BlockSpec((queries // blocks, HD), lambda j: (j, 0)),
         out_shape=jax.ShapeDtypeStruct((queries, HD), jnp.bfloat16),
-        compiler_params=pltpu.CompilerParams(vmem_limit_bytes=20 * MIB),
+        compiler_params=pltpu.CompilerParams(vmem_limit_bytes=56 * MIB),
         cost_estimate=pl.CostEstimate(
             flops=8 * queries * queries * HD, bytes_accessed=5 * MIB, transcendentals=2 * queries * queries
         ),
@@ -389,7 +395,7 @@
     text_rows, features = captions.shape[1:]
 
     def across(chip):
-        return (chip + n_chips // 2) % n_chips
+        return mirrored(chip, n_chips, lax.axis_size("x"))
 
     passed = lax.ppermute(
         proj_weight,

time: 204 us -> 203 us (level)
  local copies, waits for them, and re-layouts: 10.4 us -> 8.1 us
  Pallas kernels: 38 us -> 40.2 us
    unnamed x34 -> x30, local copies, waits for them, and re-layouts: 8.73 us -> 6.5 us
    pallas_call x1, Pallas kernels: 16 us -> 18.2 us  [self_attend(): pl.pallas_call(self_kernel, grid=(blocks,), in_specs=[pl.BlockSpec((sourc...]
  transfers between devices with their start and end apart: 16 -> 16, of which waited for: 6 -> 7; matrix products, arithmetic and copies ran while one was open for 3% -> 3% of each run, Pallas kernels for 14% -> 15%
where the time goes in v5:
time: 203 us; the launch traced here: 202 us
  starting transfers between devices  67.1 us (33%)
  blocking collectives  41.8 us (21%)
  Pallas kernels  40.2 us (20%)
  waiting for transfers between devices  22.2 us (11%)
  between operations  15.2 us (7%)
  local copies, waits for them, and re-layouts  8.1 us (4%)
  other arithmetic  7.09 us (3%)
    ppermute x5, starting transfers between devices, send(): return lax.ppermute(block, ('g', 'c', 'd'), pairs)  25.9 us
    all_to_all x1, blocking collectives, local(): by_sample = lax.all_to_all(blocks, 'd', 0, 0, tiled=True)  22.1 us
    all_to_all x1, blocking collectives, local(): lax.all_to_all(out_rows.reshape(near.shape[0], rows, HD), PLANE, 0, 0, ti...  19.7 us
    pallas_call x1, Pallas kernels, self_attend(): pl.pallas_call(self_kernel, grid=(blocks,), in_specs=[pl.BlockSpec((sourc...  18.2 us
    all_to_all x1, waiting for transfers between devices, local(): received = lax.all_to_all(sent, PLANE, 0, 0, tiled=True)  9.05 us
    pallas_call x1, Pallas kernels, cross_attend(): pl.pallas_call(cross_kernel, grid_spec=pltpu.PrefetchScalarGridSpec(num_s...  7.94 us
    ppermute x1, starting transfers between devices, local(): lax.ppermute(proj_weight, PLANE, [(2 * j + 1, 2 * across(j) + 1) for j in...  7.23 us
    unnamed x30, local copies, waits for them, and re-layouts  6.5 us
  transfers between devices with their start and end apart: 16, of which 7 were waited for; matrix products, arithmetic and copies ran while one was open for 3% of the time, Pallas kernels for 15%

profile of v5, /device:TPU:1, one launch (start us, length us, event | category | flops | bytes accessed | tf_op | source)
XLA Modules:
  0.0 201.6 jit_solution(537174449001794344)
XLA Ops:
  7.2 6.0 %collective-permute-start = (bf16[512,256]{1,0:T(8,128)(2,1)}, bf16[512,256]{1,0:T(8,128)(2,1)}, u32[]{:S(2)}, u32[]{:S(2)}) collective-permute-start(bf16[512,256]{1,0:T(8,128)(2,1)} %param.13), channel_id=1, source_target_pairs={{0,8},{16,24},{32,40},{48,56},{64,72},{80,88},{96,104},{112,120},{... | collective-permute-start | bytes 786440 | tf_op jit(solution)/shard_map/ppermute | solution.py:400
  13.2 7.2 %collective-permute-start.1 = (bf16[512,256]{1,0:T(8,128)(2,1)}, bf16[512,256]{1,0:T(8,128)(2,1)}, u32[]{:S(2)}, u32[]{:S(2)}) collective-permute-start(bf16[512,256]{1,0:T(8,128)(2,1)} %param.13), channel_id=1, source_target_pairs={{8,200},{24,216},{40,232},{56,248},{72,136},{88,152},{104,168},{12... | collective-permute-start | bytes 786440 | tf_op jit(solution)/shard_map/ppermute | solution.py:405
  27.6 4.0 %all-to-all-start = ((bf16[32,384,128]{2,1,0:T(8,128)(2,1)}), bf16[32,384,128]{2,1,0:T(8,128)(2,1)S(1)}, u32[]{:S(2)}, u32[]{:S(2)}) async-start(bf16[32,384,128]{2,1,0:T(8,128)(2,1)} %copy-done.1), calls=%async_computation | async-start | bytes 6291456 | tf_op jit(solution)/shard_map/all_to_all | solution.py:409
  34.5 8.9 %collective-permute-start.2 = (bf16[512,256]{1,0:T(8,128)(2,1)}, bf16[512,256]{1,0:T(8,128)(2,1)}, u32[]{:S(2)}, u32[]{:S(2)}) collective-permute-start(bf16[512,256]{1,0:T(8,128)(2,1)} %get-tuple-element.48), channel_id=1, source_target_pairs={{0,1},{1,2},{2,3},{3,4},{4,5},{5,6},{6,7},{7,256},{256,257},{257,2... | collective-permute-start | bytes 786440 | tf_op jit(solution)/shard_map/ppermute | solution.py:425
  43.4 3.1 %collective-permute-start.3 = (bf16[512,256]{1,0:T(8,128)(2,1)}, bf16[512,256]{1,0:T(8,128)(2,1)}, u32[]{:S(2)}, u32[]{:S(2)}) collective-permute-start(bf16[512,256]{1,0:T(8,128)(2,1)} %get-tuple-element.47), channel_id=1, source_target_pairs={{0,2},{1,3},{2,4},{3,5},{4,6},{5,7},{6,256},{7,257},{256,258},{257... | collective-permute-start | bytes 786440 | tf_op jit(solution)/shard_map/ppermute | solution.py:425
  46.5 4.7 %collective-permute-start.4 = (bf16[512,256]{1,0:T(8,128)(2,1)}, bf16[512,256]{1,0:T(8,128)(2,1)}, u32[]{:S(2)}, u32[]{:S(2)}) collective-permute-start(bf16[512,256]{1,0:T(8,128)(2,1)} %get-tuple-element.42), channel_id=1, source_target_pairs={{0,3},{1,4},{2,5},{3,6},{4,7},{5,256},{6,257},{7,258},{256,259},{2... | collective-permute-start | bytes 786440 | tf_op jit(solution)/shard_map/ppermute | solution.py:425
  52.0 2.8 %collective-permute-start.5 = (bf16[512,128]{1,0:T(8,128)(2,1)}, bf16[512,128]{1,0:T(8,128)(2,1)S(1)}, u32[]{:S(2)}, u32[]{:S(2)}) collective-permute-start(bf16[512,128]{1,0:T(8,128)(2,1)} %get-tuple-element.46), channel_id=1, source_target_pairs={{8,268},{9,269},{10,270},{11,271},{12,8},{13,9},{14,10},{15,11},{2... | collective-permute-start | bytes 393224 | tf_op jit(solution)/shard_map/ppermute | solution.py:425
  54.8 6.4 %collective-permute-start.6 = (bf16[512,128]{1,0:T(8,128)(2,1)}, bf16[512,128]{1,0:T(8,128)(2,1)}, u32[]{:S(2)}, u32[]{:S(2)}) collective-permute-start(bf16[512,128]{1,0:T(8,128)(2,1)} %get-tuple-element.45), channel_id=1, source_target_pairs={{8,12},{9,13},{10,14},{11,15},{12,264},{13,265},{14,266},{15,267},... | collective-permute-start | bytes 393224 | tf_op jit(solution)/shard_map/ppermute | solution.py:425
  61.2 9.0 %all-to-all-done.text_ref.q_ref.c_ref = bf16[32,384,128]{2,1,0:T(8,128)(2,1)S(1)} async-done(((bf16[32,384,128]{2,1,0:T(8,128)(2,1)}), bf16[32,384,128]{2,1,0:T(8,128)(2,1)S(1)}, u32[]{:S(2)}, u32[]{:S(2)}) %all-to-all-start) | async-done | bytes 3145760 | tf_op jit(solution)/shard_map/all_to_all | solution.py:409
  70.3 4.3 %project.1.near_ref = f32[512,256]{1,0:T(8,128)} custom-call(s32[4]{0:T(128)S(1)} %pad_add_fusion.spot_ref, bf16[32,384,128]{2,1,0:T(8,128)(2,1)S(1)} %all-to-all-done.text_ref.q_ref.c_ref, bf16[512,256]{1,0:T(8,128)(2,1)S(1)} %get-tuple-element.49.refs_0_, bf16[512,256]{1,0:T(8,128)(2,1)} %collective-permute-done.2.refs_1_, ...), custom_call_target="tpu_custom_call" | custom-call | flops 536870912 | bytes 4194304 | tf_op jit(solution)/shard_map/project/pallas_call | solution.py:198
  74.5 3.4 %collective-permute-start.7 = (f32[512,256]{1,0:T(8,128)}, f32[512,256]{1,0:T(8,128)}, u32[]{:S(2)}, u32[]{:S(2)}) collective-permute-start(f32[512,256]{1,0:T(8,128)} %project.1.near_ref), channel_id=1, source_target_pairs={{0,8},{8,0},{1,9},{9,1},{2,10},{10,2},{3,11},{11,3},{4,12},{12,4},... | collective-permute-start | bytes 1572872 | tf_op jit(solution)/shard_map/ppermute | solution.py:437
  79.8 3.8 %all-to-all-start.1 = ((bf16[32,2,64,128]{3,2,1,0:T(8,128)(2,1)}), bf16[32,2,64,128]{3,2,1,0:T(8,128)(2,1)S(1)}, u32[]{:S(2)}, u32[]{:S(2)}) async-start(bf16[32,2,64,128]{3,2,1,0:T(8,128)(2,1)} %pack.1), calls=%async_computation.1 | async-start | bytes 2097152 | tf_op jit(solution)/shard_map/all_to_all | solution.py:434
  84.4 7.9 %cross.1 = (f32[2048,128]{1,0:T(8,128)}, f32[256,256]{1,0:T(8,128)}, f32[256,256]{1,0:T(8,128)}) custom-call(s32[1]{0:T(128)S(6)} %copy.9.length_ref, s32[4]{0:T(128)} %copy-done.9, bf16[32,384,128]{2,1,0:T(8,128)(2,1)} %copy-done, bf16[32,384,128]{2,1,0:T(8,128)(2,1)} %copy-done, f32[512,256]{1,0:T(8,128)} %project.1.near_ref, ...), custom_call_target="tpu_custom_call" | custom-call | flops 1342177280 | bytes 4194304 | tf_op jit(solution)/shard_map/cross/pallas_call | solution.py:269
  97.6 3.3 %all-to-all-done.1.near_ref = bf16[32,2,64,128]{3,2,1,0:T(8,128)(2,1)S(1)} async-done(((bf16[32,2,64,128]{3,2,1,0:T(8,128)(2,1)}), bf16[32,2,64,128]{3,2,1,0:T(8,128)(2,1)S(1)}, u32[]{:S(2)}, u32[]{:S(2)}) %all-to-all-start.1) | async-done | bytes 1048608 | tf_op jit(solution)/shard_map/all_to_all | solution.py:434
  100.9 22.1 %all_to_all.25 = bf16[8,16,512]{2,1,0:T(8,128)(2,1)S(1)} all-to-all(bf16[8,16,512]{2,1,0:T(8,128)(2,1)S(1)} %copy-done.8), channel_id=1, replica_groups=mesh['g'=2,'y'=4,'x'=4,'c'=2,'d'=8] {'d'}, dimensions={0} | all-to-all | bytes 262144 | tf_op jit(solution)/shard_map/all_to_all | solution.py:446
  124.6 4.1 %all-to-all-start.3 = ((bf16[16,8,16,512]{3,2,1,0:T(8,128)(2,1)}), bf16[16,8,16,512]{3,2,1,0:T(8,128)(2,1)S(1)}, u32[]{:S(2)}, u32[]{:S(2)}) async-start(bf16[16,8,16,512]{3,2,1,0:T(8,128)(2,1)} %broadcast_in_dim.2), calls=%async_computation.3 | async-start | bytes 4194304 | tf_op jit(solution)/shard_map/all_to_all | solution.py:447
  128.7 4.0 %collective-permute-start.9 = (bf16[32,2,64,128]{3,2,1,0:T(8,128)(2,1)}, bf16[32,2,64,128]{3,2,1,0:T(8,128)(2,1)S(1)}, u32[]{:S(2)}, u32[]{:S(2)}) collective-permute-start(bf16[32,2,64,128]{3,2,1,0:T(8,128)(2,1)} %copy-done.12), channel_id=1, source_target_pairs={{0,8},{8,0},{1,9},{9,1},{2,10},{10,2},{3,11},{11,3},{4,12},{12,4},... | collective-permute-start | bytes 3145736 | tf_op jit(solution)/shard_map/ppermute | solution.py:451
  132.7 2.5 %collective-permute-done.9.far_ref = bf16[32,2,64,128]{3,2,1,0:T(8,128)(2,1)S(1)} collective-permute-done((bf16[32,2,64,128]{3,2,1,0:T(8,128)(2,1)}, bf16[32,2,64,128]{3,2,1,0:T(8,128)(2,1)S(1)}, u32[]{:S(2)}, u32[]{:S(2)}) %collective-permute-start.9) | collective-permute-done | bytes 1048608 | tf_op jit(solution)/shard_map/ppermute | solution.py:451
  136.2 18.2 %self_attention.1 = bf16[2048,128]{1,0:T(8,128)(2,1)} custom-call(bf16[32,384,128]{2,1,0:T(8,128)(2,1)} %copy-done, bf16[32,2,64,128]{3,2,1,0:T(8,128)(2,1)} %copy-done.12, bf16[32,2,64,128]{3,2,1,0:T(8,128)(2,1)} %copy-done.14, f32[2048,128]{1,0:T(8,128)} %get-tuple-element.33.cross_ref), custom_call_target="tpu_custom_call" | custom-call | flops 4294967296 | bytes 5242880 | tf_op jit(solution)/shard_map/self_attention/pallas_call | solution.py:321
  155.8 19.7 %all_to_all.26.in_ref = bf16[32,64,128]{2,1,0:T(8,128)(2,1)S(1)} all-to-all(bf16[32,64,128]{2,1,0:T(8,128)(2,1)} %bitcast.7), channel_id=1, replica_groups=mesh['g'=2,'y'=4,'x'=4,'c'=2,'d'=8] {'y','x','c'}, dimensions={0} | all-to-all | bytes 1048576 | tf_op jit(solution)/shard_map/all_to_all | solution.py:454
  175.4 5.0 %finish.1 = (f32[512,256]{1,0:T(8,128)}, f32[512,256]{1,0:T(8,128)}) custom-call(s32[4]{0:T(128)} %copy-done.9, bf16[16,8,16,512]{3,2,1,0:T(8,128)(2,1)} %copy-done.11, bf16[16,256,256]{2,1,0:T(8,128)(2,1)} %bitcast.6), custom_call_target="tpu_custom_call" | custom-call | flops 1073741824 | bytes 6291456 | tf_op jit(solution)/shard_map/finish/pallas_call | solution.py:372
  180.4 2.4 %collective-permute-start.10 = (f32[512,256]{1,0:T(8,128)}, f32[512,256]{1,0:T(8,128)S(1)}, u32[]{:S(2)}, u32[]{:S(2)}) collective-permute-start(f32[512,256]{1,0:T(8,128)} %get-tuple-element.39), channel_id=1, source_target_pairs={{0,8},{8,0},{1,9},{9,1},{2,10},{10,2},{3,11},{11,3},{4,12},{12,4},... | collective-permute-start | bytes 1572872 | tf_op jit(solution)/shard_map/ppermute | solution.py:459
  185.6 4.1 %collective-permute-start.11 = (bf16[512,256]{1,0:T(8,128)(2,1)S(1)}, bf16[512,256]{1,0:T(8,128)(2,1)S(1)}, u32[]{:S(2)}, u32[]{:S(2)}) collective-permute-start(bf16[512,256]{1,0:T(8,128)(2,1)S(1)} %get-tuple-element.40), channel_id=1, source_target_pairs={{8,200},{24,216},{40,232},{56,248},{72,136},{88,152},{104,168},{12... | collective-permute-start | bytes 786440 | tf_op jit(solution)/shard_map/ppermute | solution.py:460
  191.2 2.7 %collective-permute-done.11 = bf16[512,256]{1,0:T(8,128)(2,1)S(1)} collective-permute-done((bf16[512,256]{1,0:T(8,128)(2,1)S(1)}, bf16[512,256]{1,0:T(8,128)(2,1)S(1)}, u32[]{:S(2)}, u32[]{:S(2)}) %collective-permute-start.11) | collective-permute-done | bytes 262176 | tf_op jit(solution)/shard_map/ppermute | solution.py:460
  (56 shorter events, 26.9 us)
Async XLA Ops:
  7.2 20.4 %collective-permute-start = (bf16[512,256]{1,0:T(8,128)(2,1)}, bf16[512,256]{1,0:T(8,128)(2,1)}, u32[]{:S(2)}, u32[]{:S(2)}) collective-permute-start(bf16[512,256]{1,0:T(8,128)(2,1)} %param.13), channel_id=1, source_target_pairs={{0,8},{16,24},{32,40},{48,56},{64,72},{80,88},{96,104},{112,120},{... | collective-permute-start | bytes 786440 | tf_op jit(solution)/shard_map/ppermute | solution.py:400
  13.2 14.4 %collective-permute-start.1 = (bf16[512,256]{1,0:T(8,128)(2,1)}, bf16[512,256]{1,0:T(8,128)(2,1)}, u32[]{:S(2)}, u32[]{:S(2)}) collective-permute-start(bf16[512,256]{1,0:T(8,128)(2,1)} %param.13), channel_id=1, source_target_pairs={{8,200},{24,216},{40,232},{56,248},{72,136},{88,152},{104,168},{12... | collective-permute-start | bytes 786440 | tf_op jit(solution)/shard_map/ppermute | solution.py:405
  23.7 54.2 %copy-start.9 = (s32[4]{0:T(128)}, s32[4]{0:T(128)S(1)}, u32[]{:S(2)}) copy-start(s32[4]{0:T(128)S(1)} %pad_add_fusion.spot_ref) | copy-start | bytes 52
  27.6 42.6 %all-to-all-start = ((bf16[32,384,128]{2,1,0:T(8,128)(2,1)}), bf16[32,384,128]{2,1,0:T(8,128)(2,1)S(1)}, u32[]{:S(2)}, u32[]{:S(2)}) async-start(bf16[32,384,128]{2,1,0:T(8,128)(2,1)} %copy-done.1), calls=%async_computation | async-start | bytes 6291456 | tf_op jit(solution)/shard_map/all_to_all | solution.py:409
  34.5 35.8 %collective-permute-start.2 = (bf16[512,256]{1,0:T(8,128)(2,1)}, bf16[512,256]{1,0:T(8,128)(2,1)}, u32[]{:S(2)}, u32[]{:S(2)}) collective-permute-start(bf16[512,256]{1,0:T(8,128)(2,1)} %get-tuple-element.48), channel_id=1, source_target_pairs={{0,1},{1,2},{2,3},{3,4},{4,5},{5,6},{6,7},{7,256},{256,257},{257,2... | collective-permute-start | bytes 786440 | tf_op jit(solution)/shard_map/ppermute | solution.py:425
  43.4 26.8 %collective-permute-start.3 = (bf16[512,256]{1,0:T(8,128)(2,1)}, bf16[512,256]{1,0:T(8,128)(2,1)}, u32[]{:S(2)}, u32[]{:S(2)}) collective-permute-start(bf16[512,256]{1,0:T(8,128)(2,1)} %get-tuple-element.47), channel_id=1, source_target_pairs={{0,2},{1,3},{2,4},{3,5},{4,6},{5,7},{6,256},{7,257},{256,258},{257... | collective-permute-start | bytes 786440 | tf_op jit(solution)/shard_map/ppermute | solution.py:425
  46.5 23.8 %collective-permute-start.4 = (bf16[512,256]{1,0:T(8,128)(2,1)}, bf16[512,256]{1,0:T(8,128)(2,1)}, u32[]{:S(2)}, u32[]{:S(2)}) collective-permute-start(bf16[512,256]{1,0:T(8,128)(2,1)} %get-tuple-element.42), channel_id=1, source_target_pairs={{0,3},{1,4},{2,5},{3,6},{4,7},{5,256},{6,257},{7,258},{256,259},{2... | collective-permute-start | bytes 786440 | tf_op jit(solution)/shard_map/ppermute | solution.py:425
  52.0 18.2 %collective-permute-start.5 = (bf16[512,128]{1,0:T(8,128)(2,1)}, bf16[512,128]{1,0:T(8,128)(2,1)S(1)}, u32[]{:S(2)}, u32[]{:S(2)}) collective-permute-start(bf16[512,128]{1,0:T(8,128)(2,1)} %get-tuple-element.46), channel_id=1, source_target_pairs={{8,268},{9,269},{10,270},{11,271},{12,8},{13,9},{14,10},{15,11},{2... | collective-permute-start | bytes 393224 | tf_op jit(solution)/shard_map/ppermute | solution.py:425
  54.8 15.4 %collective-permute-start.6 = (bf16[512,128]{1,0:T(8,128)(2,1)}, bf16[512,128]{1,0:T(8,128)(2,1)}, u32[]{:S(2)}, u32[]{:S(2)}) collective-permute-start(bf16[512,128]{1,0:T(8,128)(2,1)} %get-tuple-element.45), channel_id=1, source_target_pairs={{8,12},{9,13},{10,14},{11,15},{12,264},{13,265},{14,266},{15,267},... | collective-permute-start | bytes 393224 | tf_op jit(solution)/shard_map/ppermute | solution.py:425
  70.2 4.3 %copy-start = (bf16[32,384,128]{2,1,0:T(8,128)(2,1)}, bf16[32,384,128]{2,1,0:T(8,128)(2,1)S(1)}, u32[]{:S(2)}) copy-start(bf16[32,384,128]{2,1,0:T(8,128)(2,1)S(1)} %all-to-all-done.text_ref.q_ref.c_ref) | copy-start | bytes 9437188
  70.3 7.7 %copy-start.3 = (bf16[1,128,4096]{2,1,0:T(8,128)(2,1)S(1)}, bf16[1,128,4096]{2,1,0:T(8,128)(2,1)}, u32[]{:S(2)}) copy-start(bf16[1,128,4096]{2,1,0:T(8,128)(2,1)} %wide_ref) | copy-start | bytes 3145732
  70.3 7.7 %copy-start.5 = (bf16[1,128,2048]{2,1,0:T(8,128)(2,1)S(1)}, bf16[1,128,2048]{2,1,0:T(8,128)(2,1)}, u32[]{:S(2)}) copy-start(bf16[1,128,2048]{2,1,0:T(8,128)(2,1)} %half_ref) | copy-start | bytes 1572868
  74.5 9.8 %collective-permute-start.7 = (f32[512,256]{1,0:T(8,128)}, f32[512,256]{1,0:T(8,128)}, u32[]{:S(2)}, u32[]{:S(2)}) collective-permute-start(f32[512,256]{1,0:T(8,128)} %project.1.near_ref), channel_id=1, source_target_pairs={{0,8},{8,0},{1,9},{9,1},{2,10},{10,2},{3,11},{11,3},{4,12},{12,4},... | collective-permute-start | bytes 1572872 | tf_op jit(solution)/shard_map/ppermute | solution.py:437
  79.8 21.0 %all-to-all-start.1 = ((bf16[32,2,64,128]{3,2,1,0:T(8,128)(2,1)}), bf16[32,2,64,128]{3,2,1,0:T(8,128)(2,1)S(1)}, u32[]{:S(2)}, u32[]{:S(2)}) async-start(bf16[32,2,64,128]{3,2,1,0:T(8,128)(2,1)} %pack.1), calls=%async_computation.1 | async-start | bytes 2097152 | tf_op jit(solution)/shard_map/all_to_all | solution.py:434
  83.7 91.8 %all-gather.3.cloned.1.call-start = ((), (), s32[]{:S(2)}) async-start(), calls=%async_computation.5 | async-start | bytes 2228224 | tf_op jit(solution)/shard_map/all_gather | solution.py:444
  84.3 16.5 %copy-start.8 = (bf16[8,16,512]{2,1,0:T(8,128)(2,1)S(1)}, bf16[8,16,512]{2,1,0:T(8,128)(2,1)}, u32[]{:S(2)}) copy-start(bf16[8,16,512]{2,1,0:T(8,128)(2,1)} %copy-done.7) | copy-start | bytes 393220
  92.3 3.6 %collective-permute-start.8 = (f32[256,256]{1,0:T(8,128)}, f32[256,256]{1,0:T(8,128)S(1)}, u32[]{:S(2)}, u32[]{:S(2)}) collective-permute-start(f32[256,256]{1,0:T(8,128)} %get-tuple-element.27), channel_id=1, source_target_pairs={{0,8},{8,0},{1,9},{9,1},{2,10},{10,2},{3,11},{11,3},{4,12},{12,4},... | collective-permute-start | bytes 786440 | tf_op jit(solution)/shard_map/ppermute | solution.py:441
  100.8 23.8 %copy-start.12 = (bf16[32,2,64,128]{3,2,1,0:T(8,128)(2,1)}, bf16[32,2,64,128]{3,2,1,0:T(8,128)(2,1)S(1)}, u32[]{:S(2)}) copy-start(bf16[32,2,64,128]{3,2,1,0:T(8,128)(2,1)S(1)} %all-to-all-done.1.near_ref) | copy-start | bytes 3145732
  124.6 31.2 %all-to-all-start.3 = ((bf16[16,8,16,512]{3,2,1,0:T(8,128)(2,1)}), bf16[16,8,16,512]{3,2,1,0:T(8,128)(2,1)S(1)}, u32[]{:S(2)}, u32[]{:S(2)}) async-start(bf16[16,8,16,512]{3,2,1,0:T(8,128)(2,1)} %broadcast_in_dim.2), calls=%async_computation.3 | async-start | bytes 4194304 | tf_op jit(solution)/shard_map/all_to_all | solution.py:447
  128.7 6.5 %collective-permute-start.9 = (bf16[32,2,64,128]{3,2,1,0:T(8,128)(2,1)}, bf16[32,2,64,128]{3,2,1,0:T(8,128)(2,1)S(1)}, u32[]{:S(2)}, u32[]{:S(2)}) collective-permute-start(bf16[32,2,64,128]{3,2,1,0:T(8,128)(2,1)} %copy-done.12), channel_id=1, source_target_pairs={{0,8},{8,0},{1,9},{9,1},{2,10},{10,2},{3,11},{11,3},{4,12},{12,4},... | collective-permute-start | bytes 3145736 | tf_op jit(solution)/shard_map/ppermute | solution.py:451
  155.8 19.7 %copy-start.11 = (bf16[16,8,16,512]{3,2,1,0:T(8,128)(2,1)}, bf16[16,8,16,512]{3,2,1,0:T(8,128)(2,1)S(1)}, u32[]{:S(2)}) copy-start(bf16[16,8,16,512]{3,2,1,0:T(8,128)(2,1)S(1)} %all-to-all-done.3.text_any) | copy-start | bytes 6291460
  175.4 14.3 %copy-start.10 = (s32[4]{0:T(128)S(1)}, s32[4]{0:T(128)}, u32[]{:S(2)}) copy-start(s32[4]{0:T(128)} %copy-done.9) | copy-start | bytes 52
  180.4 4.1 %collective-permute-start.10 = (f32[512,256]{1,0:T(8,128)}, f32[512,256]{1,0:T(8,128)S(1)}, u32[]{:S(2)}, u32[]{:S(2)}) collective-permute-start(f32[512,256]{1,0:T(8,128)} %get-tuple-element.39), channel_id=1, source_target_pairs={{0,8},{8,0},{1,9},{9,1},{2,10},{10,2},{3,11},{11,3},{4,12},{12,4},... | collective-permute-start | bytes 1572872 | tf_op jit(solution)/shard_map/ppermute | solution.py:459
  185.6 8.3 %collective-permute-start.11 = (bf16[512,256]{1,0:T(8,128)(2,1)S(1)}, bf16[512,256]{1,0:T(8,128)(2,1)S(1)}, u32[]{:S(2)}, u32[]{:S(2)}) collective-permute-start(bf16[512,256]{1,0:T(8,128)(2,1)S(1)} %get-tuple-element.40), channel_id=1, source_target_pairs={{8,200},{24,216},{40,232},{56,248},{72,136},{88,152},{104,168},{12... | collective-permute-start | bytes 786440 | tf_op jit(solution)/shard_map/ppermute | solution.py:460
  (7 other events, 10.7 us)
Sparse Core Ops, SparseCore 0:
  101.0 64.7 all-gather.2
